TPU v7x, 32 devices: a whole 2x2x4 slice. The times are simulated.
32 devices in a mesh: dp: 8 (over z, core), tensor: 4 (over y, x).
Axes of the slice: x: 2, y: 2, z: 4, core: 2. Of those that a mesh axis runs over, the one named last changes fastest.
Arguments:
- tokens: bfloat16 [8192, 2560], P(('dp', 'tensor')), may hold values from -6 to 6
- segments: int32 [8192], P(('dp', 'tensor')), may hold values from 0 to 15, never falling along the last dimension, each value on 1 to 2048 neighbouring positions
- cotangent: bfloat16 [8192, 2560], P(('dp', 'tensor')), may hold values from -6 to 6
- norm_gain: float32 [2560], replicated, may hold values from 0.25 to 1.75
- w_y: bfloat16 [2560, 2560], P('dp', 'tensor'), may hold values from -0.125 to 0.125
- w_x: bfloat16 [2560, 2560], P('dp', 'tensor'), may hold values from -0.125 to 0.125
- conv_w: float32 [4, 2560], replicated, may hold values from -3 to 3
- gate_w: bfloat16 [2, 10, 256, 256], replicated, may hold values from -0.375 to 0.375
- decay_param: float32 [2560], replicated, may hold values from -8.5 to 0.5
- w_out: bfloat16 [2560, 2560], P('dp', 'tensor'), may hold values from -0.125 to 0.125
- mlp_gain: float32 [2560], replicated, may hold values from 0.25 to 1.75
- w_gate: bfloat16 [2560, 7680], P('dp', 'tensor'), may hold values from -0.125 to 0.125
- w_up: bfloat16 [2560, 7680], P('dp', 'tensor'), may hold values from -0.125 to 0.125
- w_down: bfloat16 [2560, 7680], P('dp', 'tensor'), may hold values from -0.0625 to 0.0625
Outputs:
- mixed: bfloat16 [8192, 2560], P(('dp', 'tensor'))
- grad_input: float32 [8192, 2560], P(('dp', 'tensor'))
- grad_norm_gain: float32 [2560], replicated
- grad_w_y: float32 [2560, 2560], P('dp', 'tensor')
- grad_w_x: float32 [2560, 2560], P('dp', 'tensor')
- grad_conv_w: float32 [4, 2560], replicated
- grad_gate_w: float32 [2, 10, 256, 256], replicated
- grad_decay_param: float32 [2560], replicated
- grad_w_out: float32 [2560, 2560], P('dp', 'tensor')
- grad_mlp_gain: float32 [2560], replicated
- grad_w_gate: float32 [2560, 7680], P('dp', 'tensor')
- grad_w_up: float32 [2560, 7680], P('dp', 'tensor')
- grad_w_down: float32 [2560, 7680], P('dp', 'tensor')
Inputs may be any that keep to these rules, and one draw needn't show every extreme that they name: `segments`: segment numbers never fall along the tokens and a document holds at most 2048 tokens; the recurrence and the convolution also start afresh every 1024 tokens.
All inputs are finite; a program needn't handle non-finite values.
Results may differ from a plain program's by a relative error of at most 0.0095.
Values may be sent and summed in bfloat16 or wider, within the bound.
A program may use at most 384 MiB of HBM per device.

v0:
```python
import math
from functools import partial

import jax
import jax.numpy as jnp
from jax import lax
from jax.experimental import pallas as pl
from jax.experimental.pallas import tpu as pltpu
from jax.sharding import PartitionSpec as P

EPSILON = 1e-06
MESH = pl.DeviceIdType.MESH
VMEM_BYTES = 56 * 1024 * 1024
CHUNK = 16
F32 = jnp.float32
BF16 = jnp.bfloat16


def subsets(bits):
    found = [()]
    for bit in bits:
        found = found + [chosen + (bit,) for chosen in found]
    return found


def flipped(index, bits):
    for bit in bits:
        mine = (index // (1 << bit)) % 2
        index = index + (1 - 2 * mine) * (1 << bit)
    return index


def log2_of(count):
    assert count & (count - 1) == 0
    return count.bit_length() - 1


def greet(axis_bits):
    barrier = pltpu.get_barrier_semaphore()
    for axis, bit in axis_bits:
        peer = flipped(lax.axis_index(axis), (bit,))
        pl.semaphore_signal(barrier, inc=1, device_id={axis: peer}, device_id_type=MESH)
    pl.semaphore_wait(barrier, len(axis_bits))


def halves_of(nbits, columns):
    half = columns // 2
    ups = tuple(range(nbits))
    return ((ups, 0, half), (ups[::-1], half, half))


class Gather:
    def __init__(self, ref, rows, nbits, send_sems, recv_sems):
        self.ref, self.rows, self.nbits = ref, rows, nbits
        self.sems = (send_sems, recv_sems)
        self.me = lax.axis_index("tensor")
        self.plan = []
        number = 0
        for half, (order, at, width) in enumerate(halves_of(nbits, ref.shape[1])):
            for step, bit in enumerate(order):
                for known in subsets(order[:step]):
                    self.plan.append((half, step, known, bit, at, width, number))
                    number += 1
        self.count = number

    def copy(self, item):
        half, step, known, bit, at, width, number = item
        row = pl.multiple_of(flipped(self.me, known) * self.rows, self.rows)
        piece = self.ref.at[pl.ds(row, self.rows), pl.ds(at, width)]
        return pltpu.make_async_remote_copy(
            src_ref=piece,
            dst_ref=piece,
            send_sem=self.sems[0].at[number],
            recv_sem=self.sems[1].at[number],
            device_id={"tensor": flipped(self.me, (bit,))},
            device_id_type=MESH,
        )

    def begin(self):
        for item in sorted(self.plan, key=lambda it: it[1]):
            if item[2] == ():
                self.copy(item).start()

    def advance(self, step):
        for item in self.plan:
            half, at_step, known, bit, at, width, number = item
            if at_step == step:
                self.copy(item).wait_recv()
                block = known + (bit,)
                for later in self.plan:
                    if later[0] == half and set(later[2]) == set(block):
                        self.copy(later).start()

    def finish(self, step=0):
        for at_step in range(step, self.nbits):
            self.advance(at_step)
        for item in self.plan:
            self.copy(item).wait_send()


def gather_copies(nbits):
    return 2 * ((1 << nbits) - 1)


class Scatter:
    def __init__(self, ref, landed, staged, rows, nbits, send_sems, recv_sems):
        self.ref, self.landed, self.staged = ref, landed, staged
        self.rows, self.nbits = rows, nbits
        self.sems = (send_sems, recv_sems)
        self.me = lax.axis_index("tensor")
        self.plan, self.slot = [], {}
        number = 0
        for half, (order, at, width) in enumerate(halves_of(nbits, ref.shape[1])):
            for step, bit in enumerate(order):
                for rest in subsets(order[step + 1 :])[::-1]:
                    self.plan.append((half, step, rest, bit, at, width, number))
                    if step > 0:
                        self.slot[number] = len(self.slot)
                    number += 1

    def copy(self, item):
        half, step, rest, bit, at, width, number = item
        if step == 0:
            row = pl.multiple_of(flipped(self.me, rest + (bit,)) * self.rows, self.rows)
            source = self.ref.at[pl.ds(row, self.rows), pl.ds(at, width)]
        else:
            source = self.staged.at[self.slot[number]]
        return pltpu.make_async_remote_copy(
            src_ref=source,
            dst_ref=self.landed.at[number],
            send_sem=self.sems[0].at[number],
            recv_sem=self.sems[1].at[number],
            device_id={"tensor": flipped(self.me, (bit,))},
            device_id_type=MESH,
        )

    def begin(self):
        for item in sorted(self.plan, key=lambda it: (len(it[2]) == 0)):
            if item[1] == 0:
                self.copy(item).start()

    def partial_sum(self, half, block, before, row, size):
        at, width = halves_of(self.nbits, self.ref.shape[1])[half][1:]
        base = pl.multiple_of(flipped(self.me, block) * self.rows + row, size)
        total = self.ref[pl.ds(base, size), pl.ds(at, width)].astype(F32)
        for it in self.plan:
            if it[0] == half and it[1] < before and set(it[2]) == set(block):
                total = total + self.landed[it[6], pl.ds(row, size), :].astype(F32)
        return total

    def advance(self, step):
        for half in range(2):
            for item in self.plan:
                if item[0] == half and item[1] == step:
                    self.copy(item).wait_recv()
            for item in self.plan:
                if item[0] == half and item[1] == step + 1:

                    def fill(row, item=item):
                        value = self.partial_sum(
                            item[0], item[2] + (item[3],), item[1], row, CHUNK
                        )
                        where = (self.slot[item[6]], pl.ds(row, CHUNK))
                        self.staged[where + (slice(None),)] = value.astype(BF16)

                    chunks(self.rows, fill)
                    self.copy(item).start()

    def run(self):
        for step in range(self.nbits):
            self.advance(step)

    def total(self, row, size):
        return jnp.concatenate(
            [self.partial_sum(half, (), self.nbits, row, size) for half in range(2)], axis=1
        )

    def drain(self):
        for item in self.plan:
            self.copy(item).wait_send()


def scatter_scratch(rows, columns, nbits):
    copies = gather_copies(nbits)
    later = max(1, copies - (1 << nbits))
    return [
        pltpu.VMEM((copies, rows, columns // 2), BF16),
        pltpu.VMEM((later, rows, columns // 2), BF16),
        pltpu.SemaphoreType.DMA((copies,)),
        pltpu.SemaphoreType.DMA((copies,)),
    ]


def gather_sems(nbits):
    copies = gather_copies(nbits)
    return [pltpu.SemaphoreType.DMA((copies,)), pltpu.SemaphoreType.DMA((copies,))]


def tensor_bits(nbits):
    return [("tensor", bit) for bit in range(nbits)]


def rms_scale_of(values):
    return lax.rsqrt(jnp.mean(values * values, axis=-1, keepdims=True) + EPSILON)


def chunks(rows, body):
    def step(i, carry):
        body(pl.multiple_of(i * CHUNK, CHUNK))
        return carry

    lax.fori_loop(0, rows // CHUNK, step, 0)


def own_row(row, rows):
    return pl.multiple_of(lax.axis_index("tensor") * rows + row, CHUNK)


def dp_place():
    me = lax.axis_index("dp")
    return me // 2, me % 2, lax.axis_size("dp") // 2


def dp_index(chip, core):
    return chip * 2 + core


UP, DOWN = 1, -1


class LineGather:
    def __init__(self, own, whole, send_sems, recv_sems, columns=None):
        self.own, self.whole = own, whole
        self.sems = (send_sems, recv_sems)
        self.chip, self.core, self.chips = dp_place()
        self.rows = own.shape[0]
        self.columns = slice(None) if columns is None else columns

    def block(self, chip):
        row = pl.multiple_of(dp_index(chip, self.core) * self.rows, self.rows)
        return self.whole.at[pl.ds(row, self.rows), self.columns]

    def has(self, way, distance):
        return self.chip >= distance if way == UP else self.chip + distance < self.chips

    def number(self, way, distance):
        return (0 if way == UP else self.chips) + distance

    def along(self, way, distance):
        block = self.block(self.chip - way * distance)
        return pltpu.make_async_remote_copy(
            src_ref=self.own if distance == 0 else block,
            dst_ref=block,
            send_sem=self.sems[0].at[self.number(way, distance)],
            recv_sem=self.sems[1].at[self.number(way, distance + 1)],
            device_id={"dp": dp_index(self.chip + way, self.core)},
            device_id_type=MESH,
        )

    def arrival(self, way, distance):
        block = self.block(self.chip - way * distance)
        return pltpu.make_async_remote_copy(
            src_ref=block,
            dst_ref=block,
            send_sem=self.sems[0].at[self.number(way, distance)],
            recv_sem=self.sems[1].at[self.number(way, distance)],
            device_id={"dp": dp_index(self.chip + way, self.core)},
            device_id_type=MESH,
        )

    def across(self, way, distance):
        block = self.block(self.chip - way * distance)
        number = 2 * self.chips + self.number(way, distance)
        return pltpu.make_async_remote_copy(
            src_ref=self.own if distance == 0 else block,
            dst_ref=block,
            send_sem=self.sems[0].at[number],
            recv_sem=self.sems[1].at[number],
            device_id={"dp": dp_index(self.chip, 1 - self.core)},
            device_id_type=MESH,
        )

    def local(self):
        return pltpu.make_async_copy(
            self.own, self.block(self.chip), self.sems[0].at[4 * self.chips]
        )

    def begin(self):
        for way in (UP, DOWN):

            @pl.when(self.has(-way, 1))
            def _(way=way):
                self.along(way, 0).start()

        self.across(UP, 0).start()
        self.local().start()

    def pass_on(self, distance):
        for way in (UP, DOWN):

            @pl.when(self.has(way, distance))
            def _(way=way):
                self.arrival(way, distance).wait_recv()

                @pl.when(self.has(-way, 1))
                def _():
                    self.along(way, distance).start()

                self.across(way, distance).start()

    def finish(self):
        self.across(UP, 0).wait()
        self.local().wait()
        for way in (UP, DOWN):
            for distance in range(self.chips):

                @pl.when(self.has(way, distance) & self.has(-way, 1))
                def _(way=way, distance=distance):
                    self.along(way, distance).wait_send()

                if distance:

                    @pl.when(self.has(way, distance))
                    def _(way=way, distance=distance):
                        self.across(way, distance).wait()


def line_sems(ndp):
    chips = ndp // 2
    return [pltpu.SemaphoreType.DMA((4 * chips + 1,)), pltpu.SemaphoreType.DMA((4 * chips + 1,))]


def greet_peers(nbits, all_tensor, whole_dp):
    me = lax.axis_index("tensor")
    chip, core, chips = dp_place()
    barrier = pltpu.get_barrier_semaphore()

    def signal(target):
        pl.semaphore_signal(barrier, inc=1, device_id=target, device_id_type=MESH)

    met = 0
    for chosen in subsets(tuple(range(nbits))):
        if chosen and (all_tensor or len(chosen) == 1):
            signal({"tensor": flipped(me, chosen)})
            met += 1
    if whole_dp:
        for shift in range(chips):
            for turn in range(2):
                if (shift, turn) != (0, 0):
                    other = dp_index((chip + shift) % chips, core + turn * (1 - 2 * core))
                    signal({"dp": other})
                    met += 1
    else:
        signal({"dp": dp_index(chip, 1 - core)})
        met += 1

        for shift in sorted({1 % chips, chips - 1} - {0}):
            signal({"dp": dp_index((chip + shift) % chips, core)})
            met += 1

    pl.semaphore_wait(barrier, met)


def enter_kernel(
    nbits, parts_yx, tokens, seg, gain, *refs
):
    w_yx, w_out = refs[:parts_yx], refs[parts_yx]
    normed_all, seg_all, wyx_all, wout_all, s0, r0, s2, r2, l0, *line = refs[parts_yx + 1 :]
    rows = tokens.shape[0]
    me = lax.axis_index("tensor")
    peers = [chosen for chosen in subsets(tuple(range(nbits))) if chosen]
    greet_peers(nbits, True, False)
    width = wyx_all.shape[1] // parts_yx
    lines = [
        LineGather(
            own,
            wyx_all,
            line[2 * number],
            line[2 * number + 1],
            pl.ds(number * width, width) if parts_yx > 1 else None,
        )
        for number, own in enumerate(w_yx)
    ]
    lines.append(LineGather(w_out, wout_all, *line[2 * parts_yx : 2 * parts_yx + 2]))
    for item in lines:
        item.begin()

    def norm(row):
        values = tokens[pl.ds(row, CHUNK), :].astype(F32)
        scaled = values * rms_scale_of(values) * gain[...]
        normed_all[pl.ds(own_row(row, rows), CHUNK), :] = scaled.astype(BF16)

    chunks(rows, norm)
    gather = Gather(normed_all, rows, nbits, s0, r0)
    gather.begin()
    seg_own = pltpu.make_async_copy(seg, seg_all.at[me], l0.at[0])
    seg_own.start()
    seg_copies = [
        pltpu.make_async_remote_copy(
            src_ref=seg,
            dst_ref=seg_all.at[me],
            send_sem=s2.at[number],
            recv_sem=r2.at[number],
            device_id={"tensor": flipped(me, chosen)},
            device_id_type=MESH,
        )
        for number, chosen in enumerate(peers)
    ]
    for copy in seg_copies:
        copy.start()
    chips = lines[0].chips
    for item in lines:
        item.pass_on(1)
    gather.advance(0)
    for distance in range(2, chips):
        for item in lines:
            item.pass_on(distance)
    gather.finish(1)
    for item in lines:
        item.finish()
    for copy in seg_copies:
        copy.wait()
    seg_own.wait()


class Fetch:
    def __init__(self, nbits, cot, cot_all, s0, r0, l0):
        rows = cot.shape[0]
        own = pl.multiple_of(lax.axis_index("tensor") * rows, rows)
        self.local = pltpu.make_async_copy(cot, cot_all.at[pl.ds(own, rows), :], l0.at[0])
        self.gather = Gather(cot_all, rows, nbits, s0, r0)

    def begin(self):
        self.local.wait()
        self.gather.begin()

    def advance(self):
        self.gather.advance(0)

    def finish(self):
        self.gather.finish(1)


def fetch_scratch(nbits):
    return gather_sems(nbits) + [pltpu.SemaphoreType.DMA((1,))]


def fetch_kernel(nbits, cot, cot_all, *sems):
    greet(tensor_bits(nbits))
    fetch = Fetch(nbits, cot, cot_all, *sems)
    fetch.local.start()
    fetch.begin()
    fetch.advance()
    fetch.finish()


def middle_kernel(
    nbits, mixer, tokens, gain, middle, mid_all, landed, staged, s0, r0, s1, r1
):
    rows = tokens.shape[0]
    greet(tensor_bits(nbits))
    scatter = Scatter(mixer, landed, staged, rows, nbits, s0, r0)
    scatter.begin()
    scatter.run()

    def norm(row):
        values = tokens[pl.ds(row, CHUNK), :].astype(F32) + scatter.total(row, CHUNK)
        middle[pl.ds(row, CHUNK), :] = values
        scaled = values * rms_scale_of(values) * gain[...]
        mid_all[pl.ds(own_row(row, rows), CHUNK), :] = scaled.astype(BF16)

    chunks(rows, norm)
    gather = Gather(mid_all, rows, nbits, s1, r1)
    gather.begin()
    gather.finish()
    scatter.drain()


def result_kernel(nbits, ffn, middle, mixed, landed, staged, s0, r0):
    rows = middle.shape[0]
    greet(tensor_bits(nbits))
    scatter = Scatter(ffn, landed, staged, rows, nbits, s0, r0)
    scatter.begin()
    scatter.run()

    def add(row):
        values = middle[pl.ds(row, CHUNK), :] + scatter.total(row, CHUNK)
        mixed[pl.ds(row, CHUNK), :] = values.astype(BF16)

    chunks(rows, add)
    scatter.drain()


def norm_pull(values, gain, cotangent):
    scale = rms_scale_of(values)
    unit = values * scale
    inner = cotangent * gain
    back = scale * (inner - unit * jnp.mean(inner * unit, axis=-1, keepdims=True))
    return back, cotangent * unit


def eight_rows(values):
    total = values[0:8]
    for at in range(8, CHUNK, 8):
        total = total + values[at : at + 8]
    return total


def turn_kernel(
    nbits, d_norm, cot, middle, gain, d_middle, d_mixer, d_gain, landed, staged, s0, r0, s1, r1
):
    rows = middle.shape[0]
    greet(tensor_bits(nbits))
    scatter = Scatter(d_norm, landed, staged, rows, nbits, s0, r0)
    scatter.begin()
    d_gain[...] = jnp.zeros_like(d_gain)
    scatter.run()

    def pull(row):
        span = pl.ds(row, CHUNK)
        back, gains = norm_pull(middle[span, :], gain[...], scatter.total(row, CHUNK))
        values = cot[span, :].astype(F32) + back
        d_middle[span, :] = values
        d_mixer[pl.ds(own_row(row, rows), CHUNK), :] = values.astype(BF16)
        d_gain[...] += eight_rows(gains)

    chunks(rows, pull)
    gather = Gather(d_mixer, rows, nbits, s1, r1)
    gather.begin()
    gather.finish()
    scatter.drain()


class LineSum:
    def __init__(self, whole, kept, swapped, staged, landed, send_sems, recv_sems, columns=None):
        self.whole, self.kept, self.swapped = whole, kept, swapped
        self.staged, self.landed = staged, landed
        self.sems = (send_sems, recv_sems)
        self.columns = columns
        self.chip, self.core, self.chips = dp_place()
        self.rows = whole.shape[2]

    def half(self, core):
        if self.columns is None:
            return self.whole.at[:, core]
        return self.whole.at[:, core, :, self.columns]

    def local(self):
        return pltpu.make_async_copy(
            self.half(self.core), self.kept, self.sems[0].at[2 * self.chips]
        )

    def swap(self):
        return pltpu.make_async_remote_copy(
            src_ref=self.half(1 - self.core),
            dst_ref=self.swapped,
            send_sem=self.sems[0].at[0],
            recv_sem=self.sems[1].at[0],
            device_id={"dp": dp_index(self.chip, 1 - self.core)},
            device_id_type=MESH,
        )

    def has(self, way, distance):
        return self.chip + distance < self.chips if way == UP else self.chip >= distance

    def slot(self, way, distance):
        return (0 if way == UP else self.chips - 1) + distance

    def hop(self, way, distance):
        return pltpu.make_async_remote_copy(
            src_ref=self.staged.at[self.slot(way, distance - 1)],
            dst_ref=self.landed.at[self.slot(way, distance - 1)],
            send_sem=self.sems[0].at[1 + self.slot(way, distance - 1)],
            recv_sem=self.sems[1].at[1 + self.slot(way, distance - 1)],
            device_id={"dp": dp_index(self.chip + way, self.core)},
            device_id_type=MESH,
        )

    def arrival(self, way, distance):
        number = self.slot(way, distance)
        return pltpu.make_async_remote_copy(
            src_ref=self.landed.at[number],
            dst_ref=self.landed.at[number],
            send_sem=self.sems[0].at[1 + number],
            recv_sem=self.sems[1].at[1 + number],
            device_id={"dp": dp_index(self.chip - way, self.core)},
            device_id_type=MESH,
        )

    def begin(self):
        self.swap().start()
        self.local().start()

    def both(self, chip, span):
        return self.kept[chip, span, :].astype(F32) + self.swapped[chip, span, :].astype(F32)

    def send(self, distance):
        if distance == self.chips - 1:
            self.local().wait()
            self.swap().wait_recv()
        for way in (UP, DOWN):

            @pl.when(self.has(way, distance))
            def _(way=way):
                chip = self.chip + way * distance
                slot = self.slot(way, distance - 1)

                def first(row):
                    span = pl.ds(row, CHUNK)
                    self.staged[slot, span, :] = self.both(chip, span).astype(BF16)

                def later(row):
                    span = pl.ds(row, CHUNK)
                    total = self.both(chip, span) + self.landed[
                        self.slot(way, distance), span, :
                    ].astype(F32)
                    self.staged[slot, span, :] = total.astype(BF16)

                if distance == self.chips - 1:
                    chunks(self.rows, first)
                else:

                    @pl.when(self.has(-way, 1))
                    def _():
                        self.arrival(way, distance).wait_recv()
                        chunks(self.rows, later)

                    @pl.when(jnp.logical_not(self.has(-way, 1)))
                    def _():
                        chunks(self.rows, first)

                self.hop(way, distance).start()

    def finish(self, store):
        below, above = self.has(DOWN, 1), self.has(UP, 1)

        def fill(slots):
            for way in slots:
                self.arrival(way, 0).wait_recv()

            def one(row):
                span = pl.ds(row, CHUNK)
                total = self.both(self.chip, span)
                for way in slots:
                    total = total + self.landed[self.slot(way, 0), span, :].astype(F32)
                store(span, total)

            chunks(self.rows, one)

        @pl.when(below & above)
        def _():
            fill((UP, DOWN))

        @pl.when(jnp.logical_not(above))
        def _():
            fill((UP,))

        @pl.when(jnp.logical_not(below))
        def _():
            fill((DOWN,))

    def drain(self):
        self.swap().wait_send()
        for way in (UP, DOWN):
            for distance in range(1, self.chips):

                @pl.when(self.has(way, distance))
                def _(way=way, distance=distance):
                    self.hop(way, distance).wait_send()


def line_scratch(ndp, rows, columns):
    chips = ndp // 2
    return [
        pltpu.VMEM((chips, rows, columns), BF16),
        pltpu.VMEM((chips, rows, columns), BF16),
        pltpu.VMEM((2 * chips - 2, rows, columns), BF16),
        pltpu.VMEM((2 * chips - 2, rows, columns), BF16),
        pltpu.SemaphoreType.DMA((2 * chips + 1,)),
        pltpu.SemaphoreType.DMA((2 * chips + 1,)),
    ]


RING = 6


def leave_kernel(nbits, tiled, *refs):
    refs = list(refs)

    def take(count):
        taken = refs[:count]
        del refs[:count]
        return taken

    d_norm, tokens, d_middle, gain, own_small, d_gain_mid = take(6)
    pieces = take(3)
    grad_input, sum_out, sum_y, sum_x, gate_all, small_all = take(6)
    landed, staged, s0, r0 = take(4)
    share = small_all.shape[2]
    rings = [LineSum(piece, *take(RING)) for piece in pieces[:2]]
    if tiled:
        for at in (0, share):
            rings.append(LineSum(pieces[2], *take(RING), pl.ds(at, share)))
    else:
        rings.append(LineSum(pieces[2], *take(RING)))
    d_gain, gains, gains_landed, small, small_landed = take(5)
    gain_s, gain_r, vec_s, vec_r, join_s, join_r, gate_s, gate_r = take(8)
    rows = tokens.shape[0]
    me = lax.axis_index("tensor")
    chip, core, chips = dp_place()
    peers = [chosen for chosen in subsets(tuple(range(nbits))) if chosen]
    others = [(shift, turn) for shift in range(chips) for turn in range(2)][1:]
    greet_peers(nbits, True, True)
    for ring in rings:
        ring.begin()
    scatter = Scatter(d_norm, landed, staged, rows, nbits, s0, r0)
    scatter.begin()
    d_gain[...] = jnp.zeros_like(d_gain)
    far = list(range(chips - 1, 0, -1))
    for ring in rings:
        ring.send(far[0])
    if len(far) > 1:
        rings[0].send(far[1])
    scatter.advance(0)
    if len(far) > 1:
        for ring in rings[1:]:
            ring.send(far[1])
    for distance in far[2:]:
        rings[0].send(distance)
    for step in range(1, nbits):
        scatter.advance(step)

    def pull(row):
        span = pl.ds(row, CHUNK)
        back, parts = norm_pull(
            tokens[span, :].astype(F32), gain[...], scatter.total(row, CHUNK)
        )
        grad_input[span, :] = d_middle[span, :] + back
        d_gain[...] += eight_rows(parts)

    chunks(rows, pull)
    def store_gate(span, value):
        gate_all[me, chip, core, span, :] = value.astype(BF16)

    def gate_copy(number, ref, target):
        return pltpu.make_async_remote_copy(
            src_ref=ref,
            dst_ref=ref,
            send_sem=gate_s.at[number],
            recv_sem=gate_r.at[number],
            device_id=target,
            device_id_type=MESH,
        )

    def gate_line(shift):
        target = {"dp": dp_index((chip + shift) % chips, core)}
        return gate_copy(shift - 1, gate_all.at[me, chip, core], target)

    def gate_tensor(number, chosen):
        target = {"tensor": flipped(me, chosen)}
        return gate_copy(chips - 1 + number, gate_all.at[me, :, core], target)

    def gate_core():
        target = {"dp": dp_index(chip, 1 - core)}
        return gate_copy(chips - 1 + len(peers), gate_all.at[:, :, core], target)

    def start_gate():
        rings[0].finish(store_gate)
        for shift in range(1, chips):
            gate_line(shift).start()

    top = jnp.sum(d_gain[...], axis=0, keepdims=True)
    low = jnp.sum(d_gain_mid[...], axis=0, keepdims=True)
    place8 = lax.broadcasted_iota(jnp.int32, (8, share), 0)
    for index in range(1 << nbits):
        span = slice(index * share, (index + 1) * share)
        gains[index] = jnp.where(
            place8 == 6, top[:, span], jnp.where(place8 == 7, low[:, span], 0.0)
        )

    def gain_copy(number, chosen):
        peer = flipped(me, chosen)
        return pltpu.make_async_remote_copy(
            src_ref=gains.at[peer],
            dst_ref=gains_landed.at[number],
            send_sem=gain_s.at[number],
            recv_sem=gain_r.at[number],
            device_id={"tensor": peer},
            device_id_type=MESH,
        )

    for number, chosen in enumerate(peers):
        gain_copy(number, chosen).start()
    start_gate()
    for distance in far[2:]:
        for ring in rings[1:]:
            ring.send(distance)
    total = own_small[...] + gains[me]
    for number, chosen in enumerate(peers):
        gain_copy(number, chosen).wait_recv()
        total = total + gains_landed[number]
    small[...] = total

    def vec_copy(number, shift, turn):
        other = dp_index((chip + shift) % chips, core + turn * (1 - 2 * core))
        return pltpu.make_async_remote_copy(
            src_ref=small,
            dst_ref=small_landed.at[number],
            send_sem=vec_s.at[number],
            recv_sem=vec_r.at[number],
            device_id={"dp": other},
            device_id_type=MESH,
        )

    for number, (shift, turn) in enumerate(others):
        vec_copy(number, shift, turn).start()

    for shift in range(1, chips):
        gate_line(shift).wait_recv()
    for number, chosen in enumerate(peers):
        gate_tensor(number, chosen).start()
    total = small[...]
    for number, (shift, turn) in enumerate(others):
        vec_copy(number, shift, turn).wait_recv()
        total = total + small_landed[number]
    small_all[me] = total

    def join_copy(number, chosen):
        return pltpu.make_async_remote_copy(
            src_ref=small_all.at[me],
            dst_ref=small_all.at[me],
            send_sem=join_s.at[number],
            recv_sem=join_r.at[number],
            device_id={"tensor": flipped(me, chosen)},
            device_id_type=MESH,
        )

    for number, chosen in enumerate(peers):
        join_copy(number, chosen).start()
    for number, chosen in enumerate(peers):
        gate_tensor(number, chosen).wait_recv()
    gate_core().start()

    def store_in(*targets):
        def store(span, value):
            for number, ref in enumerate(targets):
                ref[span, :] = value[:, number * share : (number + 1) * share]

        return store

    rings[1].finish(store_in(sum_out))
    if tiled:
        rings[2].finish(store_in(sum_y))
        rings[3].finish(store_in(sum_x))
    else:
        rings[2].finish(store_in(sum_y, sum_x))
    gate_core().wait()
    for shift in range(1, chips):
        gate_line(shift).wait_send()
    for number, chosen in enumerate(peers):
        gate_tensor(number, chosen).wait_send()
        gain_copy(number, chosen).wait_send()
        join_copy(number, chosen).wait()
    for number, (shift, turn) in enumerate(others):
        vec_copy(number, shift, turn).wait_send()
    scatter.drain()
    for ring in rings:
        ring.drain()


def in_vmem(count):
    return [pl.BlockSpec(memory_space=pltpu.VMEM)] * count


def call_kernel(kernel, outs, scratch, number, *operands, far_in=(), far_out=(), cost_us=1):
    vmem = pl.BlockSpec(memory_space=pltpu.VMEM)
    far = pl.BlockSpec(memory_space=pl.ANY)
    return pl.pallas_call(
        kernel,
        out_shape=outs,
        in_specs=[far if i in far_in else vmem for i in range(len(operands))],
        out_specs=tuple(far if i in far_out else vmem for i in range(len(outs))),
        scratch_shapes=scratch,
        cost_estimate=pl.CostEstimate(
            flops=0, bytes_accessed=cost_us * 1_000_000, transcendentals=0
        ),
        compiler_params=pltpu.CompilerParams(
            collective_id=number, has_side_effects=True, vmem_limit_bytes=VMEM_BYTES
        ),
    )(*operands)


def sigmoid(values):
    return 1.0 / (1.0 + jnp.exp(-values))


def one_minus_exp(values):
    series = values / 7.0 + 1.0
    for order in (6.0, 5.0, 4.0, 3.0, 2.0):
        series = 1.0 + series * values / order
    return jnp.where(values > -0.3, -values * series, 1.0 - jnp.exp(values))


GELU_K = 0.7978845608028654
GELU_C = 0.044715


def gelu_parts(values):
    square = values * values
    bent = jnp.tanh(GELU_K * values * (1.0 + GELU_C * square))
    gelu = 0.5 * values * (1.0 + bent)
    slope = 0.5 * (1.0 + bent) + 0.5 * values * (1.0 - bent * bent) * GELU_K * (
        1.0 + 3.0 * GELU_C * square
    )
    return gelu, slope


def gate_terms(gate_a, gate_x, soft, since):
    sig_a = sigmoid(gate_a)
    sig_x = sigmoid(gate_x)
    log_decay = -8.0 * sig_a * soft
    decay = jnp.exp(log_decay)
    scale = jnp.sqrt(one_minus_exp(2.0 * log_decay))
    keep = since > 0.5
    return sig_a, sig_x, decay, jnp.where(keep, scale, 1.0), keep


def scan_down(decay, value, carry):
    place = lax.broadcasted_iota(jnp.int32, decay.shape, 0)
    for shift in (1, 2, 4):
        past = place >= shift
        moved = pltpu.roll(value, shift, 0)
        value = jnp.where(past, decay * moved + value, value)
        decay = jnp.where(past, decay * pltpu.roll(decay, shift, 0), decay)
    return decay * carry + value


def scan_up(decay, value, carry):
    place = lax.broadcasted_iota(jnp.int32, decay.shape, 0)
    factor = jnp.where(place < 7, pltpu.roll(decay, 7, 0), 1.0)
    for shift in (1, 2, 4):
        past = place < 8 - shift
        moved = pltpu.roll(value, 8 - shift, 0)
        value = jnp.where(past, factor * moved + value, value)
        factor = jnp.where(past, factor * pltpu.roll(factor, 8 - shift, 0), factor)
    return factor * carry + value


def forward_scan(conv_rows, gates, branch_y, soft, since, mixed, states, between=()):
    total_rows, width = states.shape

    def step(i, carry):
        row = pl.multiple_of(i * CHUNK, CHUNK)
        span = pl.ds(row, CHUNK)
        values = conv_rows(span).astype(F32)
        kept = []
        for at in range(0, CHUNK, 8):
            tile = pl.ds(row + at, 8)
            sig_a, sig_x, decay, scale, keep = gate_terms(
                gates[tile, :width], gates[tile, width:], soft[...], since[tile, :]
            )
            given = values[at : at + 8] * sig_x * scale
            state = scan_down(jnp.where(keep, decay, 0.0), given, carry)
            carry = state[7:8]
            states[tile, :] = state
            kept.append(state * gelu_parts(branch_y[tile, :])[0])
        mixed[span, :] = jnp.concatenate(kept, axis=0).astype(BF16)
        return carry

    steps, stretches = total_rows // CHUNK, len(between) + 1
    carry = jnp.zeros((1, width), F32)
    for stretch in range(stretches):
        first, last = stretch * steps // stretches, (stretch + 1) * steps // stretches
        carry = lax.fori_loop(first, last, step, carry)
        if stretch < len(between):
            between[stretch]()


def forward_scan_kernel(conv, gates, branch_y, soft, since, mixed, states):
    forward_scan(lambda span: conv[span, :], gates, branch_y, soft, since, mixed, states)


def backward_scan(
    d_mixed, conv_rows, gates, branch_y, states, soft, slope_soft, since, d_conv, d_gates, d_branch, d_decay
):
    total_rows, width = states.shape
    d_decay[...] = jnp.zeros_like(d_decay)

    def step(i, carry):
        row = pl.multiple_of(total_rows - CHUNK - i * CHUNK, CHUNK)
        span = pl.ds(row, CHUNK)
        values = conv_rows(span).astype(F32)
        kept = []
        for at in range(CHUNK - 8, -1, -8):
            tile = pl.ds(row + at, 8)
            soft_row = soft[...]
            sig_a, sig_x, decay, scale, keep = gate_terms(
                gates[tile, :width], gates[tile, width:], soft_row, since[tile, :]
            )
            value = values[at : at + 8]
            gelu, slope = gelu_parts(branch_y[tile, :])
            state = states[tile, :]
            upper = d_mixed[tile, :]
            held = jnp.where(keep, decay, 0.0)
            lam = scan_up(held, upper * gelu, carry)
            carry = held[0:1] * lam[0:1]
            d_conv[tile, :] = lam * sig_x * scale
            d_x = lam * value * scale * sig_x * (1.0 - sig_x)
            given = value * sig_x
            d_log = lam * (state - given * scale - given * decay * decay / scale)
            d_log = jnp.where(keep, d_log, 0.0)
            d_a = d_log * (-8.0 * soft_row) * sig_a * (1.0 - sig_a)
            d_decay[...] += d_log * (-8.0 * sig_a) * slope_soft[...]
            kept.append((d_a, d_x, upper * state * slope))
        kept = kept[::-1]
        d_gates[span, :width] = jnp.concatenate([k[0] for k in kept], axis=0).astype(BF16)
        d_gates[span, width:] = jnp.concatenate([k[1] for k in kept], axis=0).astype(BF16)
        d_branch[span, :] = jnp.concatenate([k[2] for k in kept], axis=0).astype(BF16)
        return carry

    lax.fori_loop(0, total_rows // CHUNK, step, jnp.zeros((1, width), F32))


def backward_scan_kernel(
    d_mixed, conv, gates, branch_y, states, soft, slope_soft, since, d_conv, d_gates, d_branch, d_decay
):
    backward_scan(
        d_mixed,
        lambda span: conv[span, :],
        gates,
        branch_y,
        states,
        soft,
        slope_soft,
        since,
        d_conv,
        d_gates,
        d_branch,
        d_decay,
    )


def times_transposed(left, right):
    return lax.dot_general(left, right, (((1,), (1,)), ((), ())), preferred_element_type=F32)


class HalfBlocks:
    def __init__(self, channels, block):
        self.odd = lax.axis_index("tensor") % 2
        self.half = block // 2
        self.block = block
        self.count = channels // block + 1
        self.channels = channels
        self.own = pl.multiple_of(self.odd * self.half, self.half)
        self.shared = (1 - self.odd) * (self.count - 1)
        self.mine_in_block = pl.multiple_of(self.odd * self.half, self.half)
        self.other_in_block = pl.multiple_of((1 - self.odd) * self.half, self.half)
        self.mine = pl.multiple_of((1 - self.odd) * (channels - self.half), self.half)
        self.pair = {"tensor": lax.axis_index("tensor") + 1 - 2 * self.odd}

    def full(self, index):
        block = index + self.odd
        return block, pl.multiple_of(index * self.block + self.odd * self.half, self.half)

    def span(self, block):
        return pl.ds(pl.multiple_of(block * self.block, self.block), self.block)

    def shared_part(self, start):
        return pl.ds(pl.multiple_of(self.shared * self.block + start, self.half), self.half)


PART = 256


def parts(rows, body):
    def step(i, carry):
        body(pl.ds(pl.multiple_of(i * PART, PART), PART))
        return carry

    lax.fori_loop(0, rows // PART, step, 0)


def recurrence_kernel(
    taps,
    nbits,
    branches,
    tap_rows,
    soft,
    since,
    weights,
    cot,
    mixed,
    states,
    window,
    gates,
    cot_all,
    send,
    recv,
    *sems,
):
    total_rows, width = states.shape
    block = weights.shape[2]
    place = HalfBlocks(width, block)
    branch_y, branch_x = branches.at[:, :width], branches.at[:, width:]
    greet(tensor_bits(nbits))
    fetch = Fetch(nbits, cot, cot_all, *sems)
    fetch.local.start()

    def conv(i, before):
        row = pl.multiple_of(i * CHUNK, CHUNK)
        kept = []
        for at in range(0, CHUNK, 8):
            tile = pl.ds(row + at, 8)
            values = branch_x[tile, :]
            line = lax.broadcasted_iota(jnp.int32, values.shape, 0)
            total = values * tap_rows[0:1, :]
            for tap in range(1, taps):
                moved = jnp.where(
                    line < tap, pltpu.roll(before, tap, 0), pltpu.roll(values, tap, 0)
                )
                moved = jnp.where(since[tile, :] > tap - 0.5, moved, 0.0)
                total = total + moved * tap_rows[tap : tap + 1, :]
            kept.append(total)
            before = values
        window[pl.ds(row, CHUNK), pl.ds(place.own, width)] = jnp.concatenate(
            kept, axis=0
        ).astype(BF16)
        return before

    lax.fori_loop(0, total_rows // CHUNK, conv, jnp.zeros((8, width), F32))
    source = window.at[:, place.shared_part(place.mine_in_block)]
    away = pl.multiple_of(place.odd * (place.count - 1) * block + place.mine_in_block, place.half)
    rim = pltpu.make_async_remote_copy(
        src_ref=source,
        dst_ref=window.at[:, pl.ds(away, place.half)],
        send_sem=send.at[0],
        recv_sem=recv.at[0],
        device_id=place.pair,
        device_id_type=MESH,
    )
    rim.start()
    fetch.begin()

    def full(span):
        for index in range(place.count - 1):
            number, at = place.full(index)
            cells = window[span, place.span(number)]
            for s in range(2):
                gates[span, pl.ds(s * width + at, block)] = jnp.dot(
                    cells, weights[s, number], preferred_element_type=F32
                )

    parts(total_rows, full)
    rim.wait()

    def shared(span):
        cells = window[span, place.span(place.shared)]
        for s in range(2):
            gates[span, pl.ds(s * width + place.mine, place.half)] = jnp.dot(
                cells,
                weights[s, place.shared, :, pl.ds(place.mine_in_block, place.half)],
                preferred_element_type=F32,
            )

    parts(total_rows, shared)
    forward_scan(
        lambda span: window[span, pl.ds(place.own, width)],
        gates,
        branch_y,
        soft,
        since,
        mixed,
        states,
        [fetch.advance],
    )
    fetch.finish()


def recurrence_back_kernel(
    taps,
    nbits,
    with_ffn,
    d_mixed,
    window,
    gates,
    branches,
    states,
    tap_rows,
    soft,
    slope_soft,
    since,
    weights,
    *refs,
):
    refs = list(refs)

    def take(count):
        taken = refs[:count]
        del refs[:count]
        return taken

    ffn, middle = take(2) if with_ffn else (None, None)
    d_branches, gate_grad, own_small = take(3)
    mixed = take(1)[0] if with_ffn else None
    d_conv, d_gates, given, taken, sums, send, recv = take(7)
    total_rows, width = states.shape
    block = weights.shape[2]
    place = HalfBlocks(width, block)
    half = place.half
    branch_y, branch_x = branches.at[:, :width], branches.at[:, width:]
    d_branch_y, d_branch_x = d_branches.at[:, :width], d_branches.at[:, width:]
    greet(tensor_bits(nbits))
    if with_ffn:
        scatter = Scatter(ffn, *take(2), middle.shape[0], nbits, *take(2))
        scatter.begin()
    backward_scan(
        d_mixed,
        lambda span: window[span, pl.ds(place.own, width)],
        gates,
        branch_y,
        states,
        soft,
        slope_soft,
        since,
        d_conv,
        d_gates,
        d_branch_y,
        sums.at[taps],
    )

    def to_pair(span):
        total = jnp.zeros((PART, half), F32)
        for s in range(2):
            total = total + times_transposed(
                d_gates[span, pl.ds(s * width + place.mine, half)],
                weights[
                    s,
                    place.shared,
                    pl.ds(place.other_in_block, half),
                    pl.ds(place.mine_in_block, half),
                ],
            )
        given[span, :] = total.astype(BF16)

    parts(total_rows, to_pair)
    rim = pltpu.make_async_remote_copy(
        src_ref=given,
        dst_ref=taken,
        send_sem=send.at[0],
        recv_sem=recv.at[0],
        device_id=place.pair,
        device_id_type=MESH,
    )
    rim.start()

    def full(span):
        for index in range(place.count - 1):
            number, at = place.full(index)
            total = d_conv[span, pl.ds(at, block)]
            for s in range(2):
                total = total + times_transposed(
                    d_gates[span, pl.ds(s * width + at, block)], weights[s, number]
                )
            d_conv[span, pl.ds(at, block)] = total
        total = d_conv[span, pl.ds(place.mine, half)]
        for s in range(2):
            total = total + times_transposed(
                d_gates[span, pl.ds(s * width + place.mine, half)],
                weights[
                    s,
                    place.shared,
                    pl.ds(place.mine_in_block, half),
                    pl.ds(place.mine_in_block, half),
                ],
            )
        d_conv[span, pl.ds(place.mine, half)] = total

    parts(total_rows, full)
    if with_ffn:
        scatter.advance(0)
    units = width // half
    for index in range(units):
        number = (index + place.odd) // 2
        cells = window[:, place.span(number)]
        both = jnp.concatenate(
            [d_gates[:, s * width + index * half : s * width + (index + 1) * half] for s in range(2)],
            axis=1,
        )
        found = lax.dot_general(
            cells, both, (((0,), (0,)), ((), ())), preferred_element_type=F32
        ).astype(BF16)
        gate_grad[2 * index] = found[:, :half]
        gate_grad[2 * index + 1] = found[:, half:]
    rim.wait()

    def add(span):
        d_conv[span, pl.ds(place.mine, half)] += taken[span, :].astype(F32)

    parts(total_rows, add)
    for tap in range(taps):
        sums[tap] = jnp.zeros((8, width), F32)

    def conv(i, after):
        row = pl.multiple_of(total_rows - CHUNK - i * CHUNK, CHUNK)
        kept = []
        for at in range(CHUNK - 8, -1, -8):
            tile = pl.ds(row + at, 8)
            values = d_conv[tile, :]
            line = lax.broadcasted_iota(jnp.int32, values.shape, 0)
            below = branch_x[tile, :]
            higher = pl.multiple_of((row + at - 8 + total_rows) % total_rows, 8)
            above = branch_x[pl.ds(higher, 8), :]
            total = values * tap_rows[0:1, :]
            sums[0] += values * below
            masked = []
            for tap in range(1, taps):
                here = jnp.where(since[tile, :] > tap - 0.5, values, 0.0)
                masked.append(here)
                moved = jnp.where(
                    line < 8 - tap,
                    pltpu.roll(here, 8 - tap, 0),
                    pltpu.roll(after[tap - 1], 8 - tap, 0),
                )
                total = total + moved * tap_rows[tap : tap + 1, :]
                source = jnp.where(
                    line < tap, pltpu.roll(above, tap, 0), pltpu.roll(below, tap, 0)
                )
                sums[tap] += here * source
            after = tuple(masked)
            kept.append(total)
        d_branch_x[pl.ds(row, CHUNK), :] = jnp.concatenate(kept[::-1], axis=0).astype(BF16)
        return after

    none = jnp.zeros((8, width), F32)
    lax.fori_loop(0, total_rows // CHUNK, conv, (none,) * (taps - 1))
    line = lax.broadcasted_iota(jnp.int32, (8, width), 0)
    total = jnp.zeros((8, width), F32)
    for tap in range(taps + 1):
        row = jnp.sum(sums[tap], axis=0, keepdims=True)
        total = jnp.where(line == tap, row, total)
    own_small[...] = total
    if with_ffn:
        for step in range(1, nbits):
            scatter.advance(step)

        def result(row):
            span = pl.ds(row, CHUNK)
            mixed[span, :] = (middle[span, :] + scatter.total(row, CHUNK)).astype(BF16)

        chunks(middle.shape[0], result)
        scatter.drain()


def finish_kernel(taps, gates, small, in_y, in_x, whole, out_y, out_x, conv, decay, gain_in, gain_mid):
    blocks = whole.shape[1]
    pieces = gates.shape[0] // blocks

    def block(n, carry):
        for piece in range(pieces):
            for s in range(2):
                whole[s, n, :, piece * 128 : (piece + 1) * 128] = gates[
                    n * pieces + piece, s
                ].astype(F32)
        return carry

    lax.fori_loop(0, blocks, block, 0)
    out_y[...] = in_y[...]
    out_x[...] = in_x[...]
    share = small.shape[2]
    for index in range(small.shape[0]):
        span = slice(index * share, (index + 1) * share)
        conv[:, span] = small[index, :taps, :]
        decay[:, span] = small[index, taps : taps + 1, :]
        gain_in[:, span] = small[index, 6:7, :]
        gain_mid[:, span] = small[index, 7:8, :]


def finish(gate_all, small_all, sum_y, sum_x, taps, gate_shape):
    _, blocks, block, _ = gate_shape
    unit = gate_all.shape[-1]
    pieces = block // unit
    width = small_all.shape[0] * small_all.shape[2]
    if unit != 128:
        whole = gate_all.reshape(blocks, pieces, 2, block, unit).transpose(2, 0, 3, 1, 4)
        summed = small_all.transpose(1, 0, 2).reshape(8, width)
        whole = whole.reshape(gate_shape).astype(F32)
        rows = (summed[:taps], summed[taps], summed[6], summed[7])
        return (whole, sum_y, sum_x) + rows
    shape = jax.ShapeDtypeStruct
    row = shape((1, width), F32)
    found = scan_call(
        partial(finish_kernel, taps),
        (
            shape(gate_shape, F32),
            shape(sum_y.shape, F32),
            shape(sum_x.shape, F32),
            shape((taps, width), F32),
            row,
            row,
            row,
        ),
        gate_all.reshape(blocks * pieces, 2, block, unit),
        small_all,
        sum_y,
        sum_x,
    )
    return found[:4] + tuple(one.reshape(width) for one in found[4:])


def scan_call(kernel, outs, *operands):
    return pl.pallas_call(
        kernel,
        out_shape=outs,
        in_specs=in_vmem(len(operands)),
        out_specs=tuple(in_vmem(len(outs))),
        compiler_params=pltpu.CompilerParams(vmem_limit_bytes=VMEM_BYTES),
    )(*operands)


class Rim:
    def __init__(self, route, back, source, first, width, room):
        self.route, self.back = route, back
        self.source, self.first, self.width = source, first, width
        self.room = room

    def fetch(self, values):
        part = lax.dynamic_slice_in_dim(values, self.source, self.width, 1)
        return lax.ppermute(part, "tensor", self.route)

    def give(self, part):
        return lax.ppermute(part, "tensor", self.back)

    def add(self, values, part):
        zeros = jnp.zeros(values.shape, F32)
        return values + lax.dynamic_update_slice_in_dim(
            zeros, part.astype(F32), self.source, 1
        )

    def window(self, channels):
        return (channels // self.width + 4) * self.width


def gate_rims(channels, block_size, ntensor, offset):
    up = [(i, i + 1) for i in range(ntensor - 1)]
    down = [(i + 1, i) for i in range(ntensor - 1)]
    last = jnp.int32(channels - block_size)
    return [
        Rim(up, down, last, offset - block_size, block_size, block_size),
        Rim(down, up, jnp.int32(0), offset + channels, block_size, block_size),
    ]


def same_block(first, count, offset, channels, block_size):
    rows = (first + jnp.arange(count, dtype=jnp.int32))[:, None]
    columns = (offset + jnp.arange(channels, dtype=jnp.int32))[None, :]
    return (rows + block_size) // block_size == (columns + block_size) // block_size


def gate_dense(gate_w, offset, first, count):
    block_size = gate_w.shape[2]
    total = gate_w.shape[1] * block_size
    channels = total // lax.axis_size("tensor")
    columns = gate_w.transpose(2, 0, 1, 3).reshape(block_size, 2, total)
    columns = lax.dynamic_slice_in_dim(columns, offset, channels, 2)
    copies = -(-count // block_size) + 1
    tall = jnp.concatenate([columns] * copies, axis=0)
    tall = lax.dynamic_slice_in_dim(tall, (first + block_size) % block_size, count, 0)
    same = same_block(first, count, offset, channels, block_size)
    dense = jnp.where(same[:, None, :], tall, jnp.zeros_like(tall))
    return dense.reshape(count, 2 * channels)


def doc_starts(seg_ids, seq_len):
    places = jnp.arange(seg_ids.shape[0], dtype=jnp.int32)
    before = jnp.concatenate([seg_ids[:1], seg_ids[:-1]])
    resets = (places % seq_len == 0) | (seg_ids != before)
    starts = lax.cummax(jnp.where(resets, places, jnp.zeros_like(places)), axis=0)
    return starts


def causal_conv(starts, values, kernel):
    places = jnp.arange(values.shape[0], dtype=jnp.int32)
    total = values * kernel[0]
    for offset_k in range(1, kernel.shape[0]):
        moved = jnp.concatenate(
            [jnp.zeros((offset_k, values.shape[1]), values.dtype), values[:-offset_k]], axis=0
        )
        valid = (places - offset_k >= starts)[:, None]
        total = total + jnp.where(valid, moved, jnp.zeros_like(moved)) * kernel[offset_k]
    return total


def geglu(gate_val, up_val):
    return jax.nn.gelu(gate_val, approximate=True) * up_val


def rows_times(left, right):
    return lax.dot_general(left, right, (((1,), (1,)), ((), ())), preferred_element_type=F32)


def rows_back(lefts, rights):
    total = rows_times(lefts[0], rights[0])
    return total + rows_times(lefts[1], rights[1])


def inner_rows(left, right):
    return lax.dot_general(left, right, (((0,), (0,)), ((), ())), preferred_element_type=F32)


def halved(grad, ndp):
    return grad.reshape(ndp // 2, 2, grad.shape[0] // ndp, grad.shape[1])


def body(
    tokens,
    segments,
    cotangent,
    norm_gain,
    w_y,
    w_x,
    conv_w,
    gate_w,
    decay_param,
    w_out,
    mlp_gain,
    w_gate,
    w_up,
    w_down,
):
    ntensor = lax.axis_size("tensor")
    ndp = lax.axis_size("dp")
    nbits = log2_of(ntensor)
    tindex = lax.axis_index("tensor")
    own_rows, width = tokens.shape
    group_rows = own_rows * ntensor
    block_size = gate_w.shape[2]
    nblocks = gate_w.shape[1]
    dp_rows, channels = w_y.shape
    taps = conv_w.shape[0]
    offset = tindex * channels
    shape = jax.ShapeDtypeStruct
    gain_in = norm_gain.reshape(1, width)
    gain_mid = mlp_gain.reshape(1, width)
    seg_rows_of = own_rows // 128
    tiled = channels % 128 == 0
    w_yx = (w_y, w_x) if tiled else (jnp.concatenate([w_y, w_x], axis=1),)
    normed_rows, seg_all, wyx_loc, wout_loc = call_kernel(
        partial(enter_kernel, nbits, len(w_yx)),
        (
            shape((group_rows, width), BF16),
            shape((ntensor, seg_rows_of, 128), jnp.int32),
            shape((dp_rows * ndp, 2 * channels), BF16),
            shape((dp_rows * ndp, channels), BF16),
        ),
        gather_sems(nbits)
        + [pltpu.SemaphoreType.DMA((ntensor - 1,)), pltpu.SemaphoreType.DMA((ntensor - 1,))]
        + [pltpu.SemaphoreType.DMA((1,))]
        + line_sems(ndp) * (len(w_yx) + 1),
        0,
        tokens,
        segments.reshape(seg_rows_of, 128),
        gain_in,
        *w_yx,
        w_out,
        far_in=tuple(range(3, 4 + len(w_yx))),
        far_out=(2, 3),
    )
    units = w_gate.shape[1]
    w_both = jnp.concatenate([w_gate, w_up], axis=1)
    w_both, w_down, normed_rows = lax.optimization_barrier((w_both, w_down, normed_rows))
    both_loc = lax.all_gather(w_both, "dp", axis=0, tiled=True)
    wd_loc = lax.all_gather(w_down, "dp", axis=0, tiled=True)
    seg_rows = seg_all.reshape(group_rows)
    starts = doc_starts(seg_rows, group_rows)
    conv_loc = lax.dynamic_slice_in_dim(conv_w, offset, channels, 1)
    decay_loc = lax.dynamic_slice_in_dim(decay_param, offset, channels, 0).reshape(1, channels)
    soft = jax.nn.softplus(decay_loc)
    slope_soft = jax.nn.sigmoid(decay_loc)
    half_blocks = (
        channels % block_size == block_size // 2 and ntensor % 2 == 0 and block_size % 256 == 0
    )
    since = (jnp.arange(group_rows, dtype=jnp.int32) - starts).astype(F32)[:, None]
    branches = jnp.dot(normed_rows, wyx_loc, preferred_element_type=F32)
    if half_blocks:
        span_blocks = channels // block_size + 1
        w_window = lax.dynamic_slice_in_dim(gate_w, offset // block_size, span_blocks, 1)
        taps_pad = jnp.concatenate([conv_loc, jnp.zeros((8 - taps, channels), F32)], axis=0)
        mixed_low, states, window, gate_pre, cot_rows = call_kernel(
            partial(recurrence_kernel, taps, nbits),
            (
                shape((group_rows, channels), BF16),
                shape((group_rows, channels), F32),
                shape((group_rows, span_blocks * block_size), BF16),
                shape((group_rows, 2 * channels), F32),
                shape((group_rows, width), BF16),
            ),
            [pltpu.SemaphoreType.DMA((1,)), pltpu.SemaphoreType.DMA((1,))]
            + fetch_scratch(nbits),
            5,
            branches,
            taps_pad,
            soft,
            since,
            w_window,
            cotangent,
        )
    else:
        branch_y, branch_x = branches[:, :channels], branches[:, channels:]
        (cot_rows,) = call_kernel(
            partial(fetch_kernel, nbits),
            (shape((group_rows, width), BF16),),
            fetch_scratch(nbits),
            5,
            cotangent,
        )
        rims = gate_rims(channels, block_size, ntensor, offset)
        own_dense = gate_dense(gate_w, offset, offset, channels)
        rim_dense = [gate_dense(gate_w, offset, rim.first, rim.width) for rim in rims]
        conv_out, conv_pull = jax.vjp(partial(causal_conv, starts), branch_x, conv_loc)
        conv_low = conv_out.astype(BF16)
        rim_cells = [rim.fetch(conv_low) for rim in rims]
        gate_pre = jnp.dot(conv_low, own_dense, preferred_element_type=F32)
        for cells, dense in zip(rim_cells, rim_dense):
            gate_pre = gate_pre + jnp.dot(cells, dense, preferred_element_type=F32)
        mixed_low, states = scan_call(
            forward_scan_kernel,
            (shape((group_rows, channels), BF16), shape((group_rows, channels), F32)),
            conv_low,
            gate_pre,
            branch_y,
            soft,
            since,
        )
    middle, mid_rows = call_kernel(
        partial(middle_kernel, nbits),
        (shape((own_rows, width), F32), shape((group_rows, width), BF16)),
        scatter_scratch(own_rows, width, nbits) + gather_sems(nbits),
        1,
        rows_times(mixed_low, wout_loc).astype(BF16),
        tokens,
        gain_mid,
    )
    pre = jnp.dot(mid_rows, both_loc, preferred_element_type=F32)
    hidden, act_pull = jax.vjp(geglu, pre[:, :units], pre[:, units:])
    hidden_low = hidden.astype(BF16)
    grad_wd = inner_rows(cot_rows, hidden_low).astype(BF16)
    sum_wd = lax.psum_scatter(grad_wd, "dp", scatter_dimension=0, tiled=True)
    grad_wd, wd_loc = lax.optimization_barrier((grad_wd, wd_loc))
    d_hidden = jnp.dot(cot_rows, wd_loc, preferred_element_type=F32)
    d_gate, d_up = act_pull(d_hidden)
    d_pre = jnp.concatenate([d_gate.astype(BF16), d_up.astype(BF16)], axis=1)
    grad_both = inner_rows(mid_rows, d_pre).astype(BF16)
    sum_both = lax.psum_scatter(grad_both, "dp", scatter_dimension=0, tiled=True)
    d_pre, grad_both = lax.optimization_barrier((d_pre, grad_both))
    d_mid_part = rows_times(d_pre, both_loc).astype(BF16)
    d_middle, d_mixer, d_gain_mid = call_kernel(
        partial(turn_kernel, nbits),
        (
            shape((own_rows, width), F32),
            shape((group_rows, width), BF16),
            shape((8, width), F32),
        ),
        scatter_scratch(own_rows, width, nbits) + gather_sems(nbits),
        2,
        d_mid_part,
        cotangent,
        middle,
        gain_mid,
    )
    d_mixer, sum_wd = lax.optimization_barrier((d_mixer, sum_wd))
    d_mixed_in = jnp.dot(d_mixer, wout_loc, preferred_element_type=F32)
    unit = math.gcd(channels, block_size)
    ffn_part = rows_times(hidden_low, wd_loc).astype(BF16)
    merged = half_blocks and nbits <= 2
    if half_blocks:
        found = call_kernel(
            partial(recurrence_back_kernel, taps, nbits, merged),
            (
                shape((group_rows, 2 * channels), BF16),
                shape((channels // unit * 2, block_size, unit), BF16),
                shape((8, channels), F32),
            )
            + ((shape((own_rows, width), BF16),) if merged else ()),
            [
                pltpu.VMEM((group_rows, channels), F32),
                pltpu.VMEM((group_rows, 2 * channels), BF16),
                pltpu.VMEM((group_rows, unit), BF16),
                pltpu.VMEM((group_rows, unit), BF16),
                pltpu.VMEM((taps + 1, 8, channels), F32),
                pltpu.SemaphoreType.DMA((1,)),
                pltpu.SemaphoreType.DMA((1,)),
            ]
            + (scatter_scratch(own_rows, width, nbits) if merged else []),
            6,
            d_mixed_in,
            window,
            gate_pre,
            branches,
            states,
            taps_pad,
            soft,
            slope_soft,
            since,
            w_window,
            *((ffn_part, middle) if merged else ()),
        )
        d_branches, gate_grad, own_small = found[:3]
        d_branches, sum_both = lax.optimization_barrier((d_branches, sum_both))
        gate_grad = gate_grad.reshape(channels // unit * 2 * block_size, unit)
    else:
        d_conv, d_gate_low, d_branch_y, d_decay = scan_call(
            backward_scan_kernel,
            (
                shape((group_rows, channels), F32),
                shape((group_rows, 2 * channels), BF16),
                shape((group_rows, channels), BF16),
                shape((8, channels), F32),
            ),
            d_mixed_in,
            conv_low,
            gate_pre,
            branch_y,
            states,
            soft,
            slope_soft,
            since,
        )
        given = [rows_times(d_gate_low, dense).astype(BF16) for dense in rim_dense]
        taken = [rim.give(part) for rim, part in zip(rims, given)]
        d_conv_out = d_conv + rows_times(d_gate_low, own_dense)
        for rim, part in zip(rims, taken):
            d_conv_out = rim.add(d_conv_out, part)
        d_branch_x, grad_conv_loc = conv_pull(d_conv_out)
        d_branches = jnp.concatenate([d_branch_y, d_branch_x.astype(BF16)], axis=1)
        base = offset // block_size * block_size - rims[0].room
        window_rows = rims[0].window(channels)
        picked = jnp.zeros((window_rows, 2 * channels), F32)
        for first, cells in [(offset, conv_low)] + [(r.first, c) for r, c in zip(rims, rim_cells)]:
            part = inner_rows(cells, d_gate_low)
            same = same_block(first, cells.shape[1], offset, channels, block_size)
            part = jnp.where(jnp.concatenate([same, same], axis=1), part, 0.0)
            picked = lax.dynamic_update_slice(picked, part, (first - base, jnp.int32(0)))
        picked = picked.reshape(window_rows // block_size, block_size, 2, channels // unit, unit)
        gate_grad = picked.sum(axis=0).astype(BF16).transpose(2, 1, 0, 3)
        gate_grad = gate_grad.reshape(channels // unit * 2 * block_size, unit)
        own_small = jnp.concatenate(
            [
                grad_conv_loc,
                jnp.sum(d_decay, axis=0, keepdims=True),
                jnp.zeros((7 - taps, channels), F32),
            ],
            axis=0,
        )

    grad_wout = inner_rows(d_mixer, mixed_low).astype(BF16)
    grad_wyx = inner_rows(normed_rows, d_branches).astype(BF16)
    d_normed = rows_times(d_branches, wyx_loc).astype(BF16)

    pieces = [halved(grad, ndp) for grad in (gate_grad, grad_wout, grad_wyx)]
    peers = ntensor - 1
    gate_rows = gate_grad.shape[0] // ndp
    dma = pltpu.SemaphoreType.DMA
    scratch = scatter_scratch(own_rows, width, nbits)
    scratch += line_scratch(ndp, gate_rows, unit) + line_scratch(ndp, dp_rows, channels)
    if tiled:
        scratch += line_scratch(ndp, dp_rows, channels) * 2
    else:
        scratch += line_scratch(ndp, dp_rows, 2 * channels)
    scratch += [
        pltpu.VMEM((8, width), F32),
        pltpu.VMEM((ntensor, 8, channels), F32),
        pltpu.VMEM((peers, 8, channels), F32),
        pltpu.VMEM((8, channels), F32),
        pltpu.VMEM((ndp - 1, 8, channels), F32),
    ]
    scratch += [dma((peers,)), dma((peers,)), dma((ndp - 1,)), dma((ndp - 1,))]
    scratch += [dma((peers,)), dma((peers,)), dma((peers + ndp,)), dma((peers + ndp,))]
    grad_input, sum_wout, sum_wy, sum_wx, gate_all, small_all = call_kernel(
        partial(leave_kernel, nbits, tiled),
        (shape((own_rows, width), F32),)
        + (shape((dp_rows, channels), F32),) * 3
        + (
            shape((ntensor, ndp // 2, 2, gate_rows, unit), BF16),
            shape((ntensor, 8, channels), F32),
        ),
        scratch,
        3,
        d_normed,
        tokens,
        d_middle,
        gain_in,
        own_small,
        d_gain_mid,
        *pieces,
        far_in=(6, 7, 8),
    )
    if merged:
        mixed = found[3]
    else:
        (mixed,) = call_kernel(
            partial(result_kernel, nbits),
            (shape((own_rows, width), BF16),),
            scatter_scratch(own_rows, width, nbits),
            4,
            ffn_part,
            middle,
        )
    sum_gate, sum_wy, sum_wx, sum_conv, sum_decay, sum_gain_in, sum_gain_mid = finish(
        gate_all, small_all, sum_wy, sum_wx, taps, gate_w.shape
    )
    return (
        mixed,
        grad_input,
        sum_gain_in,
        sum_wy,
        sum_wx,
        sum_conv,
        sum_gate,
        sum_decay,
        sum_wout,
        sum_gain_mid,
        sum_both[:, :units].astype(F32),
        sum_both[:, units:].astype(F32),
        sum_wd.astype(F32),
    )


def solution(mesh):
    split = P(("dp", "tensor"), None)
    weight = P("dp", "tensor")
    return jax.shard_map(
        body,
        mesh=mesh,
        in_specs=(
            split,
            P(("dp", "tensor")),
            split,
            P(),
            weight,
            weight,
            P(),
            P(),
            P(),
            weight,
            P(),
            weight,
            weight,
            weight,
        ),
        out_specs=(
            split,
            split,
            P(),
            weight,
            weight,
            P(),
            P(),
            P(),
            weight,
            P(),
            weight,
            weight,
            weight,
        ),
        check_vma=False,
    )
```

profile of v0, /device:TPU:0, one launch (start us, length us, event | category | flops | bytes accessed | tf_op | source)
XLA Modules:
  0.0 833.7 jit_solution(6599364658927090915)
XLA Ops:
  8.7 3.3 pad_maximum_fusion.1
  12.0 91.7 %shard_map.237 = (bf16[1024,2560]{1,0:T(8,128)(2,1)}, s32[4,2,128]{2,1,0:T(2,128)}, bf16[2560,1280]{1,0:T(8,128)(2,1)}, bf16[2560,640]{1,0:T(8,128)(2,1)}) custom-call(bf16[256,2560]{1,0:T(8,128)(2,1)} %refs_1_.3, s32[2,128]{1,0:T(2,128)} %bitcast.48, f32[1,2560]{1,0:T(1,128)} %reshape.121.gain.refs_3_, bf16[320,640]{1,0:T(8,128)(2,1)} %refs_0_.1, ...), custom_call_target="tpu_custom_call" | custom-call | bytes 1000000 | tf_op jit(solution)/shard_map/pallas_call | solution.py:878
  113.1 14.0 %fusion.12.branches = f32[1024,1280]{1,0:T(8,128)} fusion(bf16[1024,2560]{1,0:T(8,128)(2,1)} %get-tuple-element.54, bf16[2560,1280]{1,0:T(8,128)(2,1)} %get-tuple-element.55), kind=kOutput, calls=%fused_computation.41 | convolution fusion | flops 6710886400 | bytes 17039360 | tf_op jit(solution)/shard_map/dot_general | solution.py:1583
  127.1 66.1 %shard_map.238 = (bf16[1024,640]{1,0:T(8,128)(2,1)}, f32[1024,640]{1,0:T(8,128)}, bf16[1024,768]{1,0:T(8,128)(2,1)}, f32[1024,1280]{1,0:T(8,128)}, bf16[1024,2560]{1,0:T(8,128)(2,1)}) custom-call(f32[1024,1280]{1,0:T(8,128)} %fusion.12.branches, f32[8,640]{1,0:T(8,128)} %concatenate.15.tap_rows, f32[1,640]{1,0:T(1,128)} %select_n.32.soft, ...), custom_call_target="tpu_custom_call" | custom-call | bytes 1000000 | tf_op jit(solution)/shard_map/pallas_call | solution.py:878
  193.2 7.4 convolution_convert_fusion.4.mixer
  200.6 97.2 %shard_map.239 = (f32[256,2560]{1,0:T(8,128)}, bf16[1024,2560]{1,0:T(8,128)(2,1)}) custom-call(bf16[1024,2560]{1,0:T(8,128)(2,1)} %convolution_convert_fusion.4.mixer, bf16[256,2560]{1,0:T(8,128)(2,1)} %refs_1_.3, f32[1,2560]{1,0:T(1,128)} %reshape.125.gain), custom_call_target="tpu_custom_call" | custom-call | bytes 1000000 | tf_op jit(solution)/shard_map/pallas_call | solution.py:878
  297.8 25.0 %fusion.13 = f32[1024,3840]{1,0:T(8,128)S(1)} fusion(bf16[1024,2560]{1,0:T(8,128)(2,1)} %get-tuple-element.60, bf16[2560,3840]{1,0:T(8,128)(2,1)} %all-gather.3.cloned.1.call-done), kind=kOutput, calls=%fused_computation.42 | convolution fusion | flops 20132659200 | bytes 40632320 | tf_op jit(solution)/shard_map/dot_general | solution.py:1643
  330.3 15.7 %convolution_convert_fusion.2 = bf16[2560,1920]{1,0:T(8,128)(2,1)} fusion(bf16[1024,2560]{1,0:T(8,128)(2,1)} %get-tuple-element.57, bf16[1024,1920]{1,0:T(8,128)(2,1)S(1)} %multiply_convert_fusion.1), kind=kOutput, calls=%fused_computation.2 | convolution fusion | flops 10071244800 | bytes 19005440 | tf_op jit(solution)/shard_map/dot_general | solution.py:1507
  346.1 25.6 %all-gather.5.cloned.1.call-done = bf16[2560,1920]{1,0:T(8,128)(2,1)} async-done(((bf16[320,1920]{1,0:T(8,128)(2,1)}), bf16[2560,1920]{1,0:T(8,128)(2,1)}) %all-gather.5.cloned.1.call-update) | async-done | bytes 9830416 | tf_op jit(solution)/shard_map/all_gather | solution.py:1572
  371.7 24.7 %fusion.6 = (bf16[1024,1920]{1,0:T(8,128)(2,1)S(1)}, bf16[1024,1920]{1,0:T(8,128)(2,1)S(1)}) fusion(f32[1024,3840]{1,0:T(8,128)} %copy-done.2, bf16[1024,2560]{1,0:T(8,128)(2,1)} %get-tuple-element.57, bf16[2560,1920]{1,0:T(8,128)(2,1)} %all-gather.5.cloned.1.call-done), kind=kOutput, calls=%fused_computation.11 | convolution fusion | flops 10113515520 | bytes 38666240 | tf_op jit(solution)/shard_map/dot_general | solution.py:1649
  399.5 26.7 %convolution_convert_fusion = bf16[2560,3840]{1,0:T(8,128)(2,1)} fusion(bf16[1024,2560]{1,0:T(8,128)(2,1)} %get-tuple-element.60, bf16[1024,1920]{1,0:T(8,128)(2,1)S(1)} %get-tuple-element.94, bf16[1024,1920]{1,0:T(8,128)(2,1)S(1)} %get-tuple-element.93), kind=kOutput, calls=%fused_computation | convolution fusion | flops 20158218240 | bytes 32768000 | tf_op jit(solution)/shard_map/dot_general | solution.py:1507
  426.9 6.9 pad_maximum_fusion
  433.8 27.1 %convolution_convert_fusion.6.d_norm = bf16[1024,2560]{1,0:T(8,128)(2,1)} fusion(bf16[1024,3840]{1,0:T(8,128)(2,1)} %pad_maximum_fusion, bf16[2560,3840]{1,0:T(8,128)(2,1)} %all-gather.3.cloned.1.call-done), kind=kOutput, calls=%fused_computation.19 | convolution fusion | flops 20135280640 | bytes 32768000 | tf_op jit(solution)/shard_map/dot_general | solution.py:1498
  460.9 102.6 %shard_map.240 = (f32[256,2560]{1,0:T(8,128)}, bf16[1024,2560]{1,0:T(8,128)(2,1)}, f32[8,2560]{1,0:T(8,128)}) custom-call(bf16[1024,2560]{1,0:T(8,128)(2,1)} %convolution_convert_fusion.6.d_norm, bf16[256,2560]{1,0:T(8,128)(2,1)} %cot.3, f32[256,2560]{1,0:T(8,128)} %get-tuple-element.65.middle.refs_1_, f32[1,2560]{1,0:T(1,128)} %reshape.125.gain), custom_call_target="tpu_custom_call" | custom-call | bytes 1000000 | tf_op jit(solution)/shard_map/pallas_call | solution.py:878
  563.5 15.2 %convolution_convert_fusion.3.refs_0_ = bf16[1024,2560]{1,0:T(8,128)(2,1)} fusion(bf16[1024,1920]{1,0:T(8,128)(2,1)S(1)} %copy-done.4, bf16[2560,1920]{1,0:T(8,128)(2,1)} %all-gather.5.cloned.1.call-done), kind=kOutput, calls=%fused_computation.16 | convolution fusion | flops 10068951040 | bytes 19005440 | tf_op jit(solution)/shard_map/dot_general | solution.py:1498
  578.7 9.7 %fusion.14.d_mixed = f32[1024,640]{1,0:T(8,128)} fusion(bf16[1024,2560]{1,0:T(8,128)(2,1)} %get-tuple-element.67, bf16[2560,640]{1,0:T(8,128)(2,1)} %get-tuple-element.59), kind=kOutput, calls=%fused_computation.43 | convolution fusion | flops 3355443200 | bytes 11141120 | tf_op jit(solution)/shard_map/dot_general | solution.py:1671
  588.4 61.1 %shard_map.241 = (bf16[1024,1280]{1,0:T(8,128)(2,1)}, bf16[10,256,128]{2,1,0:T(8,128)(2,1)}, f32[8,640]{1,0:T(8,128)}, bf16[256,2560]{1,0:T(8,128)(2,1)}) custom-call(f32[1024,640]{1,0:T(8,128)} %fusion.14.d_mixed, bf16[1024,768]{1,0:T(8,128)(2,1)} %get-tuple-element.68.window, f32[1024,1280]{1,0:T(8,128)} %get-tuple-element.69.gates, ...), custom_call_target="tpu_custom_call" | custom-call | bytes 1000000 | tf_op jit(solution)/shard_map/pallas_call | solution.py:878
  651.1 7.6 convolution_convert_fusion.7
  658.7 13.1 %reduce-scatter.5.cloned.1.call-done = bf16[320,3840]{1,0:T(8,128)(2,1)} async-done(((bf16[2560,3840]{1,0:T(8,128)(2,1)}), bf16[320,3840]{1,0:T(8,128)(2,1)}) %reduce-scatter.5.cloned.1.call-update) | async-done | bytes 2457616 | tf_op jit(solution)/shard_map/reduce_scatter | solution.py:1653
  671.8 11.5 %convolution_convert_fusion.5.refs_0_ = bf16[1024,2560]{1,0:T(8,128)(2,1)} fusion(bf16[1024,1280]{1,0:T(8,128)(2,1)S(1)} %copy-done.12, bf16[2560,1280]{1,0:T(8,128)(2,1)} %get-tuple-element.55), kind=kOutput, calls=%fused_computation.18 | convolution fusion | flops 6713507840 | bytes 14417920 | tf_op jit(solution)/shard_map/dot_general | solution.py:1498
  683.3 10.7 %convolution_convert_fusion.1 = bf16[2560,1280]{1,0:T(8,128)(2,1)} fusion(bf16[1024,2560]{1,0:T(8,128)(2,1)} %get-tuple-element.54, bf16[1024,1280]{1,0:T(8,128)(2,1)S(1)} %copy-done.12), kind=kOutput, calls=%fused_computation.1 | convolution fusion | flops 6714163200 | bytes 14417920 | tf_op jit(solution)/shard_map/dot_general | solution.py:1507
  694.0 113.7 %shard_map.242 = (f32[256,2560]{1,0:T(8,128)}, f32[320,640]{1,0:T(8,128)}, f32[320,640]{1,0:T(8,128)}, f32[320,640]{1,0:T(8,128)}, bf16[4,4,2,320,128]{4,3,2,1,0:T(8,128)(2,1)}, /*index=5*/f32[4,8,640]{2,1,0:T(8,128)}) custom-call(bf16[1024,2560]{1,0:T(8,128)(2,1)} %convolution_convert_fusion.5.refs_0_, bf16[256,2560]{1,0:T(8,128)(2,1)} %refs_1_.3, ...), custom_call_target="tpu_custom_call" | custom-call | bytes 1000000 | tf_op jit(solution)/shard_map/pallas_call | solution.py:878
  810.4 5.6 shard_map.243
  822.4 3.4 copy.32
  (66 shorter events, 33.7 us)
Async XLA Ops:
  7.2 104.1 %copy-start = (bf16[2,10,256,256]{3,2,1,0:T(8,128)(2,1)S(1)}, bf16[2,10,256,256]{3,2,1,0:T(8,128)(2,1)}, u32[]{:S(2)}) copy-start(bf16[2,10,256,256]{3,2,1,0:T(8,128)(2,1)} %param.21) | copy-start | bytes 7864324
  7.2 290.6 %all-gather.3.cloned.1.call-start = ((), (), s32[]{:S(2)}) async-start(), calls=%async_computation.2 | async-start | bytes 22118400 | tf_op jit(solution)/shard_map/all_gather | solution.py:1571
  8.7 97.2 %copy-start.10 = (f32[2560]{0:T(1024)S(1)}, f32[2560]{0:T(1024)}, u32[]{:S(2)}) copy-start(f32[2560]{0:T(1024)} %param.24) | copy-start | bytes 30724
  103.7 268.0 %all-gather.5.cloned.1.call-start = ((), (), s32[]{:S(2)}) async-start(), calls=%async_computation.3 | async-start | bytes 11059200 | tf_op jit(solution)/shard_map/all_gather | solution.py:1572
  104.4 474.3 %reduce-scatter.3.cloned.1.call-start = ((), (), s32[]{:S(2)}) async-start(), calls=%async_computation.4 | async-start | bytes 11059200 | tf_op jit(solution)/shard_map/reduce_scatter | solution.py:1647
  127.1 66.1 %copy-start.11 = (bf16[2560,640]{1,0:T(8,128)(2,1)S(1)}, bf16[2560,640]{1,0:T(8,128)(2,1)}, u32[]{:S(2)}) copy-start(bf16[2560,640]{1,0:T(8,128)(2,1)} %get-tuple-element.59) | copy-start | bytes 9830404
  322.9 5.5 copy-start.2
  328.4 1.9 copy-start.3
  346.1 325.7 %reduce-scatter.5.cloned.1.call-start = ((), (), s32[]{:S(2)}) async-start(), calls=%async_computation.5 | async-start | bytes 22118400 | tf_op jit(solution)/shard_map/reduce_scatter | solution.py:1653
  396.3 1.9 copy-start.5
  396.4 3.2 copy-start.6
  460.9 102.6 %copy-start.4 = (bf16[1024,1920]{1,0:T(8,128)(2,1)S(1)}, bf16[1024,1920]{1,0:T(8,128)(2,1)}, u32[]{:S(2)}) copy-start(bf16[1024,1920]{1,0:T(8,128)(2,1)} %copy-done.3) | copy-start | bytes 11796484
  578.7 72.4 %slice-start = ((s8[5242880]{0:T(1024)(128)(4,1)}), s8[4194304]{0:T(1024)(128)(4,1)S(1)}, s32[]{:S(2)}) async-start(s8[5242880]{0:T(1024)(128)(4,1)} %bitcast.49), calls=%async_computation.6 | async-start | bytes 8388608
  588.4 61.1 %copy-start.8 = (bf16[320,1920]{1,0:T(8,128)(2,1)S(1)}, bf16[320,1920]{1,0:T(8,128)(2,1)}, u32[]{:S(2)}) copy-start(bf16[320,1920]{1,0:T(8,128)(2,1)} %reduce-scatter.3.cloned.1.call-done) | copy-start | bytes 3686404
  588.4 62.7 %slice-start.1 = ((s8[5242880]{0:T(1024)(128)(4,1)}), s8[1048576]{0:T(1024)(128)(4,1)S(1)}, s32[]{:S(2)}) async-start(s8[5242880]{0:T(1024)(128)(4,1)} %bitcast.49), calls=%async_computation.7 | async-start | bytes 2097152
  651.1 20.7 %copy-start.12 = (bf16[1024,1280]{1,0:T(8,128)(2,1)S(1)}, bf16[1024,1280]{1,0:T(8,128)(2,1)}, u32[]{:S(2)}) copy-start(bf16[1024,1280]{1,0:T(8,128)(2,1)} %get-tuple-element.73) | copy-start | bytes 7864324
  694.0 113.7 %copy-start.7 = (bf16[320,3840]{1,0:T(8,128)(2,1)S(1)}, bf16[320,3840]{1,0:T(8,128)(2,1)}, u32[]{:S(2)}) copy-start(bf16[320,3840]{1,0:T(8,128)(2,1)} %reduce-scatter.5.cloned.1.call-done) | copy-start | bytes 7372804
  810.4 15.5 %copy-start.9 = (f32[320,640]{1,0:T(8,128)S(1)}, f32[320,640]{1,0:T(8,128)}, u32[]{:S(2)}) copy-start(f32[320,640]{1,0:T(8,128)} %get-tuple-element.120) | copy-start | bytes 2457604
  810.4 16.4 %copy-start.1 = (bf16[2,10,256,256]{3,2,1,0:T(8,128)(2,1)S(1)}, bf16[2,10,256,256]{3,2,1,0:T(8,128)(2,1)}, u32[]{:S(2)}) copy-start(bf16[2,10,256,256]{3,2,1,0:T(8,128)(2,1)} %param.21) | copy-start | bytes 7864324
Sparse Core Ops, SparseCore 0:
  103.8 173.9 all-gather.2
  279.5 92.1 all-gather.4
  374.0 101.6 reduce-scatter.2
  478.1 193.7 reduce-scatter.4
where the time goes:
time: 844 us; the launch traced here: 834 us
  Pallas kernels  538 us (64%)
  matrix products  195 us (23%)
  waiting for transfers between devices  39.4 us (5%)
  other arithmetic  24.7 us (3%)
  local copies, waits for them, and re-layouts  21.7 us (3%)
  between operations  14.4 us (2%)
    pallas_call x6, Pallas kernels, call_kernel(): pl.pallas_call(kernel, out_shape=outs, in_specs=[far if i in far_in else...  532 us
    dot_general x4, matrix products, rows_times(): lax.dot_general(left, right, (((1,), (1,)), ((), ())), preferred_element_...  61.1 us
    dot_general x4, matrix products, inner_rows(): lax.dot_general(left, right, (((0,), (0,)), ((), ())), preferred_element_...  60.8 us
    all_gather x1, waiting for transfers between devices, body(): wd_loc = lax.all_gather(w_down, 'dp', axis=0, tiled=True)  25.6 us
    dot_general x1, matrix products, body(): pre = jnp.dot(mid_rows, both_loc, preferred_element_type=F32)  25 us
    dot_general x1, matrix products, body(): d_hidden = jnp.dot(cot_rows, wd_loc, preferred_element_type=F32)  24.7 us
  transfers between devices with their start and end apart: 4, of which 2 were waited for; matrix products, arithmetic and copies ran while one was open for 23% of the time, Pallas kernels for 39%

commit v1 on v0

--- a/solution.py
+++ b/solution.py
@@ -506,15 +506,78 @@
     return total
 
 
+class Product:
+    def __init__(self, left, right, out, held, sems):
+        self.left, self.right, self.out = left, right, out
+        self.held, self.sems = held, sems
+        self.width = held.shape[1]
+        self.count = right.shape[0] // self.width
+        self.done = 0
+
+    def fetch(self, block):
+        return pltpu.make_async_copy(
+            self.right.at[pl.ds(block * self.width, self.width), :],
+            self.held.at[block % 2],
+            self.sems.at[block % 2],
+        )
+
+    def begin(self):
+        self.fetch(0).start()
+
+    def work(self, blocks):
+        for block in range(self.done, min(self.done + blocks, self.count)):
+            if block + 1 < self.count:
+                self.fetch(block + 1).start()
+            self.fetch(block).wait()
+
+            def rows(span, block=block):
+                found = times_transposed(self.left[span, :], self.held[block % 2])
+                at = slice(block * self.width, (block + 1) * self.width)
+                self.out[span, at] = found.astype(BF16)
+
+            parts(self.left.shape[0], rows)
+        self.done = min(self.done + blocks, self.count)
+
+
+PRODUCT_BLOCK = 256
+
+
+def product_scratch(depth):
+    return [pltpu.VMEM((2, PRODUCT_BLOCK, depth), BF16), pltpu.SemaphoreType.DMA((2,))]
+
+
 def turn_kernel(
-    nbits, d_norm, cot, middle, gain, d_middle, d_mixer, d_gain, landed, staged, s0, r0, s1, r1
+    nbits,
+    d_norm,
+    cot,
+    middle,
+    gain,
+    hidden,
+    w_down,
+    d_middle,
+    d_mixer,
+    d_gain,
+    ffn,
+    landed,
+    staged,
+    s0,
+    r0,
+    s1,
+    r1,
+    *product,
 ):
     rows = middle.shape[0]
+    ahead = Product(hidden, w_down, ffn, *product)
+    ahead.begin()
     greet(tensor_bits(nbits))
     scatter = Scatter(d_norm, landed, staged, rows, nbits, s0, r0)
     scatter.begin()
     d_gain[...] = jnp.zeros_like(d_gain)
-    scatter.run()
+    ahead.work(4)
+    for step in range(nbits):
+        scatter.advance(step)
+        if step + 1 < nbits:
+            ahead.work(2)
 
     def pull(row):
         span = pl.ds(row, CHUNK)
@@ -527,7 +590,10 @@
     chunks(rows, pull)
     gather = Gather(d_mixer, rows, nbits, s1, r1)
     gather.begin()
-    gather.finish()
+    ahead.work(2)
+    gather.advance(0)
+    ahead.work(ahead.count)
+    gather.finish(1)
     scatter.drain()
 
 
@@ -693,16 +759,15 @@
         return taken
 
     d_norm, tokens, d_middle, gain, own_small, d_gain_mid = take(6)
-    pieces = take(3)
-    grad_input, sum_out, sum_y, sum_x, gate_all, small_all = take(6)
+    pieces = take(2)
+    grad_input, sum_y, sum_x, gate_all, small_all = take(5)
     landed, staged, s0, r0 = take(4)
     share = small_all.shape[2]
-    rings = [LineSum(piece, *take(RING)) for piece in pieces[:2]]
+    gate = LineSum(pieces[0], *take(RING))
     if tiled:
-        for at in (0, share):
-            rings.append(LineSum(pieces[2], *take(RING), pl.ds(at, share)))
+        lines = [LineSum(pieces[1], *take(RING), pl.ds(at, share)) for at in (0, share)]
     else:
-        rings.append(LineSum(pieces[2], *take(RING)))
+        lines = [LineSum(pieces[1], *take(RING))]
     d_gain, gains, gains_landed, small, small_landed = take(5)
     gain_s, gain_r, vec_s, vec_r, join_s, join_r, gate_s, gate_r = take(8)
     rows = tokens.shape[0]
@@ -711,22 +776,20 @@
     peers = [chosen for chosen in subsets(tuple(range(nbits))) if chosen]
     others = [(shift, turn) for shift in range(chips) for turn in range(2)][1:]
     greet_peers(nbits, True, True)
-    for ring in rings:
-        ring.begin()
+    for line in [gate] + lines:
+        line.begin()
     scatter = Scatter(d_norm, landed, staged, rows, nbits, s0, r0)
     scatter.begin()
     d_gain[...] = jnp.zeros_like(d_gain)
     far = list(range(chips - 1, 0, -1))
-    for ring in rings:
-        ring.send(far[0])
-    if len(far) > 1:
-        rings[0].send(far[1])
+    for distance in far:
+        gate.send(distance)
+    for line in lines:
+        line.send(far[0])
     scatter.advance(0)
-    if len(far) > 1:
-        for ring in rings[1:]:
-            ring.send(far[1])
-    for distance in far[2:]:
-        rings[0].send(distance)
+    for distance in far[1:-1]:
+        for line in lines:
+            line.send(distance)
     for step in range(1, nbits):
         scatter.advance(step)
 
@@ -765,7 +828,7 @@
         return gate_copy(chips - 1 + len(peers), gate_all.at[:, :, core], target)
 
     def start_gate():
-        rings[0].finish(store_gate)
+        gate.finish(store_gate)
         for shift in range(1, chips):
             gate_line(shift).start()
 
@@ -792,9 +855,9 @@
     for number, chosen in enumerate(peers):
         gain_copy(number, chosen).start()
     start_gate()
-    for distance in far[2:]:
-        for ring in rings[1:]:
-            ring.send(distance)
+    if len(far) > 1:
+        for line in lines:
+            line.send(far[-1])
     total = own_small[...] + gains[me]
     for number, chosen in enumerate(peers):
         gain_copy(number, chosen).wait_recv()
@@ -848,12 +911,11 @@
 
         return store
 
-    rings[1].finish(store_in(sum_out))
     if tiled:
-        rings[2].finish(store_in(sum_y))
-        rings[3].finish(store_in(sum_x))
+        lines[0].finish(store_in(sum_y))
+        lines[1].finish(store_in(sum_x))
     else:
-        rings[2].finish(store_in(sum_y, sum_x))
+        lines[0].finish(store_in(sum_y, sum_x))
     gate_core().wait()
     for shift in range(1, chips):
         gate_line(shift).wait_send()
@@ -864,8 +926,8 @@
     for number, (shift, turn) in enumerate(others):
         vec_copy(number, shift, turn).wait_send()
     scatter.drain()
-    for ring in rings:
-        ring.drain()
+    for line in [gate] + lines:
+        line.drain()
 
 
 def in_vmem(count):
@@ -1351,7 +1413,24 @@
         scatter.drain()
 
 
-def finish_kernel(taps, gates, small, in_y, in_x, whole, out_y, out_x, conv, decay, gain_in, gain_mid):
+def finish_kernel(
+    taps,
+    gates,
+    small,
+    in_y,
+    in_x,
+    in_grad,
+    in_mixed,
+    whole,
+    out_y,
+    out_x,
+    out_grad,
+    out_mixed,
+    conv,
+    decay,
+    gain_in,
+    gain_mid,
+):
     blocks = whole.shape[1]
     pieces = gates.shape[0] // blocks
 
@@ -1366,16 +1445,25 @@
     lax.fori_loop(0, blocks, block, 0)
     out_y[...] = in_y[...]
     out_x[...] = in_x[...]
+
+    def copy(row):
+        span = pl.ds(row, CHUNK)
+        out_grad[span, :] = in_grad[span, :]
+        out_mixed[span, :] = in_mixed[span, :]
+
+    chunks(in_grad.shape[0], copy)
     share = small.shape[2]
     for index in range(small.shape[0]):
         span = slice(index * share, (index + 1) * share)
         conv[:, span] = small[index, :taps, :]
-        decay[:, span] = small[index, taps : taps + 1, :]
-        gain_in[:, span] = small[index, 6:7, :]
-        gain_mid[:, span] = small[index, 7:8, :]
-
-
-def finish(gate_all, small_all, sum_y, sum_x, taps, gate_shape):
+        for at in range(0, share, 128):
+            row = (index * share + at) // 128
+            decay[row : row + 1, :] = small[index, taps : taps + 1, at : at + 128]
+            gain_in[row : row + 1, :] = small[index, 6:7, at : at + 128]
+            gain_mid[row : row + 1, :] = small[index, 7:8, at : at + 128]
+
+
+def finish(gate_all, small_all, sum_y, sum_x, grad_input, mixed, taps, gate_shape):
     _, blocks, block, _ = gate_shape
     unit = gate_all.shape[-1]
     pieces = block // unit
@@ -1385,15 +1473,17 @@
         summed = small_all.transpose(1, 0, 2).reshape(8, width)
         whole = whole.reshape(gate_shape).astype(F32)
         rows = (summed[:taps], summed[taps], summed[6], summed[7])
-        return (whole, sum_y, sum_x) + rows
+        return (whole, sum_y, sum_x, grad_input, mixed) + rows
     shape = jax.ShapeDtypeStruct
-    row = shape((1, width), F32)
+    row = shape((width // 128, 128), F32)
     found = scan_call(
         partial(finish_kernel, taps),
         (
             shape(gate_shape, F32),
             shape(sum_y.shape, F32),
             shape(sum_x.shape, F32),
+            shape(grad_input.shape, F32),
+            shape(mixed.shape, BF16),
             shape((taps, width), F32),
             row,
             row,
@@ -1403,8 +1493,10 @@
         small_all,
         sum_y,
         sum_x,
+        grad_input,
+        mixed,
     )
-    return found[:4] + tuple(one.reshape(width) for one in found[4:])
+    return found[:6] + tuple(one.reshape(width) for one in found[6:])
 
 
 def scan_call(kernel, outs, *operands):
@@ -1653,24 +1745,27 @@
     sum_both = lax.psum_scatter(grad_both, "dp", scatter_dimension=0, tiled=True)
     d_pre, grad_both = lax.optimization_barrier((d_pre, grad_both))
     d_mid_part = rows_times(d_pre, both_loc).astype(BF16)
-    d_middle, d_mixer, d_gain_mid = call_kernel(
+    d_middle, d_mixer, d_gain_mid, ffn_part = call_kernel(
         partial(turn_kernel, nbits),
         (
             shape((own_rows, width), F32),
             shape((group_rows, width), BF16),
             shape((8, width), F32),
+            shape((group_rows, width), BF16),
         ),
-        scatter_scratch(own_rows, width, nbits) + gather_sems(nbits),
+        scatter_scratch(own_rows, width, nbits) + gather_sems(nbits) + product_scratch(units),
         2,
         d_mid_part,
         cotangent,
         middle,
         gain_mid,
+        hidden_low,
+        wd_loc,
+        far_in=(5,),
     )
     d_mixer, sum_wd = lax.optimization_barrier((d_mixer, sum_wd))
     d_mixed_in = jnp.dot(d_mixer, wout_loc, preferred_element_type=F32)
     unit = math.gcd(channels, block_size)
-    ffn_part = rows_times(hidden_low, wd_loc).astype(BF16)
     merged = half_blocks and nbits <= 2
     if half_blocks:
         found = call_kernel(
@@ -1705,7 +1800,6 @@
             *((ffn_part, middle) if merged else ()),
         )
         d_branches, gate_grad, own_small = found[:3]
-        d_branches, sum_both = lax.optimization_barrier((d_branches, sum_both))
         gate_grad = gate_grad.reshape(channels // unit * 2 * block_size, unit)
     else:
         d_conv, d_gate_low, d_branch_y, d_decay = scan_call(
@@ -1755,13 +1849,17 @@
     grad_wout = inner_rows(d_mixer, mixed_low).astype(BF16)
     grad_wyx = inner_rows(normed_rows, d_branches).astype(BF16)
     d_normed = rows_times(d_branches, wyx_loc).astype(BF16)
-
-    pieces = [halved(grad, ndp) for grad in (gate_grad, grad_wout, grad_wyx)]
+    d_normed, grad_wyx, grad_wout, sum_both = lax.optimization_barrier(
+        (d_normed, grad_wyx, grad_wout, sum_both)
+    )
+    sum_wout = lax.psum_scatter(grad_wout, "dp", scatter_dimension=0, tiled=True)
+
+    pieces = [halved(grad, ndp) for grad in (gate_grad, grad_wyx)]
     peers = ntensor - 1
     gate_rows = gate_grad.shape[0] // ndp
     dma = pltpu.SemaphoreType.DMA
     scratch = scatter_scratch(own_rows, width, nbits)
-    scratch += line_scratch(ndp, gate_rows, unit) + line_scratch(ndp, dp_rows, channels)
+    scratch += line_scratch(ndp, gate_rows, unit)
     if tiled:
         scratch += line_scratch(ndp, dp_rows, channels) * 2
     else:
@@ -1775,10 +1873,10 @@
     ]
     scratch += [dma((peers,)), dma((peers,)), dma((ndp - 1,)), dma((ndp - 1,))]
     scratch += [dma((peers,)), dma((peers,)), dma((peers + ndp,)), dma((peers + ndp,))]
-    grad_input, sum_wout, sum_wy, sum_wx, gate_all, small_all = call_kernel(
+    grad_input, sum_wy, sum_wx, gate_all, small_all = call_kernel(
         partial(leave_kernel, nbits, tiled),
         (shape((own_rows, width), F32),)
-        + (shape((dp_rows, channels), F32),) * 3
+        + (shape((dp_rows, channels), F32),) * 2
         + (
             shape((ntensor, ndp // 2, 2, gate_rows, unit), BF16),
             shape((ntensor, 8, channels), F32),
@@ -1792,7 +1890,7 @@
         own_small,
         d_gain_mid,
         *pieces,
-        far_in=(6, 7, 8),
+        far_in=(6, 7),
     )
     if merged:
         mixed = found[3]
@@ -1805,8 +1903,8 @@
             ffn_part,
             middle,
         )
-    sum_gate, sum_wy, sum_wx, sum_conv, sum_decay, sum_gain_in, sum_gain_mid = finish(
-        gate_all, small_all, sum_wy, sum_wx, taps, gate_w.shape
+    sum_gate, sum_wy, sum_wx, grad_input, mixed, sum_conv, sum_decay, sum_gain_in, sum_gain_mid = finish(
+        gate_all, small_all, sum_wy, sum_wx, grad_input, mixed, taps, gate_w.shape
     )
     return (
         mixed,
@@ -1817,7 +1915,7 @@
         sum_conv,
         sum_gate,
         sum_decay,
-        sum_wout,
+        sum_wout.astype(F32),
         sum_gain_mid,
         sum_both[:, :units].astype(F32),
         sum_both[:, units:].astype(F32),

time: 844 us -> 815 us (0.966)
  matrix products: 195 us -> 180 us
  waiting for transfers between devices: 39.4 us -> 30.6 us
    dot_general x4 -> x3, matrix products: 61.1 us -> 46.3 us  [rows_times(): lax.dot_general(left, right, (((1,), (1,)), ((), ())), preferred_element_...]
    reduce_scatter x1, waiting for transfers between devices: 13.1 us -> 4.19 us  [body(): lax.psum_scatter(grad_both, 'dp', scatter_dimension=0, tiled=True)]
  transfers between devices with their start and end apart: 4 -> 5, of which waited for: 2 -> 2; matrix products, arithmetic and copies ran while one was open for 23% -> 25% of each run, Pallas kernels for 39% -> 56%
where the time goes in v1:
time: 815 us; the launch traced here: 805 us
  Pallas kernels  542 us (67%)
  matrix products  180 us (22%)
  waiting for transfers between devices  30.6 us (4%)
  other arithmetic  22.7 us (3%)
  local copies, waits for them, and re-layouts  14.9 us (2%)
  between operations  14.3 us (2%)
    pallas_call x6, Pallas kernels, call_kernel(): pl.pallas_call(kernel, out_shape=outs, in_specs=[far if i in far_in else...  534 us
    dot_general x4, matrix products, inner_rows(): lax.dot_general(left, right, (((0,), (0,)), ((), ())), preferred_element_...  60.5 us
    dot_general x3, matrix products, rows_times(): lax.dot_general(left, right, (((1,), (1,)), ((), ())), preferred_element_...  46.3 us
    all_gather x1, waiting for transfers between devices, body(): wd_loc = lax.all_gather(w_down, 'dp', axis=0, tiled=True)  25.6 us
    dot_general x1, matrix products, body(): pre = jnp.dot(mid_rows, both_loc, preferred_element_type=F32)  25 us
    dot_general x1, matrix products, body(): d_hidden = jnp.dot(cot_rows, wd_loc, preferred_element_type=F32)  24.8 us
  transfers between devices with their start and end apart: 5, of which 2 were waited for; matrix products, arithmetic and copies ran while one was open for 25% of the time, Pallas kernels for 56%

profile of v1, /device:TPU:0, one launch (start us, length us, event | category | flops | bytes accessed | tf_op | source)
XLA Modules:
  0.0 804.9 jit_solution(11136385085351601243)
XLA Ops:
  8.7 3.3 pad_maximum_fusion.1
  12.0 91.7 %shard_map.237 = (bf16[1024,2560]{1,0:T(8,128)(2,1)}, s32[4,2,128]{2,1,0:T(2,128)}, bf16[2560,1280]{1,0:T(8,128)(2,1)}, bf16[2560,640]{1,0:T(8,128)(2,1)}) custom-call(bf16[256,2560]{1,0:T(8,128)(2,1)} %refs_1_.3, s32[2,128]{1,0:T(2,128)} %bitcast.47, f32[1,2560]{1,0:T(1,128)} %reshape.118.gain.refs_3_, bf16[320,640]{1,0:T(8,128)(2,1)} %refs_0_.1, ...), custom_call_target="tpu_custom_call" | custom-call | bytes 1000000 | tf_op jit(solution)/shard_map/pallas_call | solution.py:940
  113.1 14.0 %fusion.12.branches = f32[1024,1280]{1,0:T(8,128)} fusion(bf16[1024,2560]{1,0:T(8,128)(2,1)} %get-tuple-element.58, bf16[2560,1280]{1,0:T(8,128)(2,1)} %get-tuple-element.59), kind=kOutput, calls=%fused_computation.40 | convolution fusion | flops 6710886400 | bytes 17039360 | tf_op jit(solution)/shard_map/dot_general | solution.py:1675
  127.1 66.1 %shard_map.238 = (bf16[1024,640]{1,0:T(8,128)(2,1)}, f32[1024,640]{1,0:T(8,128)}, bf16[1024,768]{1,0:T(8,128)(2,1)}, f32[1024,1280]{1,0:T(8,128)}, bf16[1024,2560]{1,0:T(8,128)(2,1)}) custom-call(f32[1024,1280]{1,0:T(8,128)} %fusion.12.branches, f32[8,640]{1,0:T(8,128)} %concatenate.15.tap_rows, f32[1,640]{1,0:T(1,128)} %select_n.32.soft, ...), custom_call_target="tpu_custom_call" | custom-call | bytes 1000000 | tf_op jit(solution)/shard_map/pallas_call | solution.py:940
  193.2 7.4 convolution_convert_fusion.3.mixer
  200.6 97.2 %shard_map.239 = (f32[256,2560]{1,0:T(8,128)}, bf16[1024,2560]{1,0:T(8,128)(2,1)}) custom-call(bf16[1024,2560]{1,0:T(8,128)(2,1)} %convolution_convert_fusion.3.mixer, bf16[256,2560]{1,0:T(8,128)(2,1)} %refs_1_.3, f32[1,2560]{1,0:T(1,128)} %reshape.122.gain), custom_call_target="tpu_custom_call" | custom-call | bytes 1000000 | tf_op jit(solution)/shard_map/pallas_call | solution.py:940
  297.9 25.0 %fusion.13 = f32[1024,3840]{1,0:T(8,128)S(1)} fusion(bf16[1024,2560]{1,0:T(8,128)(2,1)} %get-tuple-element.64, bf16[2560,3840]{1,0:T(8,128)(2,1)} %all-gather.3.cloned.1.call-done), kind=kOutput, calls=%fused_computation.41 | convolution fusion | flops 20132659200 | bytes 40632320 | tf_op jit(solution)/shard_map/dot_general | solution.py:1735
  322.9 2.8 multiply_convert_fusion.1.hidden
  325.7 2.7 copy-done.3
  330.3 15.7 %convolution_convert_fusion.2 = bf16[2560,1920]{1,0:T(8,128)(2,1)} fusion(bf16[1024,2560]{1,0:T(8,128)(2,1)} %get-tuple-element.61, bf16[1024,1920]{1,0:T(8,128)(2,1)S(1)} %multiply_convert_fusion.1.hidden), kind=kOutput, calls=%fused_computation.2 | convolution fusion | flops 10071244800 | bytes 19005440 | tf_op jit(solution)/shard_map/dot_general | solution.py:1599
  346.1 25.6 %all-gather.5.cloned.1.call-done.w_down = bf16[2560,1920]{1,0:T(8,128)(2,1)} async-done(((bf16[320,1920]{1,0:T(8,128)(2,1)}), bf16[2560,1920]{1,0:T(8,128)(2,1)}) %all-gather.5.cloned.1.call-update) | async-done | bytes 9830416 | tf_op jit(solution)/shard_map/all_gather | solution.py:1664
  371.7 24.8 %fusion.6 = (bf16[1024,1920]{1,0:T(8,128)(2,1)S(1)}, bf16[1024,1920]{1,0:T(8,128)(2,1)S(1)}) fusion(f32[1024,3840]{1,0:T(8,128)} %copy-done.3, bf16[1024,2560]{1,0:T(8,128)(2,1)} %get-tuple-element.61, bf16[2560,1920]{1,0:T(8,128)(2,1)} %all-gather.5.cloned.1.call-done.w_down), kind=kOutput, calls=%fused_computation.11 | convolution fusion | flops 10113515520 | bytes 38666240 | tf_op jit(solution)/shard_map/dot_general | solution.py:1741
  399.7 26.7 %convolution_convert_fusion = bf16[2560,3840]{1,0:T(8,128)(2,1)} fusion(bf16[1024,2560]{1,0:T(8,128)(2,1)} %get-tuple-element.64, bf16[1024,1920]{1,0:T(8,128)(2,1)S(1)} %get-tuple-element.102, bf16[1024,1920]{1,0:T(8,128)(2,1)S(1)} %get-tuple-element.101), kind=kOutput, calls=%fused_computation | convolution fusion | flops 20158218240 | bytes 32768000 | tf_op jit(solution)/shard_map/dot_general | solution.py:1599
  427.1 7.0 pad_maximum_fusion
  434.1 27.1 %convolution_convert_fusion.5.d_norm = bf16[1024,2560]{1,0:T(8,128)(2,1)} fusion(bf16[1024,3840]{1,0:T(8,128)(2,1)} %pad_maximum_fusion, bf16[2560,3840]{1,0:T(8,128)(2,1)} %all-gather.3.cloned.1.call-done), kind=kOutput, calls=%fused_computation.18 | convolution fusion | flops 20135280640 | bytes 32768000 | tf_op jit(solution)/shard_map/dot_general | solution.py:1590
  461.1 105.3 %shard_map.240 = (f32[256,2560]{1,0:T(8,128)}, bf16[1024,2560]{1,0:T(8,128)(2,1)}, f32[8,2560]{1,0:T(8,128)}, bf16[1024,2560]{1,0:T(8,128)(2,1)}) custom-call(bf16[1024,2560]{1,0:T(8,128)(2,1)} %convolution_convert_fusion.5.d_norm, bf16[256,2560]{1,0:T(8,128)(2,1)} %cot.3, f32[256,2560]{1,0:T(8,128)} %get-tuple-element.69.middle.refs_1_, ...), custom_call_target="tpu_custom_call" | custom-call | bytes 1000000 | tf_op jit(solution)/shard_map/pallas_call | solution.py:940
  566.5 9.4 %fusion.14.d_mixed = f32[1024,640]{1,0:T(8,128)} fusion(bf16[1024,2560]{1,0:T(8,128)(2,1)} %get-tuple-element.71, bf16[2560,640]{1,0:T(8,128)(2,1)} %get-tuple-element.63), kind=kOutput, calls=%fused_computation.42 | convolution fusion | flops 3355443200 | bytes 11141120 | tf_op jit(solution)/shard_map/dot_general | solution.py:1767
  575.9 61.6 %shard_map.241 = (bf16[1024,1280]{1,0:T(8,128)(2,1)}, bf16[10,256,128]{2,1,0:T(8,128)(2,1)}, f32[8,640]{1,0:T(8,128)}, bf16[256,2560]{1,0:T(8,128)(2,1)}) custom-call(f32[1024,640]{1,0:T(8,128)} %fusion.14.d_mixed, bf16[1024,768]{1,0:T(8,128)(2,1)} %get-tuple-element.72.window, f32[1024,1280]{1,0:T(8,128)} %get-tuple-element.73.gates, ...), custom_call_target="tpu_custom_call" | custom-call | bytes 1000000 | tf_op jit(solution)/shard_map/pallas_call | solution.py:940
  637.5 7.3 convolution_convert_fusion.6
  644.8 11.9 %convolution_convert_fusion.4.refs_0_ = bf16[1024,2560]{1,0:T(8,128)(2,1)} fusion(bf16[1024,1280]{1,0:T(8,128)(2,1)S(1)} %copy-done.10, bf16[2560,1280]{1,0:T(8,128)(2,1)} %get-tuple-element.59), kind=kOutput, calls=%fused_computation.17 | convolution fusion | flops 6713507840 | bytes 14417920 | tf_op jit(solution)/shard_map/dot_general | solution.py:1590
  656.7 10.9 %convolution_convert_fusion.1 = bf16[2560,1280]{1,0:T(8,128)(2,1)} fusion(bf16[1024,2560]{1,0:T(8,128)(2,1)} %get-tuple-element.58, bf16[1024,1280]{1,0:T(8,128)(2,1)S(1)} %copy-done.11), kind=kOutput, calls=%fused_computation.1 | convolution fusion | flops 6714163200 | bytes 14417920 | tf_op jit(solution)/shard_map/dot_general | solution.py:1599
  667.6 4.2 reduce-scatter.6.cloned.1.call-done
  673.4 111.6 %shard_map.242 = (f32[256,2560]{1,0:T(8,128)}, f32[320,640]{1,0:T(8,128)}, f32[320,640]{1,0:T(8,128)}, bf16[4,4,2,320,128]{4,3,2,1,0:T(8,128)(2,1)}, f32[4,8,640]{2,1,0:T(8,128)}) custom-call(bf16[1024,2560]{1,0:T(8,128)(2,1)} %convolution_convert_fusion.4.refs_0_, bf16[256,2560]{1,0:T(8,128)(2,1)} %refs_1_.3, f32[256,2560]{1,0:T(8,128)} %get-tuple-element.78.refs_2_, ...), custom_call_target="tpu_custom_call" | custom-call | bytes 1000000 | tf_op jit(solution)/shard_map/pallas_call | solution.py:940
  785.1 8.5 %shard_map.243 = (f32[2,10,256,256]{3,2,1,0:T(8,128)}, f32[320,640]{1,0:T(8,128)}, f32[320,640]{1,0:T(8,128)}, f32[256,2560]{1,0:T(8,128)}, bf16[256,2560]{1,0:T...) custom-call(bf16[20,2,256,128]{3,2,1,0:T(8,128)(2,1)} %bitcast.41, ...), custom_call_target="tpu_custom_call" | custom-call | tf_op jit(solution)/shard_map/pallas_call | solution.py:1503
  (61 shorter events, 22.9 us)
Async XLA Ops:
  7.2 104.1 %copy-start = (bf16[2,10,256,256]{3,2,1,0:T(8,128)(2,1)S(1)}, bf16[2,10,256,256]{3,2,1,0:T(8,128)(2,1)}, u32[]{:S(2)}) copy-start(bf16[2,10,256,256]{3,2,1,0:T(8,128)(2,1)} %param.21) | copy-start | bytes 7864324
  7.2 290.7 %all-gather.3.cloned.1.call-start = ((), (), s32[]{:S(2)}) async-start(), calls=%async_computation.3 | async-start | bytes 22118400 | tf_op jit(solution)/shard_map/all_gather | solution.py:1663
  8.7 97.2 %copy-start.8 = (f32[2560]{0:T(1024)S(1)}, f32[2560]{0:T(1024)}, u32[]{:S(2)}) copy-start(f32[2560]{0:T(1024)} %param.24) | copy-start | bytes 30724
  103.7 268.0 %all-gather.5.cloned.1.call-start = ((), (), s32[]{:S(2)}) async-start(), calls=%async_computation.4 | async-start | bytes 11059200 | tf_op jit(solution)/shard_map/all_gather | solution.py:1664
  104.4 462.0 %reduce-scatter.4.cloned.1.call-start = ((), (), s32[]{:S(2)}) async-start(), calls=%async_computation.5 | async-start | bytes 11059200 | tf_op jit(solution)/shard_map/reduce_scatter | solution.py:1739
  127.1 66.1 %copy-start.9 = (bf16[2560,640]{1,0:T(8,128)(2,1)S(1)}, bf16[2560,640]{1,0:T(8,128)(2,1)}, u32[]{:S(2)}) copy-start(bf16[2560,640]{1,0:T(8,128)(2,1)} %get-tuple-element.63) | copy-start | bytes 9830404
  322.9 5.5 copy-start.3
  328.4 1.9 copy-start.2
  346.0 325.8 %reduce-scatter.6.cloned.1.call-start = ((), (), s32[]{:S(2)}) async-start(), calls=%async_computation.6 | async-start | bytes 22118400 | tf_op jit(solution)/shard_map/reduce_scatter | solution.py:1745
  396.5 1.9 copy-start.4
  396.5 3.2 copy-start.5
  426.4 369.8 %reduce-scatter.8.cloned.1.call-start = ((), (), s32[]{:S(2)}) async-start(), calls=%async_computation.7 | async-start | bytes 3686400 | tf_op jit(solution)/shard_map/reduce_scatter | solution.py:1855
  566.4 71.1 %slice-start = ((s8[5242880]{0:T(1024)(128)(4,1)}), s8[4194304]{0:T(1024)(128)(4,1)S(1)}, s32[]{:S(2)}) async-start(s8[5242880]{0:T(1024)(128)(4,1)} %bitcast.48), calls=%async_computation.8 | async-start | bytes 8388608
  575.9 61.6 %slice-start.1 = ((s8[5242880]{0:T(1024)(128)(4,1)}), s8[1048576]{0:T(1024)(128)(4,1)S(1)}, s32[]{:S(2)}) async-start(s8[5242880]{0:T(1024)(128)(4,1)} %bitcast.48), calls=%async_computation.9 | async-start | bytes 2097152
  637.5 7.3 copy-start.10
  644.8 11.9 %copy-start.11 = (bf16[1024,1280]{1,0:T(8,128)(2,1)S(1)}, bf16[1024,1280]{1,0:T(8,128)(2,1)}, u32[]{:S(2)}) copy-start(bf16[1024,1280]{1,0:T(8,128)(2,1)} %get-tuple-element.76) | copy-start | bytes 7864324
  656.7 15.1 %copy-start.7 = (bf16[320,1920]{1,0:T(8,128)(2,1)S(1)}, bf16[320,1920]{1,0:T(8,128)(2,1)}, u32[]{:S(2)}) copy-start(bf16[320,1920]{1,0:T(8,128)(2,1)} %reduce-scatter.4.cloned.1.call-done) | copy-start | bytes 3686404
  785.1 8.5 %copy-start.6 = (bf16[320,3840]{1,0:T(8,128)(2,1)S(1)}, bf16[320,3840]{1,0:T(8,128)(2,1)}, u32[]{:S(2)}) copy-start(bf16[320,3840]{1,0:T(8,128)(2,1)} %reduce-scatter.6.cloned.1.call-done) | copy-start | bytes 7372804
  785.1 13.1 %copy-start.1 = (bf16[2,10,256,256]{3,2,1,0:T(8,128)(2,1)S(1)}, bf16[2,10,256,256]{3,2,1,0:T(8,128)(2,1)}, u32[]{:S(2)}) copy-start(bf16[2,10,256,256]{3,2,1,0:T(8,128)(2,1)} %param.21) | copy-start | bytes 7864324
Sparse Core Ops, SparseCore 0:
  103.8 173.9 all-gather.2
  279.5 92.1 all-gather.4
  374.0 101.6 reduce-scatter.3
  478.1 193.7 reduce-scatter.5
  674.0 68.4 reduce-scatter.7

commit v2 on v1

--- a/solution.py
+++ b/solution.py
@@ -1262,19 +1262,24 @@
         return taken
 
     ffn, middle = take(2) if with_ffn else (None, None)
-    d_branches, gate_grad, own_small = take(3)
+    grad_out = take(1)[0]
+    d_branches, gate_grad, own_small, sum_out = take(4)
     mixed = take(1)[0] if with_ffn else None
     d_conv, d_gates, given, taken, sums, send, recv = take(7)
+    flow = LineSum(grad_out, *take(RING))
+    far = list(range(flow.chips - 1, 0, -1))
     total_rows, width = states.shape
     block = weights.shape[2]
     place = HalfBlocks(width, block)
     half = place.half
     branch_y, branch_x = branches.at[:, :width], branches.at[:, width:]
     d_branch_y, d_branch_x = d_branches.at[:, :width], d_branches.at[:, width:]
-    greet(tensor_bits(nbits))
+    greet_peers(nbits, False, False)
+    flow.begin()
     if with_ffn:
         scatter = Scatter(ffn, *take(2), middle.shape[0], nbits, *take(2))
         scatter.begin()
+    flow.send(far[0])
     backward_scan(
         d_mixed,
         lambda span: window[span, pl.ds(place.own, width)],
@@ -1314,6 +1319,8 @@
         device_id_type=MESH,
     )
     rim.start()
+    for distance in far[1:-1]:
+        flow.send(distance)
 
     def full(span):
         for index in range(place.count - 1):
@@ -1354,6 +1361,8 @@
         gate_grad[2 * index] = found[:, :half]
         gate_grad[2 * index + 1] = found[:, half:]
     rim.wait()
+    if len(far) > 1:
+        flow.send(far[-1])
 
     def add(span):
         d_conv[span, pl.ds(place.mine, half)] += taken[span, :].astype(F32)
@@ -1412,91 +1421,130 @@
         chunks(middle.shape[0], result)
         scatter.drain()
 
+    def store(span, value):
+        sum_out[span, :] = value
+
+    flow.finish(store)
+    flow.drain()
+
 
 def finish_kernel(
     taps,
     gates,
     small,
+    in_out,
     in_y,
     in_x,
     in_grad,
     in_mixed,
+    in_both,
+    in_down,
     whole,
+    out_out,
     out_y,
     out_x,
     out_grad,
     out_mixed,
+    out_gate,
+    out_up,
+    out_down,
     conv,
     decay,
     gain_in,
     gain_mid,
 ):
-    blocks = whole.shape[1]
-    pieces = gates.shape[0] // blocks
-
-    def block(n, carry):
-        for piece in range(pieces):
-            for s in range(2):
-                whole[s, n, :, piece * 128 : (piece + 1) * 128] = gates[
-                    n * pieces + piece, s
-                ].astype(F32)
-        return carry
-
-    lax.fori_loop(0, blocks, block, 0)
+    for piece in range(gates.shape[0]):
+        for s in range(2):
+            whole[s, 0, :, piece * 128 : (piece + 1) * 128] = gates[piece, s].astype(F32)
+    out_out[...] = in_out[...]
     out_y[...] = in_y[...]
     out_x[...] = in_x[...]
-
-    def copy(row):
-        span = pl.ds(row, CHUNK)
-        out_grad[span, :] = in_grad[span, :]
-        out_mixed[span, :] = in_mixed[span, :]
-
-    chunks(in_grad.shape[0], copy)
-    share = small.shape[2]
-    for index in range(small.shape[0]):
-        span = slice(index * share, (index + 1) * share)
-        conv[:, span] = small[index, :taps, :]
-        for at in range(0, share, 128):
-            row = (index * share + at) // 128
-            decay[row : row + 1, :] = small[index, taps : taps + 1, at : at + 128]
-            gain_in[row : row + 1, :] = small[index, 6:7, at : at + 128]
-            gain_mid[row : row + 1, :] = small[index, 7:8, at : at + 128]
-
-
-def finish(gate_all, small_all, sum_y, sum_x, grad_input, mixed, taps, gate_shape):
+    out_grad[...] = in_grad[...]
+    out_mixed[...] = in_mixed[...]
+    units = out_gate.shape[1]
+    out_gate[...] = in_both[:, :units].astype(F32)
+    out_up[...] = in_both[:, units:].astype(F32)
+    out_down[...] = in_down[...].astype(F32)
+
+    @pl.when(pl.program_id(0) == 0)
+    def _():
+        share = small.shape[2]
+        for index in range(small.shape[0]):
+            span = slice(index * share, (index + 1) * share)
+            conv[:, span] = small[index, :taps, :]
+            for at in range(0, share, 128):
+                row = (index * share + at) // 128
+                decay[row : row + 1, :] = small[index, taps : taps + 1, at : at + 128]
+                gain_in[row : row + 1, :] = small[index, 6:7, at : at + 128]
+                gain_mid[row : row + 1, :] = small[index, 7:8, at : at + 128]
+
+
+def finish(gate_all, small_all, sums, grad_input, mixed, both, down, taps, gate_shape):
     _, blocks, block, _ = gate_shape
     unit = gate_all.shape[-1]
     pieces = block // unit
     width = small_all.shape[0] * small_all.shape[2]
-    if unit != 128:
+    rows, units = down.shape
+    own_rows = grad_input.shape[0]
+    steps, held = rows // blocks, own_rows // 8
+    if unit != 128 or rows % (16 * blocks) or own_rows % 128:
         whole = gate_all.reshape(blocks, pieces, 2, block, unit).transpose(2, 0, 3, 1, 4)
         summed = small_all.transpose(1, 0, 2).reshape(8, width)
         whole = whole.reshape(gate_shape).astype(F32)
-        rows = (summed[:taps], summed[taps], summed[6], summed[7])
-        return (whole, sum_y, sum_x, grad_input, mixed) + rows
+        wide = tuple(one.astype(F32) for one in (both[:, :units], both[:, units:], down))
+        last = (summed[:taps], summed[taps], summed[6], summed[7])
+        return (whole, *sums, grad_input, mixed, *wide, *last)
     shape = jax.ShapeDtypeStruct
-    row = shape((width // 128, 128), F32)
-    found = scan_call(
+
+    def by_rows(count, columns):
+        return pl.BlockSpec((count, columns), lambda n: (n, 0))
+
+    def by_held(columns):
+        return pl.BlockSpec((held, columns), lambda n: (jnp.minimum(n, 7), 0))
+
+    def whole_array(*dims):
+        return pl.BlockSpec(dims, lambda n: (0,) * len(dims))
+
+    columns = sums[0].shape[1]
+    d_width = grad_input.shape[1]
+    lines = width // 128
+    found = pl.pallas_call(
         partial(finish_kernel, taps),
-        (
-            shape(gate_shape, F32),
-            shape(sum_y.shape, F32),
-            shape(sum_x.shape, F32),
-            shape(grad_input.shape, F32),
-            shape(mixed.shape, BF16),
-            shape((taps, width), F32),
-            row,
-            row,
-            row,
+        grid=(blocks,),
+        in_specs=[
+            pl.BlockSpec((pieces, 2, block, unit), lambda n: (n, 0, 0, 0)),
+            whole_array(*small_all.shape),
+        ]
+        + [by_rows(steps, columns)] * 3
+        + [by_held(d_width)] * 2
+        + [by_rows(steps, 2 * units), by_rows(steps, units)],
+        out_specs=(
+            (pl.BlockSpec((2, 1, block, block), lambda n: (0, n, 0, 0)),)
+            + (by_rows(steps, columns),) * 3
+            + (by_held(d_width),) * 2
+            + (by_rows(steps, units),) * 3
+            + (whole_array(taps, width),)
+            + (whole_array(lines, 128),) * 3
         ),
+        out_shape=(
+            (shape(gate_shape, F32),)
+            + (shape((rows, columns), F32),) * 3
+            + (shape(grad_input.shape, F32), shape(mixed.shape, BF16))
+            + (shape((rows, units), F32),) * 3
+            + (shape((taps, width), F32),)
+            + (shape((lines, 128), F32),) * 3
+        ),
+        compiler_params=pltpu.CompilerParams(vmem_limit_bytes=VMEM_BYTES),
+    )(
         gate_all.reshape(blocks * pieces, 2, block, unit),
         small_all,
-        sum_y,
-        sum_x,
+        *sums,
         grad_input,
         mixed,
+        both,
+        down,
     )
-    return found[:6] + tuple(one.reshape(width) for one in found[6:])
+    return found[:10] + tuple(one.reshape(width) for one in found[10:])
 
 
 def scan_call(kernel, outs, *operands):
@@ -1764,6 +1812,7 @@
         far_in=(5,),
     )
     d_mixer, sum_wd = lax.optimization_barrier((d_mixer, sum_wd))
+    grad_wout = inner_rows(d_mixer, mixed_low).astype(BF16)
     d_mixed_in = jnp.dot(d_mixer, wout_loc, preferred_element_type=F32)
     unit = math.gcd(channels, block_size)
     merged = half_blocks and nbits <= 2
@@ -1774,6 +1823,7 @@
                 shape((group_rows, 2 * channels), BF16),
                 shape((channels // unit * 2, block_size, unit), BF16),
                 shape((8, channels), F32),
+                shape((dp_rows, channels), F32),
             )
             + ((shape((own_rows, width), BF16),) if merged else ()),
             [
@@ -1785,6 +1835,7 @@
                 pltpu.SemaphoreType.DMA((1,)),
                 pltpu.SemaphoreType.DMA((1,)),
             ]
+            + line_scratch(ndp, dp_rows, channels)
             + (scatter_scratch(own_rows, width, nbits) if merged else []),
             6,
             d_mixed_in,
@@ -1798,8 +1849,10 @@
             since,
             w_window,
             *((ffn_part, middle) if merged else ()),
-        )
-        d_branches, gate_grad, own_small = found[:3]
+            halved(grad_wout, ndp),
+            far_in=(12 if merged else 10,),
+        )
+        d_branches, gate_grad, own_small, sum_wout = found[:4]
         gate_grad = gate_grad.reshape(channels // unit * 2 * block_size, unit)
     else:
         d_conv, d_gate_low, d_branch_y, d_decay = scan_call(
@@ -1846,13 +1899,12 @@
             axis=0,
         )
 
-    grad_wout = inner_rows(d_mixer, mixed_low).astype(BF16)
     grad_wyx = inner_rows(normed_rows, d_branches).astype(BF16)
     d_normed = rows_times(d_branches, wyx_loc).astype(BF16)
-    d_normed, grad_wyx, grad_wout, sum_both = lax.optimization_barrier(
-        (d_normed, grad_wyx, grad_wout, sum_both)
-    )
-    sum_wout = lax.psum_scatter(grad_wout, "dp", scatter_dimension=0, tiled=True)
+    d_normed, grad_wyx, sum_both = lax.optimization_barrier((d_normed, grad_wyx, sum_both))
+    if not half_blocks:
+        sum_wout = lax.psum_scatter(grad_wout, "dp", scatter_dimension=0, tiled=True)
+        sum_wout = sum_wout.astype(F32)
 
     pieces = [halved(grad, ndp) for grad in (gate_grad, grad_wyx)]
     peers = ntensor - 1
@@ -1893,7 +1945,7 @@
         far_in=(6, 7),
     )
     if merged:
-        mixed = found[3]
+        mixed = found[4]
     else:
         (mixed,) = call_kernel(
             partial(result_kernel, nbits),
@@ -1903,9 +1955,19 @@
             ffn_part,
             middle,
         )
-    sum_gate, sum_wy, sum_wx, grad_input, mixed, sum_conv, sum_decay, sum_gain_in, sum_gain_mid = finish(
-        gate_all, small_all, sum_wy, sum_wx, grad_input, mixed, taps, gate_w.shape
+    found = finish(
+        gate_all,
+        small_all,
+        (sum_wout, sum_wy, sum_wx),
+        grad_input,
+        mixed,
+        sum_both,
+        sum_wd,
+        taps,
+        gate_w.shape,
     )
+    sum_gate, sum_wout, sum_wy, sum_wx, grad_input, mixed = found[:6]
+    sum_wg, sum_wu, sum_wd, sum_conv, sum_decay, sum_gain_in, sum_gain_mid = found[6:]
     return (
         mixed,
         grad_input,
@@ -1915,11 +1977,11 @@
         sum_conv,
         sum_gate,
         sum_decay,
-        sum_wout.astype(F32),
+        sum_wout,
         sum_gain_mid,
-        sum_both[:, :units].astype(F32),
-        sum_both[:, units:].astype(F32),
-        sum_wd.astype(F32),
+        sum_wg,
+        sum_wu,
+        sum_wd,
     )
 
 

time: 815 us -> 822 us (level)
  waiting for transfers between devices: 30.6 us -> 39.7 us
    dot_general x3, matrix products: 46.3 us -> 56.6 us  [rows_times(): lax.dot_general(left, right, (((1,), (1,)), ((), ())), preferred_element_...]
    reduce_scatter x1, waiting for transfers between devices: 4.19 us -> 13.3 us  [body(): lax.psum_scatter(grad_both, 'dp', scatter_dimension=0, tiled=True)]
  transfers between devices with their start and end apart: 5 -> 4, of which waited for: 2 -> 2; matrix products, arithmetic and copies ran while one was open for 25% -> 25% of each run, Pallas kernels for 56% -> 42%
where the time goes in v2:
time: 822 us; the launch traced here: 811 us
  Pallas kernels  539 us (66%)
  matrix products  186 us (23%)
  waiting for transfers between devices  39.7 us (5%)
  other arithmetic  16.5 us (2%)
  local copies, waits for them, and re-layouts  14.9 us (2%)
  between operations  14.4 us (2%)
    pallas_call x6, Pallas kernels, call_kernel(): pl.pallas_call(kernel, out_shape=outs, in_specs=[far if i in far_in else...  525 us
    dot_general x4, matrix products, inner_rows(): lax.dot_general(left, right, (((0,), (0,)), ((), ())), preferred_element_...  60.1 us
    dot_general x3, matrix products, rows_times(): lax.dot_general(left, right, (((1,), (1,)), ((), ())), preferred_element_...  56.6 us
    all_gather x1, waiting for transfers between devices, body(): wd_loc = lax.all_gather(w_down, 'dp', axis=0, tiled=True)  25.7 us
    dot_general x1, matrix products, body(): pre = jnp.dot(mid_rows, both_loc, preferred_element_type=F32)  25 us
    dot_general x1, matrix products, body(): d_hidden = jnp.dot(cot_rows, wd_loc, preferred_element_type=F32)  24.7 us
  transfers between devices with their start and end apart: 4, of which 2 were waited for; matrix products, arithmetic and copies ran while one was open for 25% of the time, Pallas kernels for 42%

profile of v2, /device:TPU:0, one launch (start us, length us, event | category | flops | bytes accessed | tf_op | source)
XLA Modules:
  0.0 811.4 jit_solution(7304815789298946237)
XLA Ops:
  8.7 3.3 pad_maximum_fusion.1
  12.0 91.7 %shard_map.237 = (bf16[1024,2560]{1,0:T(8,128)(2,1)}, s32[4,2,128]{2,1,0:T(2,128)}, bf16[2560,1280]{1,0:T(8,128)(2,1)}, bf16[2560,640]{1,0:T(8,128)(2,1)}) custom-call(bf16[256,2560]{1,0:T(8,128)(2,1)} %refs_1_.3, s32[2,128]{1,0:T(2,128)} %bitcast.49, f32[1,2560]{1,0:T(1,128)} %reshape.121.gain.refs_3_, bf16[320,640]{1,0:T(8,128)(2,1)} %refs_0_.1, ...), custom_call_target="tpu_custom_call" | custom-call | bytes 1000000 | tf_op jit(solution)/shard_map/pallas_call | solution.py:940
  113.1 14.0 %fusion.12.branches = f32[1024,1280]{1,0:T(8,128)} fusion(bf16[1024,2560]{1,0:T(8,128)(2,1)} %get-tuple-element.62, bf16[2560,1280]{1,0:T(8,128)(2,1)} %get-tuple-element.63), kind=kOutput, calls=%fused_computation.38 | convolution fusion | flops 6710886400 | bytes 17039360 | tf_op jit(solution)/shard_map/dot_general | solution.py:1723
  127.1 66.1 %shard_map.238 = (bf16[1024,640]{1,0:T(8,128)(2,1)}, f32[1024,640]{1,0:T(8,128)}, bf16[1024,768]{1,0:T(8,128)(2,1)}, f32[1024,1280]{1,0:T(8,128)}, bf16[1024,2560]{1,0:T(8,128)(2,1)}) custom-call(f32[1024,1280]{1,0:T(8,128)} %fusion.12.branches, f32[8,640]{1,0:T(8,128)} %concatenate.15.tap_rows, f32[1,640]{1,0:T(1,128)} %select_n.32.soft, ...), custom_call_target="tpu_custom_call" | custom-call | bytes 1000000 | tf_op jit(solution)/shard_map/pallas_call | solution.py:940
  193.2 7.3 convolution_convert_fusion.3.mixer
  200.5 97.2 %shard_map.239 = (f32[256,2560]{1,0:T(8,128)}, bf16[1024,2560]{1,0:T(8,128)(2,1)}) custom-call(bf16[1024,2560]{1,0:T(8,128)(2,1)} %convolution_convert_fusion.3.mixer, bf16[256,2560]{1,0:T(8,128)(2,1)} %refs_1_.3, f32[1,2560]{1,0:T(1,128)} %reshape.125.gain), custom_call_target="tpu_custom_call" | custom-call | bytes 1000000 | tf_op jit(solution)/shard_map/pallas_call | solution.py:940
  297.7 25.0 %fusion.13 = f32[1024,3840]{1,0:T(8,128)S(1)} fusion(bf16[1024,2560]{1,0:T(8,128)(2,1)} %get-tuple-element.68, bf16[2560,3840]{1,0:T(8,128)(2,1)} %all-gather.3.cloned.1.call-done), kind=kOutput, calls=%fused_computation.39 | convolution fusion | flops 20132659200 | bytes 40632320 | tf_op jit(solution)/shard_map/dot_general | solution.py:1783
  322.8 2.8 multiply_convert_fusion.1.hidden
  325.6 2.7 copy-done.3
  330.2 15.7 %convolution_convert_fusion.2 = bf16[2560,1920]{1,0:T(8,128)(2,1)} fusion(bf16[1024,2560]{1,0:T(8,128)(2,1)} %get-tuple-element.65, bf16[1024,1920]{1,0:T(8,128)(2,1)S(1)} %multiply_convert_fusion.1.hidden), kind=kOutput, calls=%fused_computation.2 | convolution fusion | flops 10071244800 | bytes 19005440 | tf_op jit(solution)/shard_map/dot_general | solution.py:1647
  346.0 25.7 %all-gather.5.cloned.1.call-done.w_down = bf16[2560,1920]{1,0:T(8,128)(2,1)} async-done(((bf16[320,1920]{1,0:T(8,128)(2,1)}), bf16[2560,1920]{1,0:T(8,128)(2,1)}) %all-gather.5.cloned.1.call-update) | async-done | bytes 9830416 | tf_op jit(solution)/shard_map/all_gather | solution.py:1712
  371.7 24.7 %fusion.6 = (bf16[1024,1920]{1,0:T(8,128)(2,1)S(1)}, bf16[1024,1920]{1,0:T(8,128)(2,1)S(1)}) fusion(f32[1024,3840]{1,0:T(8,128)} %copy-done.3, bf16[1024,2560]{1,0:T(8,128)(2,1)} %get-tuple-element.65, bf16[2560,1920]{1,0:T(8,128)(2,1)} %all-gather.5.cloned.1.call-done.w_down), kind=kOutput, calls=%fused_computation.11 | convolution fusion | flops 10113515520 | bytes 38666240 | tf_op jit(solution)/shard_map/dot_general | solution.py:1789
  399.7 26.7 %convolution_convert_fusion = bf16[2560,3840]{1,0:T(8,128)(2,1)} fusion(bf16[1024,2560]{1,0:T(8,128)(2,1)} %get-tuple-element.68, bf16[1024,1920]{1,0:T(8,128)(2,1)S(1)} %get-tuple-element.110, bf16[1024,1920]{1,0:T(8,128)(2,1)S(1)} %get-tuple-element.109), kind=kOutput, calls=%fused_computation | convolution fusion | flops 20158218240 | bytes 32768000 | tf_op jit(solution)/shard_map/dot_general | solution.py:1647
  426.9 7.0 pad_maximum_fusion
  433.9 36.9 %convolution_convert_fusion.5.d_norm = bf16[1024,2560]{1,0:T(8,128)(2,1)} fusion(bf16[1024,3840]{1,0:T(8,128)(2,1)} %pad_maximum_fusion, bf16[2560,3840]{1,0:T(8,128)(2,1)} %all-gather.3.cloned.1.call-done), kind=kOutput, calls=%fused_computation.18 | convolution fusion | flops 20135280640 | bytes 32768000 | tf_op jit(solution)/shard_map/dot_general | solution.py:1638
  470.8 105.2 %shard_map.240 = (f32[256,2560]{1,0:T(8,128)}, bf16[1024,2560]{1,0:T(8,128)(2,1)}, f32[8,2560]{1,0:T(8,128)}, bf16[1024,2560]{1,0:T(8,128)(2,1)}) custom-call(bf16[1024,2560]{1,0:T(8,128)(2,1)} %convolution_convert_fusion.5.d_norm, bf16[256,2560]{1,0:T(8,128)(2,1)} %cot.3, f32[256,2560]{1,0:T(8,128)} %get-tuple-element.73.middle.refs_1_, ...), custom_call_target="tpu_custom_call" | custom-call | bytes 1000000 | tf_op jit(solution)/shard_map/pallas_call | solution.py:940
  576.1 8.7 %convolution_convert_fusion.6 = bf16[2560,640]{1,0:T(8,128)(2,1)} fusion(bf16[1024,2560]{1,0:T(8,128)(2,1)} %get-tuple-element.75, bf16[1024,640]{1,0:T(8,128)(2,1)S(1)} %copy-done.11), kind=kOutput, calls=%fused_computation.19 | convolution fusion | flops 3357081600 | bytes 9830400 | tf_op jit(solution)/shard_map/dot_general | solution.py:1647
  584.8 5.7 fusion.14.d_mixed
  590.5 72.9 %shard_map.241 = (bf16[1024,1280]{1,0:T(8,128)(2,1)}, bf16[10,256,128]{2,1,0:T(8,128)(2,1)}, f32[8,640]{1,0:T(8,128)}, f32[320,640]{1,0:T(8,128)}, bf16[256,2560]{1,0:T(8,128)(2,1)}) custom-call(f32[1024,640]{1,0:T(8,128)} %fusion.14.d_mixed, bf16[1024,768]{1,0:T(8,128)(2,1)} %get-tuple-element.76.window, f32[1024,1280]{1,0:T(8,128)} %get-tuple-element.77.gates, ...), custom_call_target="tpu_custom_call" | custom-call | bytes 1000000 | tf_op jit(solution)/shard_map/pallas_call | solution.py:940
  663.4 12.4 %convolution_convert_fusion.4.refs_0_ = bf16[1024,2560]{1,0:T(8,128)(2,1)} fusion(bf16[1024,1280]{1,0:T(8,128)(2,1)} %get-tuple-element.80, bf16[2560,1280]{1,0:T(8,128)(2,1)} %get-tuple-element.63), kind=kOutput, calls=%fused_computation.17 | convolution fusion | flops 6713507840 | bytes 14417920 | tf_op jit(solution)/shard_map/dot_general | solution.py:1638
  675.9 9.1 %convolution_convert_fusion.1 = bf16[2560,1280]{1,0:T(8,128)(2,1)} fusion(bf16[1024,2560]{1,0:T(8,128)(2,1)S(1)} %bitcast.51, bf16[1024,1280]{1,0:T(8,128)(2,1)S(1)} %copy-done.10), kind=kOutput, calls=%fused_computation.1 | convolution fusion | flops 6714163200 | bytes 14417920 | tf_op jit(solution)/shard_map/dot_general | solution.py:1647
  684.9 13.3 %reduce-scatter.5.cloned.1.call-done.in_both = bf16[320,3840]{1,0:T(8,128)(2,1)} async-done(((bf16[2560,3840]{1,0:T(8,128)(2,1)}), bf16[320,3840]{1,0:T(8,128)(2,1)}) %reduce-scatter.5.cloned.1.call-update) | async-done | bytes 2457616 | tf_op jit(solution)/shard_map/reduce_scatter | solution.py:1793
  698.2 92.4 %shard_map.242 = (f32[256,2560]{1,0:T(8,128)}, f32[320,640]{1,0:T(8,128)}, f32[320,640]{1,0:T(8,128)}, bf16[4,4,2,320,128]{4,3,2,1,0:T(8,128)(2,1)}, f32[4,8,640]{2,1,0:T(8,128)}) custom-call(bf16[1024,2560]{1,0:T(8,128)(2,1)} %convolution_convert_fusion.4.refs_0_, bf16[256,2560]{1,0:T(8,128)(2,1)} %refs_1_.3, f32[256,2560]{1,0:T(8,128)} %get-tuple-element.82.refs_2_, ...), custom_call_target="tpu_custom_call" | custom-call | bytes 1000000 | tf_op jit(solution)/shard_map/pallas_call | solution.py:940
  790.6 13.9 %shard_map.243 = (f32[2,10,256,256]{3,2,1,0:T(8,128)}, f32[320,640]{1,0:T(8,128)}, f32[320,640]{1,0:T(8,128)}, f32[320,640]{1,0:T(8,128)}, f32[256,2560]{1,0:T(8...) custom-call(bf16[20,2,256,128]{3,2,1,0:T(8,128)(2,1)} %bitcast.43, ...), custom_call_target="tpu_custom_call" | custom-call | tf_op jit(solution)/shard_map/pallas_call | solution.py:1511
  (55 shorter events, 16.7 us)
Async XLA Ops:
  7.2 104.1 %copy-start = (bf16[2,10,256,256]{3,2,1,0:T(8,128)(2,1)S(1)}, bf16[2,10,256,256]{3,2,1,0:T(8,128)(2,1)}, u32[]{:S(2)}) copy-start(bf16[2,10,256,256]{3,2,1,0:T(8,128)(2,1)} %param.21) | copy-start | bytes 7864324
  7.2 290.5 %all-gather.3.cloned.1.call-start = ((), (), s32[]{:S(2)}) async-start(), calls=%async_computation.2 | async-start | bytes 22118400 | tf_op jit(solution)/shard_map/all_gather | solution.py:1711
  8.7 97.2 %copy-start.6 = (f32[2560]{0:T(1024)S(1)}, f32[2560]{0:T(1024)}, u32[]{:S(2)}) copy-start(f32[2560]{0:T(1024)} %param.24) | copy-start | bytes 30724
  103.7 268.0 %all-gather.5.cloned.1.call-start = ((), (), s32[]{:S(2)}) async-start(), calls=%async_computation.3 | async-start | bytes 11059200 | tf_op jit(solution)/shard_map/all_gather | solution.py:1712
  104.4 471.6 %reduce-scatter.3.cloned.1.call-start = ((), (), s32[]{:S(2)}) async-start(), calls=%async_computation.4 | async-start | bytes 11059200 | tf_op jit(solution)/shard_map/reduce_scatter | solution.py:1787
  127.1 66.1 %copy-start.8 = (bf16[2560,640]{1,0:T(8,128)(2,1)S(1)}, bf16[2560,640]{1,0:T(8,128)(2,1)}, u32[]{:S(2)}) copy-start(bf16[2560,640]{1,0:T(8,128)(2,1)} %get-tuple-element.67) | copy-start | bytes 9830404
  322.8 5.5 copy-start.3
  328.3 1.9 copy-start.2
  345.9 352.3 %reduce-scatter.5.cloned.1.call-start = ((), (), s32[]{:S(2)}) async-start(), calls=%async_computation.5 | async-start | bytes 22118400 | tf_op jit(solution)/shard_map/reduce_scatter | solution.py:1793
  396.4 1.9 copy-start.4
  396.5 3.2 copy-start.5
  470.8 105.3 %copy-start.11 = (bf16[1024,640]{1,0:T(8,128)(2,1)S(1)}, bf16[1024,640]{1,0:T(8,128)(2,1)}, u32[]{:S(2)}) copy-start(bf16[1024,640]{1,0:T(8,128)(2,1)} %get-tuple-element.66) | copy-start | bytes 3932164
  576.0 8.7 %copy-start.7 = (bf16[1024,2560]{1,0:T(8,128)(2,1)S(1)}, bf16[1024,2560]{1,0:T(8,128)(2,1)}, u32[]{:S(2)}) copy-start(bf16[1024,2560]{1,0:T(8,128)(2,1)} %get-tuple-element.75) | copy-start | bytes 15728644
  576.1 8.7 %copy-start.9 = (bf16[2560,640]{1,0:T(8,128)(2,1)S(1)}, bf16[2560,640]{1,0:T(8,128)(2,1)}, u32[]{:S(2)}) copy-start(bf16[2560,640]{1,0:T(8,128)(2,1)} %get-tuple-element.67) | copy-start | bytes 9830404
  590.5 85.4 %slice-start = ((s8[5242880]{0:T(1024)(128)(4,1)}), s8[1048576]{0:T(1024)(128)(4,1)S(1)}, s32[]{:S(2)}) async-start(s8[5242880]{0:T(1024)(128)(4,1)} %bitcast.50), calls=%async_computation.6 | async-start | bytes 2097152
  663.4 12.4 %slice-start.1 = ((s8[5242880]{0:T(1024)(128)(4,1)}), s8[4194304]{0:T(1024)(128)(4,1)S(1)}, s32[]{:S(2)}) async-start(s8[5242880]{0:T(1024)(128)(4,1)} %bitcast.50), calls=%async_computation.7 | async-start | bytes 8388608
  663.4 12.4 %copy-start.10 = (bf16[1024,1280]{1,0:T(8,128)(2,1)S(1)}, bf16[1024,1280]{1,0:T(8,128)(2,1)}, u32[]{:S(2)}) copy-start(bf16[1024,1280]{1,0:T(8,128)(2,1)} %get-tuple-element.80) | copy-start | bytes 7864324
  790.6 13.9 %copy-start.1 = (bf16[2,10,256,256]{3,2,1,0:T(8,128)(2,1)S(1)}, bf16[2,10,256,256]{3,2,1,0:T(8,128)(2,1)}, u32[]{:S(2)}) copy-start(bf16[2,10,256,256]{3,2,1,0:T(8,128)(2,1)} %param.21) | copy-start | bytes 7864324
Sparse Core Ops, SparseCore 0:
  103.8 173.9 all-gather.2
  279.5 92.1 all-gather.4
  374.0 101.6 reduce-scatter.2
  478.1 220.0 reduce-scatter.4

commit v3 on v2

--- a/solution.py
+++ b/solution.py
@@ -632,9 +632,12 @@
     def slot(self, way, distance):
         return (0 if way == UP else self.chips - 1) + distance
 
+    def stage(self, way, distance):
+        return distance - 1 if way == UP else self.chips - 1 - distance
+
     def hop(self, way, distance):
         return pltpu.make_async_remote_copy(
-            src_ref=self.staged.at[self.slot(way, distance - 1)],
+            src_ref=self.staged.at[self.stage(way, distance)],
             dst_ref=self.landed.at[self.slot(way, distance - 1)],
             send_sem=self.sems[0].at[1 + self.slot(way, distance - 1)],
             recv_sem=self.sems[1].at[1 + self.slot(way, distance - 1)],
@@ -669,7 +672,7 @@
             @pl.when(self.has(way, distance))
             def _(way=way):
                 chip = self.chip + way * distance
-                slot = self.slot(way, distance - 1)
+                slot = self.stage(way, distance)
 
                 def first(row):
                     span = pl.ds(row, CHUNK)
@@ -740,7 +743,7 @@
     return [
         pltpu.VMEM((chips, rows, columns), BF16),
         pltpu.VMEM((chips, rows, columns), BF16),
-        pltpu.VMEM((2 * chips - 2, rows, columns), BF16),
+        pltpu.VMEM((chips - 1, rows, columns), BF16),
         pltpu.VMEM((2 * chips - 2, rows, columns), BF16),
         pltpu.SemaphoreType.DMA((2 * chips + 1,)),
         pltpu.SemaphoreType.DMA((2 * chips + 1,)),
@@ -750,7 +753,7 @@
 RING = 6
 
 
-def leave_kernel(nbits, tiled, *refs):
+def leave_kernel(nbits, tiled, with_ffn, *refs):
     refs = list(refs)
 
     def take(count):
@@ -759,15 +762,18 @@
         return taken
 
     d_norm, tokens, d_middle, gain, own_small, d_gain_mid = take(6)
-    pieces = take(2)
-    grad_input, sum_y, sum_x, gate_all, small_all = take(5)
+    pieces = take(3)
+    ffn, middle = take(2) if with_ffn else (None, None)
+    grad_input, sum_out, sum_y, sum_x, gate_all, small_all = take(6)
+    mixed = take(1)[0] if with_ffn else None
     landed, staged, s0, r0 = take(4)
     share = small_all.shape[2]
     gate = LineSum(pieces[0], *take(RING))
+    lines = [LineSum(pieces[1], *take(RING))]
     if tiled:
-        lines = [LineSum(pieces[1], *take(RING), pl.ds(at, share)) for at in (0, share)]
+        lines += [LineSum(pieces[2], *take(RING), pl.ds(at, share)) for at in (0, share)]
     else:
-        lines = [LineSum(pieces[1], *take(RING))]
+        lines += [LineSum(pieces[2], *take(RING))]
     d_gain, gains, gains_landed, small, small_landed = take(5)
     gain_s, gain_r, vec_s, vec_r, join_s, join_r, gate_s, gate_r = take(8)
     rows = tokens.shape[0]
@@ -780,13 +786,18 @@
         line.begin()
     scatter = Scatter(d_norm, landed, staged, rows, nbits, s0, r0)
     scatter.begin()
+    if with_ffn:
+        second = Scatter(ffn, *take(2), rows, nbits, *take(2))
     d_gain[...] = jnp.zeros_like(d_gain)
     far = list(range(chips - 1, 0, -1))
-    for distance in far:
-        gate.send(distance)
-    for line in lines:
-        line.send(far[0])
+    for number in range(max(len(far), len(lines))):
+        if number < len(far):
+            gate.send(far[number])
+        if number < len(lines):
+            lines[number].send(far[0])
     scatter.advance(0)
+    if with_ffn:
+        second.begin()
     for distance in far[1:-1]:
         for line in lines:
             line.send(distance)
@@ -900,9 +911,20 @@
 
     for number, chosen in enumerate(peers):
         join_copy(number, chosen).start()
+    if with_ffn:
+        second.advance(0)
     for number, chosen in enumerate(peers):
         gate_tensor(number, chosen).wait_recv()
     gate_core().start()
+    if with_ffn:
+        for step in range(1, nbits):
+            second.advance(step)
+
+        def add(row):
+            span = pl.ds(row, CHUNK)
+            mixed[span, :] = (middle[span, :] + second.total(row, CHUNK)).astype(BF16)
+
+        chunks(rows, add)
 
     def store_in(*targets):
         def store(span, value):
@@ -911,11 +933,12 @@
 
         return store
 
+    lines[0].finish(store_in(sum_out))
     if tiled:
-        lines[0].finish(store_in(sum_y))
-        lines[1].finish(store_in(sum_x))
+        lines[1].finish(store_in(sum_y))
+        lines[2].finish(store_in(sum_x))
     else:
-        lines[0].finish(store_in(sum_y, sum_x))
+        lines[1].finish(store_in(sum_y, sum_x))
     gate_core().wait()
     for shift in range(1, chips):
         gate_line(shift).wait_send()
@@ -926,6 +949,8 @@
     for number, (shift, turn) in enumerate(others):
         vec_copy(number, shift, turn).wait_send()
     scatter.drain()
+    if with_ffn:
+        second.drain()
     for line in [gate] + lines:
         line.drain()
 
@@ -934,7 +959,7 @@
     return [pl.BlockSpec(memory_space=pltpu.VMEM)] * count
 
 
-def call_kernel(kernel, outs, scratch, number, *operands, far_in=(), far_out=(), cost_us=1):
+def call_kernel(kernel, outs, scratch, number, *operands, far_in=(), far_out=(), cost_us=1, vmem_bytes=VMEM_BYTES):
     vmem = pl.BlockSpec(memory_space=pltpu.VMEM)
     far = pl.BlockSpec(memory_space=pl.ANY)
     return pl.pallas_call(
@@ -947,7 +972,7 @@
             flops=0, bytes_accessed=cost_us * 1_000_000, transcendentals=0
         ),
         compiler_params=pltpu.CompilerParams(
-            collective_id=number, has_side_effects=True, vmem_limit_bytes=VMEM_BYTES
+            collective_id=number, has_side_effects=True, vmem_limit_bytes=vmem_bytes
         ),
     )(*operands)
 
@@ -1240,8 +1265,6 @@
 
 def recurrence_back_kernel(
     taps,
-    nbits,
-    with_ffn,
     d_mixed,
     window,
     gates,
@@ -1252,34 +1275,24 @@
     slope_soft,
     since,
     weights,
-    *refs,
+    d_branches,
+    gate_grad,
+    own_small,
+    d_conv,
+    d_gates,
+    given,
+    taken,
+    sums,
+    send,
+    recv,
 ):
-    refs = list(refs)
-
-    def take(count):
-        taken = refs[:count]
-        del refs[:count]
-        return taken
-
-    ffn, middle = take(2) if with_ffn else (None, None)
-    grad_out = take(1)[0]
-    d_branches, gate_grad, own_small, sum_out = take(4)
-    mixed = take(1)[0] if with_ffn else None
-    d_conv, d_gates, given, taken, sums, send, recv = take(7)
-    flow = LineSum(grad_out, *take(RING))
-    far = list(range(flow.chips - 1, 0, -1))
     total_rows, width = states.shape
     block = weights.shape[2]
     place = HalfBlocks(width, block)
     half = place.half
     branch_y, branch_x = branches.at[:, :width], branches.at[:, width:]
     d_branch_y, d_branch_x = d_branches.at[:, :width], d_branches.at[:, width:]
-    greet_peers(nbits, False, False)
-    flow.begin()
-    if with_ffn:
-        scatter = Scatter(ffn, *take(2), middle.shape[0], nbits, *take(2))
-        scatter.begin()
-    flow.send(far[0])
+    greet([("tensor", 0)])
     backward_scan(
         d_mixed,
         lambda span: window[span, pl.ds(place.own, width)],
@@ -1319,8 +1332,6 @@
         device_id_type=MESH,
     )
     rim.start()
-    for distance in far[1:-1]:
-        flow.send(distance)
 
     def full(span):
         for index in range(place.count - 1):
@@ -1345,8 +1356,6 @@
         d_conv[span, pl.ds(place.mine, half)] = total
 
     parts(total_rows, full)
-    if with_ffn:
-        scatter.advance(0)
     units = width // half
     for index in range(units):
         number = (index + place.odd) // 2
@@ -1361,8 +1370,6 @@
         gate_grad[2 * index] = found[:, :half]
         gate_grad[2 * index + 1] = found[:, half:]
     rim.wait()
-    if len(far) > 1:
-        flow.send(far[-1])
 
     def add(span):
         d_conv[span, pl.ds(place.mine, half)] += taken[span, :].astype(F32)
@@ -1410,22 +1417,6 @@
         row = jnp.sum(sums[tap], axis=0, keepdims=True)
         total = jnp.where(line == tap, row, total)
     own_small[...] = total
-    if with_ffn:
-        for step in range(1, nbits):
-            scatter.advance(step)
-
-        def result(row):
-            span = pl.ds(row, CHUNK)
-            mixed[span, :] = (middle[span, :] + scatter.total(row, CHUNK)).astype(BF16)
-
-        chunks(middle.shape[0], result)
-        scatter.drain()
-
-    def store(span, value):
-        sum_out[span, :] = value
-
-    flow.finish(store)
-    flow.drain()
 
 
 def finish_kernel(
@@ -1815,17 +1806,15 @@
     grad_wout = inner_rows(d_mixer, mixed_low).astype(BF16)
     d_mixed_in = jnp.dot(d_mixer, wout_loc, preferred_element_type=F32)
     unit = math.gcd(channels, block_size)
-    merged = half_blocks and nbits <= 2
+    merged = nbits <= 2
     if half_blocks:
-        found = call_kernel(
-            partial(recurrence_back_kernel, taps, nbits, merged),
+        d_branches, gate_grad, own_small = call_kernel(
+            partial(recurrence_back_kernel, taps),
             (
                 shape((group_rows, 2 * channels), BF16),
                 shape((channels // unit * 2, block_size, unit), BF16),
                 shape((8, channels), F32),
-                shape((dp_rows, channels), F32),
-            )
-            + ((shape((own_rows, width), BF16),) if merged else ()),
+            ),
             [
                 pltpu.VMEM((group_rows, channels), F32),
                 pltpu.VMEM((group_rows, 2 * channels), BF16),
@@ -1834,9 +1823,7 @@
                 pltpu.VMEM((taps + 1, 8, channels), F32),
                 pltpu.SemaphoreType.DMA((1,)),
                 pltpu.SemaphoreType.DMA((1,)),
-            ]
-            + line_scratch(ndp, dp_rows, channels)
-            + (scatter_scratch(own_rows, width, nbits) if merged else []),
+            ],
             6,
             d_mixed_in,
             window,
@@ -1848,11 +1835,7 @@
             slope_soft,
             since,
             w_window,
-            *((ffn_part, middle) if merged else ()),
-            halved(grad_wout, ndp),
-            far_in=(12 if merged else 10,),
-        )
-        d_branches, gate_grad, own_small, sum_wout = found[:4]
+        )
         gate_grad = gate_grad.reshape(channels // unit * 2 * block_size, unit)
     else:
         d_conv, d_gate_low, d_branch_y, d_decay = scan_call(
@@ -1901,17 +1884,13 @@
 
     grad_wyx = inner_rows(normed_rows, d_branches).astype(BF16)
     d_normed = rows_times(d_branches, wyx_loc).astype(BF16)
-    d_normed, grad_wyx, sum_both = lax.optimization_barrier((d_normed, grad_wyx, sum_both))
-    if not half_blocks:
-        sum_wout = lax.psum_scatter(grad_wout, "dp", scatter_dimension=0, tiled=True)
-        sum_wout = sum_wout.astype(F32)
-
-    pieces = [halved(grad, ndp) for grad in (gate_grad, grad_wyx)]
+
+    pieces = [halved(grad, ndp) for grad in (gate_grad, grad_wout, grad_wyx)]
     peers = ntensor - 1
     gate_rows = gate_grad.shape[0] // ndp
     dma = pltpu.SemaphoreType.DMA
     scratch = scatter_scratch(own_rows, width, nbits)
-    scratch += line_scratch(ndp, gate_rows, unit)
+    scratch += line_scratch(ndp, gate_rows, unit) + line_scratch(ndp, dp_rows, channels)
     if tiled:
         scratch += line_scratch(ndp, dp_rows, channels) * 2
     else:
@@ -1925,14 +1904,17 @@
     ]
     scratch += [dma((peers,)), dma((peers,)), dma((ndp - 1,)), dma((ndp - 1,))]
     scratch += [dma((peers,)), dma((peers,)), dma((peers + ndp,)), dma((peers + ndp,))]
-    grad_input, sum_wy, sum_wx, gate_all, small_all = call_kernel(
-        partial(leave_kernel, nbits, tiled),
+    if merged:
+        scratch += scatter_scratch(own_rows, width, nbits)
+    found = call_kernel(
+        partial(leave_kernel, nbits, tiled, merged),
         (shape((own_rows, width), F32),)
-        + (shape((dp_rows, channels), F32),) * 2
+        + (shape((dp_rows, channels), F32),) * 3
         + (
             shape((ntensor, ndp // 2, 2, gate_rows, unit), BF16),
             shape((ntensor, 8, channels), F32),
-        ),
+        )
+        + ((shape((own_rows, width), BF16),) if merged else ()),
         scratch,
         3,
         d_normed,
@@ -1942,10 +1924,13 @@
         own_small,
         d_gain_mid,
         *pieces,
-        far_in=(6, 7),
+        *((ffn_part, middle) if merged else ()),
+        far_in=(6, 7, 8),
+        vmem_bytes=60 * 1024 * 1024,
     )
+    grad_input, sum_wout, sum_wy, sum_wx, gate_all, small_all = found[:6]
     if merged:
-        mixed = found[4]
+        mixed = found[6]
     else:
         (mixed,) = call_kernel(
             partial(result_kernel, nbits),
@@ -1955,6 +1940,7 @@
             ffn_part,
             middle,
         )
+    gate_all, sum_both = lax.optimization_barrier((gate_all, sum_both))
     found = finish(
         gate_all,
         small_all,

time: 822 us -> 816 us (level)
  Pallas kernels: 539 us -> 557 us
  waiting for transfers between devices: 39.7 us -> 26.5 us
  matrix products: 186 us -> 176 us
    pallas_call x6, Pallas kernels: 525 us -> 543 us  [call_kernel(): pl.pallas_call(kernel, out_shape=outs, in_specs=[far if i in far_in else...]
    dot_general x3, matrix products: 56.6 us -> 43.3 us  [rows_times(): lax.dot_general(left, right, (((1,), (1,)), ((), ())), preferred_element_...]
    reduce_scatter x1, waiting for transfers between devices: 13.3 us -> 0.02 us  [body(): lax.psum_scatter(grad_both, 'dp', scatter_dimension=0, tiled=True)]
  transfers between devices with their start and end apart: 4 -> 4, of which waited for: 2 -> 1; matrix products, arithmetic and copies ran while one was open for 25% -> 24% of each run, Pallas kernels for 42% -> 56%
where the time goes in v3:
time: 816 us; the launch traced here: 806 us
  Pallas kernels  557 us (68%)
  matrix products  176 us (22%)
  waiting for transfers between devices  26.5 us (3%)
  other arithmetic  16.5 us (2%)
  local copies, waits for them, and re-layouts  14.9 us (2%)
  between operations  14.2 us (2%)
    pallas_call x6, Pallas kernels, call_kernel(): pl.pallas_call(kernel, out_shape=outs, in_specs=[far if i in far_in else...  543 us
    dot_general x4, matrix products, inner_rows(): lax.dot_general(left, right, (((0,), (0,)), ((), ())), preferred_element_...  60.2 us
    dot_general x3, matrix products, rows_times(): lax.dot_general(left, right, (((1,), (1,)), ((), ())), preferred_element_...  43.3 us
    all_gather x1, waiting for transfers between devices, body(): wd_loc = lax.all_gather(w_down, 'dp', axis=0, tiled=True)  25.7 us
    dot_general x1, matrix products, body(): pre = jnp.dot(mid_rows, both_loc, preferred_element_type=F32)  25 us
    dot_general x1, matrix products, body(): d_hidden = jnp.dot(cot_rows, wd_loc, preferred_element_type=F32)  24.7 us
  transfers between devices with their start and end apart: 4, of which 1 were waited for; matrix products, arithmetic and copies ran while one was open for 24% of the time, Pallas kernels for 56%

profile of v3, /device:TPU:0, one launch (start us, length us, event | category | flops | bytes accessed | tf_op | source)
XLA Modules:
  0.0 805.5 jit_solution(15116413989081271538)
XLA Ops:
  8.7 3.3 pad_maximum_fusion.1
  12.0 91.7 %shard_map.237 = (bf16[1024,2560]{1,0:T(8,128)(2,1)}, s32[4,2,128]{2,1,0:T(2,128)}, bf16[2560,1280]{1,0:T(8,128)(2,1)}, bf16[2560,640]{1,0:T(8,128)(2,1)}) custom-call(bf16[256,2560]{1,0:T(8,128)(2,1)} %refs_1_.3, s32[2,128]{1,0:T(2,128)} %bitcast.49, f32[1,2560]{1,0:T(1,128)} %reshape.121.gain.refs_3_, bf16[320,640]{1,0:T(8,128)(2,1)} %refs_0_.1, ...), custom_call_target="tpu_custom_call" | custom-call | bytes 1000000 | tf_op jit(solution)/shard_map/pallas_call | solution.py:965
  113.1 14.0 %fusion.12.branches = f32[1024,1280]{1,0:T(8,128)} fusion(bf16[1024,2560]{1,0:T(8,128)(2,1)} %get-tuple-element.61, bf16[2560,1280]{1,0:T(8,128)(2,1)} %get-tuple-element.62), kind=kOutput, calls=%fused_computation.38 | convolution fusion | flops 6710886400 | bytes 17039360 | tf_op jit(solution)/shard_map/dot_general | solution.py:1714
  127.1 66.1 %shard_map.238 = (bf16[1024,640]{1,0:T(8,128)(2,1)}, f32[1024,640]{1,0:T(8,128)}, bf16[1024,768]{1,0:T(8,128)(2,1)}, f32[1024,1280]{1,0:T(8,128)}, bf16[1024,2560]{1,0:T(8,128)(2,1)}) custom-call(f32[1024,1280]{1,0:T(8,128)} %fusion.12.branches, f32[8,640]{1,0:T(8,128)} %concatenate.15.tap_rows, f32[1,640]{1,0:T(1,128)} %select_n.32.soft, ...), custom_call_target="tpu_custom_call" | custom-call | bytes 1000000 | tf_op jit(solution)/shard_map/pallas_call | solution.py:965
  193.2 7.4 convolution_convert_fusion.3.mixer
  200.6 97.1 %shard_map.239 = (f32[256,2560]{1,0:T(8,128)}, bf16[1024,2560]{1,0:T(8,128)(2,1)}) custom-call(bf16[1024,2560]{1,0:T(8,128)(2,1)} %convolution_convert_fusion.3.mixer, bf16[256,2560]{1,0:T(8,128)(2,1)} %refs_1_.3, f32[1,2560]{1,0:T(1,128)} %reshape.125.gain), custom_call_target="tpu_custom_call" | custom-call | bytes 1000000 | tf_op jit(solution)/shard_map/pallas_call | solution.py:965
  297.7 25.0 %fusion.13 = f32[1024,3840]{1,0:T(8,128)S(1)} fusion(bf16[1024,2560]{1,0:T(8,128)(2,1)} %get-tuple-element.67, bf16[2560,3840]{1,0:T(8,128)(2,1)} %all-gather.3.cloned.1.call-done), kind=kOutput, calls=%fused_computation.39 | convolution fusion | flops 20132659200 | bytes 40632320 | tf_op jit(solution)/shard_map/dot_general | solution.py:1774
  322.8 2.8 multiply_convert_fusion.1.hidden
  325.6 2.7 copy-done.3
  328.3 1.9 copy-done.2
  330.2 15.7 %convolution_convert_fusion.2 = bf16[2560,1920]{1,0:T(8,128)(2,1)} fusion(bf16[1024,2560]{1,0:T(8,128)(2,1)} %get-tuple-element.64, bf16[1024,1920]{1,0:T(8,128)(2,1)S(1)} %multiply_convert_fusion.1.hidden), kind=kOutput, calls=%fused_computation.2 | convolution fusion | flops 10071244800 | bytes 19005440 | tf_op jit(solution)/shard_map/dot_general | solution.py:1638
  345.9 25.7 %all-gather.5.cloned.1.call-done.w_down = bf16[2560,1920]{1,0:T(8,128)(2,1)} async-done(((bf16[320,1920]{1,0:T(8,128)(2,1)}), bf16[2560,1920]{1,0:T(8,128)(2,1)}) %all-gather.5.cloned.1.call-update) | async-done | bytes 9830416 | tf_op jit(solution)/shard_map/all_gather | solution.py:1703
  371.7 24.7 %fusion.6 = (bf16[1024,1920]{1,0:T(8,128)(2,1)S(1)}, bf16[1024,1920]{1,0:T(8,128)(2,1)S(1)}) fusion(f32[1024,3840]{1,0:T(8,128)} %copy-done.3, bf16[1024,2560]{1,0:T(8,128)(2,1)} %get-tuple-element.64, bf16[2560,1920]{1,0:T(8,128)(2,1)} %all-gather.5.cloned.1.call-done.w_down), kind=kOutput, calls=%fused_computation.11 | convolution fusion | flops 10113515520 | bytes 38666240 | tf_op jit(solution)/shard_map/dot_general | solution.py:1780
  399.6 26.7 %convolution_convert_fusion = bf16[2560,3840]{1,0:T(8,128)(2,1)} fusion(bf16[1024,2560]{1,0:T(8,128)(2,1)} %get-tuple-element.67, bf16[1024,1920]{1,0:T(8,128)(2,1)S(1)} %get-tuple-element.108, bf16[1024,1920]{1,0:T(8,128)(2,1)S(1)} %get-tuple-element.107), kind=kOutput, calls=%fused_computation | convolution fusion | flops 20158218240 | bytes 32768000 | tf_op jit(solution)/shard_map/dot_general | solution.py:1638
  426.9 7.0 pad_maximum_fusion
  433.8 27.2 %convolution_convert_fusion.5.d_norm = bf16[1024,2560]{1,0:T(8,128)(2,1)} fusion(bf16[1024,3840]{1,0:T(8,128)(2,1)} %pad_maximum_fusion, bf16[2560,3840]{1,0:T(8,128)(2,1)} %all-gather.3.cloned.1.call-done), kind=kOutput, calls=%fused_computation.18 | convolution fusion | flops 20135280640 | bytes 32768000 | tf_op jit(solution)/shard_map/dot_general | solution.py:1629
  461.1 105.3 %shard_map.240 = (f32[256,2560]{1,0:T(8,128)}, bf16[1024,2560]{1,0:T(8,128)(2,1)}, f32[8,2560]{1,0:T(8,128)}, bf16[1024,2560]{1,0:T(8,128)(2,1)}) custom-call(bf16[1024,2560]{1,0:T(8,128)(2,1)} %convolution_convert_fusion.5.d_norm, bf16[256,2560]{1,0:T(8,128)(2,1)} %cot.3, f32[256,2560]{1,0:T(8,128)} %get-tuple-element.72.middle.refs_10_, ...), custom_call_target="tpu_custom_call" | custom-call | bytes 1000000 | tf_op jit(solution)/shard_map/pallas_call | solution.py:965
  566.4 9.3 %fusion.14.d_mixed = f32[1024,640]{1,0:T(8,128)} fusion(bf16[1024,2560]{1,0:T(8,128)(2,1)} %get-tuple-element.74, bf16[2560,640]{1,0:T(8,128)(2,1)} %get-tuple-element.66), kind=kOutput, calls=%fused_computation.40 | convolution fusion | flops 3355443200 | bytes 11141120 | tf_op jit(solution)/shard_map/dot_general | solution.py:1807
  575.7 35.8 %shard_map.241 = (bf16[1024,1280]{1,0:T(8,128)(2,1)}, bf16[10,256,128]{2,1,0:T(8,128)(2,1)}, f32[8,640]{1,0:T(8,128)}) custom-call(f32[1024,640]{1,0:T(8,128)} %fusion.14.d_mixed, bf16[1024,768]{1,0:T(8,128)(2,1)} %get-tuple-element.75.window, f32[1024,1280]{1,0:T(8,128)} %get-tuple-element.76.gates, f32[1024,1280]{1,0:T(8,128)} %fusion.12.branches, ...), custom_call_target="tpu_custom_call" | custom-call | bytes 1000000 | tf_op jit(solution)/shard_map/pallas_call | solution.py:965
  611.5 8.8 %convolution_convert_fusion.6 = bf16[2560,640]{1,0:T(8,128)(2,1)} fusion(bf16[1024,2560]{1,0:T(8,128)(2,1)} %get-tuple-element.74, bf16[1024,640]{1,0:T(8,128)(2,1)S(1)} %copy-done.9), kind=kOutput, calls=%fused_computation.19 | convolution fusion | flops 3357081600 | bytes 9830400 | tf_op jit(solution)/shard_map/dot_general | solution.py:1638
  620.3 8.7 %convolution_convert_fusion.4.refs_0_ = bf16[1024,2560]{1,0:T(8,128)(2,1)} fusion(bf16[1024,1280]{1,0:T(8,128)(2,1)S(1)} %copy-done.8, bf16[2560,1280]{1,0:T(8,128)(2,1)S(1)} %bitcast.51), kind=kOutput, calls=%fused_computation.17 | convolution fusion | flops 6713507840 | bytes 14417920 | tf_op jit(solution)/shard_map/dot_general | solution.py:1629
  629.0 9.0 %convolution_convert_fusion.1 = bf16[2560,1280]{1,0:T(8,128)(2,1)} fusion(bf16[1024,2560]{1,0:T(8,128)(2,1)S(1)} %bitcast.53, bf16[1024,1280]{1,0:T(8,128)(2,1)S(1)} %copy-done.8), kind=kOutput, calls=%fused_computation.1 | convolution fusion | flops 6714163200 | bytes 14417920 | tf_op jit(solution)/shard_map/dot_general | solution.py:1638
  638.0 146.8 %shard_map.242 = (f32[256,2560]{1,0:T(8,128)}, f32[320,640]{1,0:T(8,128)}, f32[320,640]{1,0:T(8,128)}, f32[320,640]{1,0:T(8,128)}, bf16[4,4,2,320,128]{4,3,2,1,0...) custom-call(bf16[1024,2560]{1,0:T(8,128)(2,1)} %convolution_convert_fusion.4.refs_0_, ...), custom_call_target="tpu_custom_call" | custom-call | bytes 1000000 | tf_op jit(solution)/shard_map/pallas_call | solution.py:965
  784.9 13.9 %shard_map.243 = (f32[2,10,256,256]{3,2,1,0:T(8,128)}, f32[320,640]{1,0:T(8,128)}, f32[320,640]{1,0:T(8,128)}, f32[320,640]{1,0:T(8,128)}, f32[256,2560]{1,0:T(8...) custom-call(bf16[20,2,256,128]{3,2,1,0:T(8,128)(2,1)} %bitcast.43, ...), custom_call_target="tpu_custom_call" | custom-call | tf_op jit(solution)/shard_map/pallas_call | solution.py:1502
  (56 shorter events, 14.8 us)
Async XLA Ops:
  7.2 104.1 %copy-start = (bf16[2,10,256,256]{3,2,1,0:T(8,128)(2,1)S(1)}, bf16[2,10,256,256]{3,2,1,0:T(8,128)(2,1)}, u32[]{:S(2)}) copy-start(bf16[2,10,256,256]{3,2,1,0:T(8,128)(2,1)} %param.21) | copy-start | bytes 7864324
  7.2 290.5 %all-gather.3.cloned.1.call-start = ((), (), s32[]{:S(2)}) async-start(), calls=%async_computation.2 | async-start | bytes 22118400 | tf_op jit(solution)/shard_map/all_gather | solution.py:1702
  8.7 97.2 %copy-start.6 = (f32[2560]{0:T(1024)S(1)}, f32[2560]{0:T(1024)}, u32[]{:S(2)}) copy-start(f32[2560]{0:T(1024)} %param.24) | copy-start | bytes 30724
  103.7 268.0 %all-gather.5.cloned.1.call-start = ((), (), s32[]{:S(2)}) async-start(), calls=%async_computation.3 | async-start | bytes 11059200 | tf_op jit(solution)/shard_map/all_gather | solution.py:1703
  104.4 462.0 %reduce-scatter.3.cloned.1.call-start = ((), (), s32[]{:S(2)}) async-start(), calls=%async_computation.4 | async-start | bytes 11059200 | tf_op jit(solution)/shard_map/reduce_scatter | solution.py:1778
  127.1 66.1 %copy-start.7 = (bf16[2560,640]{1,0:T(8,128)(2,1)S(1)}, bf16[2560,640]{1,0:T(8,128)(2,1)}, u32[]{:S(2)}) copy-start(bf16[2560,640]{1,0:T(8,128)(2,1)} %get-tuple-element.66) | copy-start | bytes 9830404
  322.8 5.5 copy-start.3
  328.3 1.9 copy-start.2
  345.9 439.0 %reduce-scatter.5.cloned.1.call-start = ((), (), s32[]{:S(2)}) async-start(), calls=%async_computation.5 | async-start | bytes 22118400 | tf_op jit(solution)/shard_map/reduce_scatter | solution.py:1784
  396.4 1.9 copy-start.4
  396.4 3.2 copy-start.5
  575.7 35.8 %copy-start.9 = (bf16[1024,640]{1,0:T(8,128)(2,1)S(1)}, bf16[1024,640]{1,0:T(8,128)(2,1)}, u32[]{:S(2)}) copy-start(bf16[1024,640]{1,0:T(8,128)(2,1)} %get-tuple-element.65) | copy-start | bytes 3932164
  575.7 44.6 %slice-start = ((s8[6553600]{0:T(1024)(128)(4,1)}), s8[2359296]{0:T(1024)(128)(4,1)S(1)}, s32[]{:S(2)}) async-start(s8[6553600]{0:T(1024)(128)(4,1)} %bitcast.50), calls=%async_computation.6 | async-start | bytes 4718592
  611.5 8.8 %slice-start.1 = ((s8[6553600]{0:T(1024)(128)(4,1)}), s8[4194304]{0:T(1024)(128)(4,1)S(1)}, s32[]{:S(2)}) async-start(s8[6553600]{0:T(1024)(128)(4,1)} %bitcast.50), calls=%async_computation.7 | async-start | bytes 8388608
  611.5 8.8 %copy-start.8 = (bf16[1024,1280]{1,0:T(8,128)(2,1)S(1)}, bf16[1024,1280]{1,0:T(8,128)(2,1)}, u32[]{:S(2)}) copy-start(bf16[1024,1280]{1,0:T(8,128)(2,1)} %get-tuple-element.78) | copy-start | bytes 7864324
  611.5 17.5 %slice-start.2 = ((s8[5242880]{0:T(1024)(128)(4,1)}), s8[4194304]{0:T(1024)(128)(4,1)S(1)}, s32[]{:S(2)}) async-start(s8[5242880]{0:T(1024)(128)(4,1)} %bitcast.52), calls=%async_computation.8 | async-start | bytes 8388608
  620.3 8.7 %slice-start.3 = ((s8[5242880]{0:T(1024)(128)(4,1)}), s8[1048576]{0:T(1024)(128)(4,1)S(1)}, s32[]{:S(2)}) async-start(s8[5242880]{0:T(1024)(128)(4,1)} %bitcast.52), calls=%async_computation.9 | async-start | bytes 2097152
  784.9 13.9 %copy-start.1 = (bf16[2,10,256,256]{3,2,1,0:T(8,128)(2,1)S(1)}, bf16[2,10,256,256]{3,2,1,0:T(8,128)(2,1)}, u32[]{:S(2)}) copy-start(bf16[2,10,256,256]{3,2,1,0:T(8,128)(2,1)} %param.21) | copy-start | bytes 7864324
Sparse Core Ops, SparseCore 0:
  103.8 174.0 all-gather.2
  279.6 92.0 all-gather.4
  374.0 101.6 reduce-scatter.2
  478.1 212.8 reduce-scatter.4

commit v4 on v2

--- a/solution.py
+++ b/solution.py
@@ -361,11 +361,18 @@
     pl.semaphore_wait(barrier, met)
 
 
+def widen(rows, wide):
+    for row in range(rows.shape[0]):
+        wide[:, row * 128 : (row + 1) * 128] = rows[row : row + 1, :]
+
+
 def enter_kernel(
     nbits, parts_yx, tokens, seg, gain, *refs
 ):
     w_yx, w_out = refs[:parts_yx], refs[parts_yx]
-    normed_all, seg_all, wyx_all, wout_all, s0, r0, s2, r2, l0, *line = refs[parts_yx + 1 :]
+    normed_all, seg_all, wyx_all, wout_all, gain_row, s0, r0, s2, r2, l0, *line = refs[
+        parts_yx + 1 :
+    ]
     rows = tokens.shape[0]
     me = lax.axis_index("tensor")
     peers = [chosen for chosen in subsets(tuple(range(nbits))) if chosen]
@@ -384,10 +391,11 @@
     lines.append(LineGather(w_out, wout_all, *line[2 * parts_yx : 2 * parts_yx + 2]))
     for item in lines:
         item.begin()
+    widen(gain, gain_row)
 
     def norm(row):
         values = tokens[pl.ds(row, CHUNK), :].astype(F32)
-        scaled = values * rms_scale_of(values) * gain[...]
+        scaled = values * rms_scale_of(values) * gain_row[...]
         normed_all[pl.ds(own_row(row, rows), CHUNK), :] = scaled.astype(BF16)
 
     chunks(rows, norm)
@@ -782,10 +790,11 @@
     scatter.begin()
     d_gain[...] = jnp.zeros_like(d_gain)
     far = list(range(chips - 1, 0, -1))
-    for distance in far:
-        gate.send(distance)
-    for line in lines:
-        line.send(far[0])
+    for number in range(max(len(far), len(lines))):
+        if number < len(far):
+            gate.send(far[number])
+        if number < len(lines):
+            lines[number].send(far[0])
     scatter.advance(0)
     for distance in far[1:-1]:
         for line in lines:
@@ -1262,24 +1271,19 @@
         return taken
 
     ffn, middle = take(2) if with_ffn else (None, None)
-    grad_out = take(1)[0]
-    d_branches, gate_grad, own_small, sum_out = take(4)
+    d_branches, gate_grad, own_small = take(3)
     mixed = take(1)[0] if with_ffn else None
     d_conv, d_gates, given, taken, sums, send, recv = take(7)
-    flow = LineSum(grad_out, *take(RING))
-    far = list(range(flow.chips - 1, 0, -1))
     total_rows, width = states.shape
     block = weights.shape[2]
     place = HalfBlocks(width, block)
     half = place.half
     branch_y, branch_x = branches.at[:, :width], branches.at[:, width:]
     d_branch_y, d_branch_x = d_branches.at[:, :width], d_branches.at[:, width:]
-    greet_peers(nbits, False, False)
-    flow.begin()
+    greet(tensor_bits(nbits))
     if with_ffn:
         scatter = Scatter(ffn, *take(2), middle.shape[0], nbits, *take(2))
         scatter.begin()
-    flow.send(far[0])
     backward_scan(
         d_mixed,
         lambda span: window[span, pl.ds(place.own, width)],
@@ -1319,8 +1323,6 @@
         device_id_type=MESH,
     )
     rim.start()
-    for distance in far[1:-1]:
-        flow.send(distance)
 
     def full(span):
         for index in range(place.count - 1):
@@ -1361,8 +1363,6 @@
         gate_grad[2 * index] = found[:, :half]
         gate_grad[2 * index + 1] = found[:, half:]
     rim.wait()
-    if len(far) > 1:
-        flow.send(far[-1])
 
     def add(span):
         d_conv[span, pl.ds(place.mine, half)] += taken[span, :].astype(F32)
@@ -1421,12 +1421,6 @@
         chunks(middle.shape[0], result)
         scatter.drain()
 
-    def store(span, value):
-        sum_out[span, :] = value
-
-    flow.finish(store)
-    flow.drain()
-
 
 def finish_kernel(
     taps,
@@ -1453,18 +1447,37 @@
     gain_in,
     gain_mid,
 ):
-    for piece in range(gates.shape[0]):
-        for s in range(2):
-            whole[s, 0, :, piece * 128 : (piece + 1) * 128] = gates[piece, s].astype(F32)
-    out_out[...] = in_out[...]
-    out_y[...] = in_y[...]
-    out_x[...] = in_x[...]
-    out_grad[...] = in_grad[...]
-    out_mixed[...] = in_mixed[...]
+    held = whole.shape[1]
+    pieces = gates.shape[0] // held
+
+    def block(n, carry):
+        for piece in range(pieces):
+            for s in range(2):
+                whole[s, n, :, piece * 128 : (piece + 1) * 128] = gates[
+                    n * pieces + piece, s
+                ].astype(F32)
+        return carry
+
+    lax.fori_loop(0, held, block, 0)
     units = out_gate.shape[1]
-    out_gate[...] = in_both[:, :units].astype(F32)
-    out_up[...] = in_both[:, units:].astype(F32)
-    out_down[...] = in_down[...].astype(F32)
+
+    def copy(row):
+        span = pl.ds(row, CHUNK)
+        out_out[span, :] = in_out[span, :].astype(F32)
+        out_y[span, :] = in_y[span, :]
+        out_x[span, :] = in_x[span, :]
+        out_gate[span, :] = in_both[span, :units].astype(F32)
+        out_up[span, :] = in_both[span, units:].astype(F32)
+        out_down[span, :] = in_down[span, :].astype(F32)
+
+    chunks(out_out.shape[0], copy)
+
+    def own(row):
+        span = pl.ds(row, CHUNK)
+        out_grad[span, :] = in_grad[span, :]
+        out_mixed[span, :] = in_mixed[span, :]
+
+    chunks(out_grad.shape[0], own)
 
     @pl.when(pl.program_id(0) == 0)
     def _():
@@ -1486,13 +1499,15 @@
     width = small_all.shape[0] * small_all.shape[2]
     rows, units = down.shape
     own_rows = grad_input.shape[0]
-    steps, held = rows // blocks, own_rows // 8
-    if unit != 128 or rows % (16 * blocks) or own_rows % 128:
+    grid = 2
+    steps, held = rows // grid, own_rows // grid
+    if unit != 128 or blocks % grid or rows % (16 * grid) or own_rows % (16 * grid):
         whole = gate_all.reshape(blocks, pieces, 2, block, unit).transpose(2, 0, 3, 1, 4)
         summed = small_all.transpose(1, 0, 2).reshape(8, width)
         whole = whole.reshape(gate_shape).astype(F32)
         wide = tuple(one.astype(F32) for one in (both[:, :units], both[:, units:], down))
         last = (summed[:taps], summed[taps], summed[6], summed[7])
+        sums = tuple(one.astype(F32) for one in sums)
         return (whole, *sums, grad_input, mixed, *wide, *last)
     shape = jax.ShapeDtypeStruct
 
@@ -1500,7 +1515,7 @@
         return pl.BlockSpec((count, columns), lambda n: (n, 0))
 
     def by_held(columns):
-        return pl.BlockSpec((held, columns), lambda n: (jnp.minimum(n, 7), 0))
+        return pl.BlockSpec((held, columns), lambda n: (n, 0))
 
     def whole_array(*dims):
         return pl.BlockSpec(dims, lambda n: (0,) * len(dims))
@@ -1510,16 +1525,16 @@
     lines = width // 128
     found = pl.pallas_call(
         partial(finish_kernel, taps),
-        grid=(blocks,),
+        grid=(grid,),
         in_specs=[
-            pl.BlockSpec((pieces, 2, block, unit), lambda n: (n, 0, 0, 0)),
+            pl.BlockSpec((blocks // grid * pieces, 2, block, unit), lambda n: (n, 0, 0, 0)),
             whole_array(*small_all.shape),
         ]
         + [by_rows(steps, columns)] * 3
         + [by_held(d_width)] * 2
         + [by_rows(steps, 2 * units), by_rows(steps, units)],
         out_specs=(
-            (pl.BlockSpec((2, 1, block, block), lambda n: (0, n, 0, 0)),)
+            (pl.BlockSpec((2, blocks // grid, block, block), lambda n: (0, n, 0, 0)),)
             + (by_rows(steps, columns),) * 3
             + (by_held(d_width),) * 2
             + (by_rows(steps, units),) * 3
@@ -1692,14 +1707,15 @@
             shape((dp_rows * ndp, 2 * channels), BF16),
             shape((dp_rows * ndp, channels), BF16),
         ),
-        gather_sems(nbits)
+        [pltpu.VMEM((1, width), F32)]
+        + gather_sems(nbits)
         + [pltpu.SemaphoreType.DMA((ntensor - 1,)), pltpu.SemaphoreType.DMA((ntensor - 1,))]
         + [pltpu.SemaphoreType.DMA((1,))]
         + line_sems(ndp) * (len(w_yx) + 1),
         0,
         tokens,
         segments.reshape(seg_rows_of, 128),
-        gain_in,
+        norm_gain.reshape(width // 128, 128),
         *w_yx,
         w_out,
         far_in=tuple(range(3, 4 + len(w_yx))),
@@ -1812,7 +1828,6 @@
         far_in=(5,),
     )
     d_mixer, sum_wd = lax.optimization_barrier((d_mixer, sum_wd))
-    grad_wout = inner_rows(d_mixer, mixed_low).astype(BF16)
     d_mixed_in = jnp.dot(d_mixer, wout_loc, preferred_element_type=F32)
     unit = math.gcd(channels, block_size)
     merged = half_blocks and nbits <= 2
@@ -1823,7 +1838,6 @@
                 shape((group_rows, 2 * channels), BF16),
                 shape((channels // unit * 2, block_size, unit), BF16),
                 shape((8, channels), F32),
-                shape((dp_rows, channels), F32),
             )
             + ((shape((own_rows, width), BF16),) if merged else ()),
             [
@@ -1835,7 +1849,6 @@
                 pltpu.SemaphoreType.DMA((1,)),
                 pltpu.SemaphoreType.DMA((1,)),
             ]
-            + line_scratch(ndp, dp_rows, channels)
             + (scatter_scratch(own_rows, width, nbits) if merged else []),
             6,
             d_mixed_in,
@@ -1849,10 +1862,8 @@
             since,
             w_window,
             *((ffn_part, middle) if merged else ()),
-            halved(grad_wout, ndp),
-            far_in=(12 if merged else 10,),
-        )
-        d_branches, gate_grad, own_small, sum_wout = found[:4]
+        )
+        d_branches, gate_grad, own_small = found[:3]
         gate_grad = gate_grad.reshape(channels // unit * 2 * block_size, unit)
     else:
         d_conv, d_gate_low, d_branch_y, d_decay = scan_call(
@@ -1899,12 +1910,13 @@
             axis=0,
         )
 
+    grad_wout = inner_rows(d_mixer, mixed_low).astype(BF16)
     grad_wyx = inner_rows(normed_rows, d_branches).astype(BF16)
     d_normed = rows_times(d_branches, wyx_loc).astype(BF16)
-    d_normed, grad_wyx, sum_both = lax.optimization_barrier((d_normed, grad_wyx, sum_both))
-    if not half_blocks:
-        sum_wout = lax.psum_scatter(grad_wout, "dp", scatter_dimension=0, tiled=True)
-        sum_wout = sum_wout.astype(F32)
+    d_normed, grad_wyx, grad_wout, sum_both = lax.optimization_barrier(
+        (d_normed, grad_wyx, grad_wout, sum_both)
+    )
+    sum_wout = lax.psum_scatter(grad_wout, "dp", scatter_dimension=0, tiled=True)
 
     pieces = [halved(grad, ndp) for grad in (gate_grad, grad_wyx)]
     peers = ntensor - 1
@@ -1945,7 +1957,7 @@
         far_in=(6, 7),
     )
     if merged:
-        mixed = found[4]
+        mixed = found[3]
     else:
         (mixed,) = call_kernel(
             partial(result_kernel, nbits),

time: 822 us -> 812 us (0.988)
  waiting for transfers between devices: 39.7 us -> 30.8 us
    dot_general x3, matrix products: 56.6 us -> 46.3 us  [rows_times(): lax.dot_general(left, right, (((1,), (1,)), ((), ())), preferred_element_...]
    pallas_call x6, Pallas kernels: 525 us -> 534 us  [call_kernel(): pl.pallas_call(kernel, out_shape=outs, in_specs=[far if i in far_in else...]
    reduce_scatter x1, waiting for transfers between devices: 13.3 us -> 4.38 us  [body(): lax.psum_scatter(grad_both, 'dp', scatter_dimension=0, tiled=True)]
  transfers between devices with their start and end apart: 4 -> 5, of which waited for: 2 -> 2; matrix products, arithmetic and copies ran while one was open for 25% -> 25% of each run, Pallas kernels for 42% -> 55%
where the time goes in v4:
time: 812 us; the launch traced here: 802 us
  Pallas kernels  545 us (67%)
  matrix products  180 us (22%)
  waiting for transfers between devices  30.8 us (4%)
  other arithmetic  16.7 us (2%)
  between operations  14.3 us (2%)
  local copies, waits for them, and re-layouts  14.1 us (2%)
    pallas_call x6, Pallas kernels, call_kernel(): pl.pallas_call(kernel, out_shape=outs, in_specs=[far if i in far_in else...  534 us
    dot_general x4, matrix products, inner_rows(): lax.dot_general(left, right, (((0,), (0,)), ((), ())), preferred_element_...  60.5 us
    dot_general x3, matrix products, rows_times(): lax.dot_general(left, right, (((1,), (1,)), ((), ())), preferred_element_...  46.3 us
    all_gather x1, waiting for transfers between devices, body(): wd_loc = lax.all_gather(w_down, 'dp', axis=0, tiled=True)  25.6 us
    dot_general x1, matrix products, body(): pre = jnp.dot(mid_rows, both_loc, preferred_element_type=F32)  25 us
    dot_general x1, matrix products, body(): d_hidden = jnp.dot(cot_rows, wd_loc, preferred_element_type=F32)  24.8 us
  transfers between devices with their start and end apart: 5, of which 2 were waited for; matrix products, arithmetic and copies ran while one was open for 25% of the time, Pallas kernels for 55%

profile of v4, /device:TPU:0, one launch (start us, length us, event | category | flops | bytes accessed | tf_op | source)
XLA Modules:
  0.0 801.7 jit_solution(5505578202181337339)
XLA Ops:
  7.3 3.4 pad_maximum_fusion.1
  10.7 91.7 %shard_map.237 = (bf16[1024,2560]{1,0:T(8,128)(2,1)}, s32[4,2,128]{2,1,0:T(2,128)}, bf16[2560,1280]{1,0:T(8,128)(2,1)}, bf16[2560,640]{1,0:T(8,128)(2,1)}) custom-call(bf16[256,2560]{1,0:T(8,128)(2,1)} %refs_1_.3, s32[2,128]{1,0:T(2,128)} %bitcast.49, f32[20,128]{1,0:T(8,128)} %bitcast.44, bf16[320,640]{1,0:T(8,128)(2,1)} %refs_0_.1, ...), custom_call_target="tpu_custom_call" | custom-call | bytes 1000000 | tf_op jit(solution)/shard_map/pallas_call | solution.py:949
  111.8 14.0 %fusion.12.branches = f32[1024,1280]{1,0:T(8,128)} fusion(bf16[1024,2560]{1,0:T(8,128)(2,1)} %get-tuple-element.62, bf16[2560,1280]{1,0:T(8,128)(2,1)} %get-tuple-element.63), kind=kOutput, calls=%fused_computation.38 | convolution fusion | flops 6710886400 | bytes 17039360 | tf_op jit(solution)/shard_map/dot_general | solution.py:1739
  125.8 66.1 %shard_map.238 = (bf16[1024,640]{1,0:T(8,128)(2,1)}, f32[1024,640]{1,0:T(8,128)}, bf16[1024,768]{1,0:T(8,128)(2,1)}, f32[1024,1280]{1,0:T(8,128)}, bf16[1024,2560]{1,0:T(8,128)(2,1)}) custom-call(f32[1024,1280]{1,0:T(8,128)} %fusion.12.branches, f32[8,640]{1,0:T(8,128)} %concatenate.15.tap_rows, f32[1,640]{1,0:T(1,128)} %select_n.32.soft, ...), custom_call_target="tpu_custom_call" | custom-call | bytes 1000000 | tf_op jit(solution)/shard_map/pallas_call | solution.py:949
  191.9 7.3 convolution_convert_fusion.3.mixer
  199.3 97.2 %shard_map.239 = (f32[256,2560]{1,0:T(8,128)}, bf16[1024,2560]{1,0:T(8,128)(2,1)}) custom-call(bf16[1024,2560]{1,0:T(8,128)(2,1)} %convolution_convert_fusion.3.mixer, bf16[256,2560]{1,0:T(8,128)(2,1)} %refs_1_.3, f32[1,2560]{1,0:T(1,128)} %reshape.125.gain), custom_call_target="tpu_custom_call" | custom-call | bytes 1000000 | tf_op jit(solution)/shard_map/pallas_call | solution.py:949
  296.5 25.0 %fusion.13 = f32[1024,3840]{1,0:T(8,128)S(1)} fusion(bf16[1024,2560]{1,0:T(8,128)(2,1)} %get-tuple-element.68, bf16[2560,3840]{1,0:T(8,128)(2,1)} %all-gather.3.cloned.1.call-done), kind=kOutput, calls=%fused_computation.39 | convolution fusion | flops 20132659200 | bytes 40632320 | tf_op jit(solution)/shard_map/dot_general | solution.py:1799
  321.5 2.8 multiply_convert_fusion.1.hidden
  324.3 2.7 copy-done.3
  328.9 15.8 %convolution_convert_fusion.2 = bf16[2560,1920]{1,0:T(8,128)(2,1)} fusion(bf16[1024,2560]{1,0:T(8,128)(2,1)} %get-tuple-element.65, bf16[1024,1920]{1,0:T(8,128)(2,1)S(1)} %multiply_convert_fusion.1.hidden), kind=kOutput, calls=%fused_computation.2 | convolution fusion | flops 10071244800 | bytes 19005440 | tf_op jit(solution)/shard_map/dot_general | solution.py:1662
  344.8 25.6 %all-gather.5.cloned.1.call-done.w_down = bf16[2560,1920]{1,0:T(8,128)(2,1)} async-done(((bf16[320,1920]{1,0:T(8,128)(2,1)}), bf16[2560,1920]{1,0:T(8,128)(2,1)}) %all-gather.5.cloned.1.call-update) | async-done | bytes 9830416 | tf_op jit(solution)/shard_map/all_gather | solution.py:1728
  370.4 24.8 %fusion.6 = (bf16[1024,1920]{1,0:T(8,128)(2,1)S(1)}, bf16[1024,1920]{1,0:T(8,128)(2,1)S(1)}) fusion(f32[1024,3840]{1,0:T(8,128)} %copy-done.3, bf16[1024,2560]{1,0:T(8,128)(2,1)} %get-tuple-element.65, bf16[2560,1920]{1,0:T(8,128)(2,1)} %all-gather.5.cloned.1.call-done.w_down), kind=kOutput, calls=%fused_computation.11 | convolution fusion | flops 10113515520 | bytes 38666240 | tf_op jit(solution)/shard_map/dot_general | solution.py:1805
  398.4 26.7 %convolution_convert_fusion = bf16[2560,3840]{1,0:T(8,128)(2,1)} fusion(bf16[1024,2560]{1,0:T(8,128)(2,1)} %get-tuple-element.68, bf16[1024,1920]{1,0:T(8,128)(2,1)S(1)} %get-tuple-element.110, bf16[1024,1920]{1,0:T(8,128)(2,1)S(1)} %get-tuple-element.109), kind=kOutput, calls=%fused_computation | convolution fusion | flops 20158218240 | bytes 32768000 | tf_op jit(solution)/shard_map/dot_general | solution.py:1662
  425.8 7.0 pad_maximum_fusion
  432.7 27.0 %convolution_convert_fusion.5.d_norm = bf16[1024,2560]{1,0:T(8,128)(2,1)} fusion(bf16[1024,3840]{1,0:T(8,128)(2,1)} %pad_maximum_fusion, bf16[2560,3840]{1,0:T(8,128)(2,1)} %all-gather.3.cloned.1.call-done), kind=kOutput, calls=%fused_computation.18 | convolution fusion | flops 20135280640 | bytes 32768000 | tf_op jit(solution)/shard_map/dot_general | solution.py:1653
  459.8 105.2 %shard_map.240 = (f32[256,2560]{1,0:T(8,128)}, bf16[1024,2560]{1,0:T(8,128)(2,1)}, f32[8,2560]{1,0:T(8,128)}, bf16[1024,2560]{1,0:T(8,128)(2,1)}) custom-call(bf16[1024,2560]{1,0:T(8,128)(2,1)} %convolution_convert_fusion.5.d_norm, bf16[256,2560]{1,0:T(8,128)(2,1)} %cot.3, f32[256,2560]{1,0:T(8,128)} %get-tuple-element.73.middle.refs_1_, ...), custom_call_target="tpu_custom_call" | custom-call | bytes 1000000 | tf_op jit(solution)/shard_map/pallas_call | solution.py:949
  565.1 9.4 %fusion.14.d_mixed = f32[1024,640]{1,0:T(8,128)} fusion(bf16[1024,2560]{1,0:T(8,128)(2,1)} %get-tuple-element.75, bf16[2560,640]{1,0:T(8,128)(2,1)} %get-tuple-element.67), kind=kOutput, calls=%fused_computation.40 | convolution fusion | flops 3355443200 | bytes 11141120 | tf_op jit(solution)/shard_map/dot_general | solution.py:1831
  574.5 61.6 %shard_map.241 = (bf16[1024,1280]{1,0:T(8,128)(2,1)}, bf16[10,256,128]{2,1,0:T(8,128)(2,1)}, f32[8,640]{1,0:T(8,128)}, bf16[256,2560]{1,0:T(8,128)(2,1)}) custom-call(f32[1024,640]{1,0:T(8,128)} %fusion.14.d_mixed, bf16[1024,768]{1,0:T(8,128)(2,1)} %get-tuple-element.76.window, f32[1024,1280]{1,0:T(8,128)} %get-tuple-element.77.gates, ...), custom_call_target="tpu_custom_call" | custom-call | bytes 1000000 | tf_op jit(solution)/shard_map/pallas_call | solution.py:949
  636.1 7.3 convolution_convert_fusion.6
  643.4 11.9 %convolution_convert_fusion.4.refs_0_ = bf16[1024,2560]{1,0:T(8,128)(2,1)} fusion(bf16[1024,1280]{1,0:T(8,128)(2,1)S(1)} %copy-done.9, bf16[2560,1280]{1,0:T(8,128)(2,1)} %get-tuple-element.63), kind=kOutput, calls=%fused_computation.17 | convolution fusion | flops 6713507840 | bytes 14417920 | tf_op jit(solution)/shard_map/dot_general | solution.py:1653
  655.3 10.8 %convolution_convert_fusion.1 = bf16[2560,1280]{1,0:T(8,128)(2,1)} fusion(bf16[1024,2560]{1,0:T(8,128)(2,1)} %get-tuple-element.62, bf16[1024,1280]{1,0:T(8,128)(2,1)S(1)} %copy-done.10), kind=kOutput, calls=%fused_computation.1 | convolution fusion | flops 6714163200 | bytes 14417920 | tf_op jit(solution)/shard_map/dot_general | solution.py:1662
  666.1 4.4 reduce-scatter.6.cloned.1.call-done.in_both
  671.1 112.7 %shard_map.242 = (f32[256,2560]{1,0:T(8,128)}, f32[320,640]{1,0:T(8,128)}, f32[320,640]{1,0:T(8,128)}, bf16[4,4,2,320,128]{4,3,2,1,0:T(8,128)(2,1)}, f32[4,8,640]{2,1,0:T(8,128)}) custom-call(bf16[1024,2560]{1,0:T(8,128)(2,1)} %convolution_convert_fusion.4.refs_0_, bf16[256,2560]{1,0:T(8,128)(2,1)} %refs_1_.3, f32[256,2560]{1,0:T(8,128)} %get-tuple-element.82.refs_2_, ...), custom_call_target="tpu_custom_call" | custom-call | bytes 1000000 | tf_op jit(solution)/shard_map/pallas_call | solution.py:949
  783.9 11.0 %shard_map.243 = (f32[2,10,256,256]{3,2,1,0:T(8,128)}, f32[320,640]{1,0:T(8,128)}, f32[320,640]{1,0:T(8,128)}, f32[320,640]{1,0:T(8,128)}, f32[256,2560]{1,0:T(8...) custom-call(bf16[20,2,256,128]{3,2,1,0:T(8,128)(2,1)} %bitcast.42, ...), custom_call_target="tpu_custom_call" | custom-call | tf_op jit(solution)/shard_map/pallas_call | solution.py:1526
  (56 shorter events, 15.9 us)
Async XLA Ops:
  7.2 102.8 %copy-start = (bf16[2,10,256,256]{3,2,1,0:T(8,128)(2,1)S(1)}, bf16[2,10,256,256]{3,2,1,0:T(8,128)(2,1)}, u32[]{:S(2)}) copy-start(bf16[2,10,256,256]{3,2,1,0:T(8,128)(2,1)} %param.21) | copy-start | bytes 7864324
  7.2 97.4 %copy-start.7 = (f32[2560]{0:T(1024)S(1)}, f32[2560]{0:T(1024)}, u32[]{:S(2)}) copy-start(f32[2560]{0:T(1024)} %param.24) | copy-start | bytes 30724
  7.2 289.2 %all-gather.3.cloned.1.call-start = ((), (), s32[]{:S(2)}) async-start(), calls=%async_computation.3 | async-start | bytes 22118400 | tf_op jit(solution)/shard_map/all_gather | solution.py:1727
  102.4 268.0 %all-gather.5.cloned.1.call-start = ((), (), s32[]{:S(2)}) async-start(), calls=%async_computation.4 | async-start | bytes 11059200 | tf_op jit(solution)/shard_map/all_gather | solution.py:1728
  103.1 461.9 %reduce-scatter.4.cloned.1.call-start = ((), (), s32[]{:S(2)}) async-start(), calls=%async_computation.5 | async-start | bytes 11059200 | tf_op jit(solution)/shard_map/reduce_scatter | solution.py:1803
  125.8 66.1 %copy-start.8 = (bf16[2560,640]{1,0:T(8,128)(2,1)S(1)}, bf16[2560,640]{1,0:T(8,128)(2,1)}, u32[]{:S(2)}) copy-start(bf16[2560,640]{1,0:T(8,128)(2,1)} %get-tuple-element.67) | copy-start | bytes 9830404
  321.5 5.5 copy-start.3
  327.0 1.9 copy-start.2
  344.7 325.8 %reduce-scatter.6.cloned.1.call-start = ((), (), s32[]{:S(2)}) async-start(), calls=%async_computation.6 | async-start | bytes 22118400 | tf_op jit(solution)/shard_map/reduce_scatter | solution.py:1809
  395.2 1.9 copy-start.4
  395.2 3.2 copy-start.5
  425.1 358.8 %reduce-scatter.8.cloned.1.call-start = ((), (), s32[]{:S(2)}) async-start(), calls=%async_computation.7 | async-start | bytes 3686400 | tf_op jit(solution)/shard_map/reduce_scatter | solution.py:1919
  565.1 71.0 %slice-start = ((s8[5242880]{0:T(1024)(128)(4,1)}), s8[4194304]{0:T(1024)(128)(4,1)S(1)}, s32[]{:S(2)}) async-start(s8[5242880]{0:T(1024)(128)(4,1)} %bitcast.50), calls=%async_computation.8 | async-start | bytes 8388608
  574.5 61.6 %slice-start.1 = ((s8[5242880]{0:T(1024)(128)(4,1)}), s8[1048576]{0:T(1024)(128)(4,1)S(1)}, s32[]{:S(2)}) async-start(s8[5242880]{0:T(1024)(128)(4,1)} %bitcast.50), calls=%async_computation.9 | async-start | bytes 2097152
  636.1 7.3 copy-start.9
  643.4 11.9 %copy-start.10 = (bf16[1024,1280]{1,0:T(8,128)(2,1)S(1)}, bf16[1024,1280]{1,0:T(8,128)(2,1)}, u32[]{:S(2)}) copy-start(bf16[1024,1280]{1,0:T(8,128)(2,1)} %get-tuple-element.80) | copy-start | bytes 7864324
  655.3 15.2 %copy-start.6 = (f32[2560]{0:T(1024)S(1)}, f32[2560]{0:T(1024)}, u32[]{:S(2)}) copy-start(f32[2560]{0:T(1024)} %param.17) | copy-start | bytes 30724
  783.9 11.0 %copy-start.1 = (bf16[2,10,256,256]{3,2,1,0:T(8,128)(2,1)S(1)}, bf16[2,10,256,256]{3,2,1,0:T(8,128)(2,1)}, u32[]{:S(2)}) copy-start(bf16[2,10,256,256]{3,2,1,0:T(8,128)(2,1)} %param.21) | copy-start | bytes 7864324
Sparse Core Ops, SparseCore 0:
  102.5 173.9 all-gather.2
  278.2 92.1 all-gather.4
  372.7 101.6 reduce-scatter.3
  476.8 193.7 reduce-scatter.5
  672.7 69.8 reduce-scatter.7

commit v5 on v4

--- a/solution.py
+++ b/solution.py
@@ -767,15 +767,16 @@
         return taken
 
     d_norm, tokens, d_middle, gain, own_small, d_gain_mid = take(6)
-    pieces = take(2)
-    grad_input, sum_y, sum_x, gate_all, small_all = take(5)
+    pieces = take(3)
+    grad_input, sum_out, sum_y, sum_x, gate_all, small_all = take(6)
     landed, staged, s0, r0 = take(4)
     share = small_all.shape[2]
     gate = LineSum(pieces[0], *take(RING))
+    lines = [LineSum(pieces[1], *take(RING))]
     if tiled:
-        lines = [LineSum(pieces[1], *take(RING), pl.ds(at, share)) for at in (0, share)]
+        lines += [LineSum(pieces[2], *take(RING), pl.ds(at, share)) for at in (0, share)]
     else:
-        lines = [LineSum(pieces[1], *take(RING))]
+        lines += [LineSum(pieces[2], *take(RING))]
     d_gain, gains, gains_landed, small, small_landed = take(5)
     gain_s, gain_r, vec_s, vec_r, join_s, join_r, gate_s, gate_r = take(8)
     rows = tokens.shape[0]
@@ -920,11 +921,12 @@
 
         return store
 
+    lines[0].finish(store_in(sum_out))
     if tiled:
-        lines[0].finish(store_in(sum_y))
-        lines[1].finish(store_in(sum_x))
+        lines[1].finish(store_in(sum_y))
+        lines[2].finish(store_in(sum_x))
     else:
-        lines[0].finish(store_in(sum_y, sum_x))
+        lines[1].finish(store_in(sum_y, sum_x))
     gate_core().wait()
     for shift in range(1, chips):
         gate_line(shift).wait_send()
@@ -1913,17 +1915,14 @@
     grad_wout = inner_rows(d_mixer, mixed_low).astype(BF16)
     grad_wyx = inner_rows(normed_rows, d_branches).astype(BF16)
     d_normed = rows_times(d_branches, wyx_loc).astype(BF16)
-    d_normed, grad_wyx, grad_wout, sum_both = lax.optimization_barrier(
-        (d_normed, grad_wyx, grad_wout, sum_both)
-    )
-    sum_wout = lax.psum_scatter(grad_wout, "dp", scatter_dimension=0, tiled=True)
-
-    pieces = [halved(grad, ndp) for grad in (gate_grad, grad_wyx)]
+    d_normed, grad_wyx, sum_both = lax.optimization_barrier((d_normed, grad_wyx, sum_both))
+
+    pieces = [halved(grad, ndp) for grad in (gate_grad, grad_wout, grad_wyx)]
     peers = ntensor - 1
     gate_rows = gate_grad.shape[0] // ndp
     dma = pltpu.SemaphoreType.DMA
     scratch = scatter_scratch(own_rows, width, nbits)
-    scratch += line_scratch(ndp, gate_rows, unit)
+    scratch += line_scratch(ndp, gate_rows, unit) + line_scratch(ndp, dp_rows, channels)
     if tiled:
         scratch += line_scratch(ndp, dp_rows, channels) * 2
     else:
@@ -1937,10 +1936,10 @@
     ]
     scratch += [dma((peers,)), dma((peers,)), dma((ndp - 1,)), dma((ndp - 1,))]
     scratch += [dma((peers,)), dma((peers,)), dma((peers + ndp,)), dma((peers + ndp,))]
-    grad_input, sum_wy, sum_wx, gate_all, small_all = call_kernel(
+    grad_input, sum_wout, sum_wy, sum_wx, gate_all, small_all = call_kernel(
         partial(leave_kernel, nbits, tiled),
         (shape((own_rows, width), F32),)
-        + (shape((dp_rows, channels), F32),) * 2
+        + (shape((dp_rows, channels), F32),) * 3
         + (
             shape((ntensor, ndp // 2, 2, gate_rows, unit), BF16),
             shape((ntensor, 8, channels), F32),
@@ -1954,7 +1953,7 @@
         own_small,
         d_gain_mid,
         *pieces,
-        far_in=(6, 7),
+        far_in=(6, 7, 8),
     )
     if merged:
         mixed = found[3]

time: 812 us -> 809 us (level)
  transfers between devices with their start and end apart: 5 -> 4, of which waited for: 2 -> 2; matrix products, arithmetic and copies ran while one was open for 25% -> 25% of each run, Pallas kernels for 55% -> 41%
where the time goes in v5:
time: 809 us; the launch traced here: 798 us
  Pallas kernels  542 us (67%)
  matrix products  177 us (22%)
  waiting for transfers between devices  33.6 us (4%)
  other arithmetic  16.7 us (2%)
  local copies, waits for them, and re-layouts  14.8 us (2%)
  between operations  14.2 us (2%)
    pallas_call x6, Pallas kernels, call_kernel(): pl.pallas_call(kernel, out_shape=outs, in_specs=[far if i in far_in else...  531 us
    dot_general x4, matrix products, inner_rows(): lax.dot_general(left, right, (((0,), (0,)), ((), ())), preferred_element_...  60.2 us
    dot_general x3, matrix products, rows_times(): lax.dot_general(left, right, (((1,), (1,)), ((), ())), preferred_element_...  43.3 us
    all_gather x1, waiting for transfers between devices, body(): wd_loc = lax.all_gather(w_down, 'dp', axis=0, tiled=True)  25.6 us
    dot_general x1, matrix products, body(): pre = jnp.dot(mid_rows, both_loc, preferred_element_type=F32)  25 us
    dot_general x1, matrix products, body(): d_hidden = jnp.dot(cot_rows, wd_loc, preferred_element_type=F32)  24.7 us
  transfers between devices with their start and end apart: 4, of which 2 were waited for; matrix products, arithmetic and copies ran while one was open for 25% of the time, Pallas kernels for 41%

profile of v5, /device:TPU:0, one launch (start us, length us, event | category | flops | bytes accessed | tf_op | source)
XLA Modules:
  0.0 798.4 jit_solution(6133909764697247610)
XLA Ops:
  7.3 3.4 pad_maximum_fusion.1
  10.7 91.7 %shard_map.237 = (bf16[1024,2560]{1,0:T(8,128)(2,1)}, s32[4,2,128]{2,1,0:T(2,128)}, bf16[2560,1280]{1,0:T(8,128)(2,1)}, bf16[2560,640]{1,0:T(8,128)(2,1)}) custom-call(bf16[256,2560]{1,0:T(8,128)(2,1)} %refs_1_.3, s32[2,128]{1,0:T(2,128)} %bitcast.51, f32[20,128]{1,0:T(8,128)} %bitcast.46, bf16[320,640]{1,0:T(8,128)(2,1)} %refs_0_.1, ...), custom_call_target="tpu_custom_call" | custom-call | bytes 1000000 | tf_op jit(solution)/shard_map/pallas_call | solution.py:951
  111.8 14.0 %fusion.12.branches = f32[1024,1280]{1,0:T(8,128)} fusion(bf16[1024,2560]{1,0:T(8,128)(2,1)} %get-tuple-element.62, bf16[2560,1280]{1,0:T(8,128)(2,1)} %get-tuple-element.63), kind=kOutput, calls=%fused_computation.38 | convolution fusion | flops 6710886400 | bytes 17039360 | tf_op jit(solution)/shard_map/dot_general | solution.py:1741
  125.8 66.1 %shard_map.238 = (bf16[1024,640]{1,0:T(8,128)(2,1)}, f32[1024,640]{1,0:T(8,128)}, bf16[1024,768]{1,0:T(8,128)(2,1)}, f32[1024,1280]{1,0:T(8,128)}, bf16[1024,2560]{1,0:T(8,128)(2,1)}) custom-call(f32[1024,1280]{1,0:T(8,128)} %fusion.12.branches, f32[8,640]{1,0:T(8,128)} %concatenate.15.tap_rows, f32[1,640]{1,0:T(1,128)} %select_n.32.soft, ...), custom_call_target="tpu_custom_call" | custom-call | bytes 1000000 | tf_op jit(solution)/shard_map/pallas_call | solution.py:951
  191.9 7.4 convolution_convert_fusion.3.mixer
  199.2 97.2 %shard_map.239 = (f32[256,2560]{1,0:T(8,128)}, bf16[1024,2560]{1,0:T(8,128)(2,1)}) custom-call(bf16[1024,2560]{1,0:T(8,128)(2,1)} %convolution_convert_fusion.3.mixer, bf16[256,2560]{1,0:T(8,128)(2,1)} %refs_1_.3, f32[1,2560]{1,0:T(1,128)} %reshape.128.gain), custom_call_target="tpu_custom_call" | custom-call | bytes 1000000 | tf_op jit(solution)/shard_map/pallas_call | solution.py:951
  296.5 25.0 %fusion.13 = f32[1024,3840]{1,0:T(8,128)S(1)} fusion(bf16[1024,2560]{1,0:T(8,128)(2,1)} %get-tuple-element.68, bf16[2560,3840]{1,0:T(8,128)(2,1)} %all-gather.3.cloned.1.call-done), kind=kOutput, calls=%fused_computation.39 | convolution fusion | flops 20132659200 | bytes 40632320 | tf_op jit(solution)/shard_map/dot_general | solution.py:1801
  321.5 2.8 multiply_convert_fusion.1.hidden
  324.4 2.7 copy-done.3
  328.9 15.7 %convolution_convert_fusion.2 = bf16[2560,1920]{1,0:T(8,128)(2,1)} fusion(bf16[1024,2560]{1,0:T(8,128)(2,1)} %get-tuple-element.65, bf16[1024,1920]{1,0:T(8,128)(2,1)S(1)} %multiply_convert_fusion.1.hidden), kind=kOutput, calls=%fused_computation.2 | convolution fusion | flops 10071244800 | bytes 19005440 | tf_op jit(solution)/shard_map/dot_general | solution.py:1664
  344.7 25.6 %all-gather.5.cloned.1.call-done.w_down = bf16[2560,1920]{1,0:T(8,128)(2,1)} async-done(((bf16[320,1920]{1,0:T(8,128)(2,1)}), bf16[2560,1920]{1,0:T(8,128)(2,1)}) %all-gather.5.cloned.1.call-update) | async-done | bytes 9830416 | tf_op jit(solution)/shard_map/all_gather | solution.py:1730
  370.4 24.7 %fusion.6 = (bf16[1024,1920]{1,0:T(8,128)(2,1)S(1)}, bf16[1024,1920]{1,0:T(8,128)(2,1)S(1)}) fusion(f32[1024,3840]{1,0:T(8,128)} %copy-done.3, bf16[1024,2560]{1,0:T(8,128)(2,1)} %get-tuple-element.65, bf16[2560,1920]{1,0:T(8,128)(2,1)} %all-gather.5.cloned.1.call-done.w_down), kind=kOutput, calls=%fused_computation.11 | convolution fusion | flops 10113515520 | bytes 38666240 | tf_op jit(solution)/shard_map/dot_general | solution.py:1807
  398.3 26.6 %convolution_convert_fusion = bf16[2560,3840]{1,0:T(8,128)(2,1)} fusion(bf16[1024,2560]{1,0:T(8,128)(2,1)} %get-tuple-element.68, bf16[1024,1920]{1,0:T(8,128)(2,1)S(1)} %get-tuple-element.110, bf16[1024,1920]{1,0:T(8,128)(2,1)S(1)} %get-tuple-element.109), kind=kOutput, calls=%fused_computation | convolution fusion | flops 20158218240 | bytes 32768000 | tf_op jit(solution)/shard_map/dot_general | solution.py:1664
  426.8 7.0 pad_maximum_fusion
  433.8 27.3 %convolution_convert_fusion.5.d_norm = bf16[1024,2560]{1,0:T(8,128)(2,1)} fusion(bf16[1024,3840]{1,0:T(8,128)(2,1)} %pad_maximum_fusion, bf16[2560,3840]{1,0:T(8,128)(2,1)} %all-gather.3.cloned.1.call-done), kind=kOutput, calls=%fused_computation.18 | convolution fusion | flops 20135280640 | bytes 32768000 | tf_op jit(solution)/shard_map/dot_general | solution.py:1655
  461.1 104.7 %shard_map.240 = (f32[256,2560]{1,0:T(8,128)}, bf16[1024,2560]{1,0:T(8,128)(2,1)}, f32[8,2560]{1,0:T(8,128)}, bf16[1024,2560]{1,0:T(8,128)(2,1)}) custom-call(bf16[1024,2560]{1,0:T(8,128)(2,1)} %convolution_convert_fusion.5.d_norm, bf16[256,2560]{1,0:T(8,128)(2,1)} %cot.3, f32[256,2560]{1,0:T(8,128)} %get-tuple-element.73.middle.refs_1_, ...), custom_call_target="tpu_custom_call" | custom-call | bytes 1000000 | tf_op jit(solution)/shard_map/pallas_call | solution.py:951
  565.9 9.5 %fusion.14.d_mixed = f32[1024,640]{1,0:T(8,128)} fusion(bf16[1024,2560]{1,0:T(8,128)(2,1)} %get-tuple-element.75, bf16[2560,640]{1,0:T(8,128)(2,1)} %get-tuple-element.67), kind=kOutput, calls=%fused_computation.40 | convolution fusion | flops 3355443200 | bytes 11141120 | tf_op jit(solution)/shard_map/dot_general | solution.py:1833
  575.4 61.4 %shard_map.241 = (bf16[1024,1280]{1,0:T(8,128)(2,1)}, bf16[10,256,128]{2,1,0:T(8,128)(2,1)}, f32[8,640]{1,0:T(8,128)}, bf16[256,2560]{1,0:T(8,128)(2,1)}) custom-call(f32[1024,640]{1,0:T(8,128)} %fusion.14.d_mixed, bf16[1024,768]{1,0:T(8,128)(2,1)} %get-tuple-element.76.window, f32[1024,1280]{1,0:T(8,128)} %get-tuple-element.77.gates, ...), custom_call_target="tpu_custom_call" | custom-call | bytes 1000000 | tf_op jit(solution)/shard_map/pallas_call | solution.py:951
  636.8 8.7 %convolution_convert_fusion.6 = bf16[2560,640]{1,0:T(8,128)(2,1)} fusion(bf16[1024,2560]{1,0:T(8,128)(2,1)} %get-tuple-element.75, bf16[1024,640]{1,0:T(8,128)(2,1)S(1)} %copy-done.10), kind=kOutput, calls=%fused_computation.19 | convolution fusion | flops 3357081600 | bytes 9830400 | tf_op jit(solution)/shard_map/dot_general | solution.py:1664
  645.6 8.7 %convolution_convert_fusion.4.refs_0_ = bf16[1024,2560]{1,0:T(8,128)(2,1)} fusion(bf16[1024,1280]{1,0:T(8,128)(2,1)S(1)} %copy-done.9, bf16[2560,1280]{1,0:T(8,128)(2,1)S(1)} %bitcast.53), kind=kOutput, calls=%fused_computation.17 | convolution fusion | flops 6713507840 | bytes 14417920 | tf_op jit(solution)/shard_map/dot_general | solution.py:1655
  654.3 9.1 %convolution_convert_fusion.1 = bf16[2560,1280]{1,0:T(8,128)(2,1)} fusion(bf16[1024,2560]{1,0:T(8,128)(2,1)S(1)} %bitcast.55, bf16[1024,1280]{1,0:T(8,128)(2,1)S(1)} %copy-done.9), kind=kOutput, calls=%fused_computation.1 | convolution fusion | flops 6714163200 | bytes 14417920 | tf_op jit(solution)/shard_map/dot_general | solution.py:1664
  663.3 7.1 reduce-scatter.5.cloned.1.call-done.in_both
  670.5 110.1 %shard_map.242 = (f32[256,2560]{1,0:T(8,128)}, f32[320,640]{1,0:T(8,128)}, f32[320,640]{1,0:T(8,128)}, f32[320,640]{1,0:T(8,128)}, bf16[4,4,2,320,128]{4,3,2,1,0:T(8,128)(2,1)}, /*index=5*/f32[4,8,640]{2,1,0:T(8,128)}) custom-call(bf16[1024,2560]{1,0:T(8,128)(2,1)} %convolution_convert_fusion.4.refs_0_, bf16[256,2560]{1,0:T(8,128)(2,1)} %refs_1_.3, ...), custom_call_target="tpu_custom_call" | custom-call | bytes 1000000 | tf_op jit(solution)/shard_map/pallas_call | solution.py:951
  780.6 11.0 %shard_map.243 = (f32[2,10,256,256]{3,2,1,0:T(8,128)}, f32[320,640]{1,0:T(8,128)}, f32[320,640]{1,0:T(8,128)}, f32[320,640]{1,0:T(8,128)}, f32[256,2560]{1,0:T(8...) custom-call(bf16[20,2,256,128]{3,2,1,0:T(8,128)(2,1)} %bitcast.44, ...), custom_call_target="tpu_custom_call" | custom-call | tf_op jit(solution)/shard_map/pallas_call | solution.py:1528
  (58 shorter events, 16.6 us)
Async XLA Ops:
  7.2 102.8 %copy-start = (bf16[2,10,256,256]{3,2,1,0:T(8,128)(2,1)S(1)}, bf16[2,10,256,256]{3,2,1,0:T(8,128)(2,1)}, u32[]{:S(2)}) copy-start(bf16[2,10,256,256]{3,2,1,0:T(8,128)(2,1)} %param.21) | copy-start | bytes 7864324
  7.2 97.4 %copy-start.7 = (f32[2560]{0:T(1024)S(1)}, f32[2560]{0:T(1024)}, u32[]{:S(2)}) copy-start(f32[2560]{0:T(1024)} %param.24) | copy-start | bytes 30724
  7.2 289.3 %all-gather.3.cloned.1.call-start = ((), (), s32[]{:S(2)}) async-start(), calls=%async_computation.2 | async-start | bytes 22118400 | tf_op jit(solution)/shard_map/all_gather | solution.py:1729
  102.4 268.0 %all-gather.5.cloned.1.call-start = ((), (), s32[]{:S(2)}) async-start(), calls=%async_computation.3 | async-start | bytes 11059200 | tf_op jit(solution)/shard_map/all_gather | solution.py:1730
  103.1 462.8 %reduce-scatter.3.cloned.1.call-start = ((), (), s32[]{:S(2)}) async-start(), calls=%async_computation.4 | async-start | bytes 11059200 | tf_op jit(solution)/shard_map/reduce_scatter | solution.py:1805
  125.8 66.1 %copy-start.8 = (bf16[2560,640]{1,0:T(8,128)(2,1)S(1)}, bf16[2560,640]{1,0:T(8,128)(2,1)}, u32[]{:S(2)}) copy-start(bf16[2560,640]{1,0:T(8,128)(2,1)} %get-tuple-element.67) | copy-start | bytes 9830404
  321.5 5.5 copy-start.3
  327.0 1.9 copy-start.2
  344.7 325.8 %reduce-scatter.5.cloned.1.call-start = ((), (), s32[]{:S(2)}) async-start(), calls=%async_computation.5 | async-start | bytes 22118400 | tf_op jit(solution)/shard_map/reduce_scatter | solution.py:1811
  395.1 1.9 copy-start.4
  395.1 3.2 copy-start.5
  424.9 0.7 copy-start.6
  575.4 61.4 %copy-start.10 = (bf16[1024,640]{1,0:T(8,128)(2,1)S(1)}, bf16[1024,640]{1,0:T(8,128)(2,1)}, u32[]{:S(2)}) copy-start(bf16[1024,640]{1,0:T(8,128)(2,1)} %get-tuple-element.66) | copy-start | bytes 3932164
  575.4 70.2 %slice-start = ((s8[6553600]{0:T(1024)(128)(4,1)}), s8[2359296]{0:T(1024)(128)(4,1)S(1)}, s32[]{:S(2)}) async-start(s8[6553600]{0:T(1024)(128)(4,1)} %bitcast.52), calls=%async_computation.6 | async-start | bytes 4718592
  636.8 8.8 %slice-start.1 = ((s8[6553600]{0:T(1024)(128)(4,1)}), s8[4194304]{0:T(1024)(128)(4,1)S(1)}, s32[]{:S(2)}) async-start(s8[6553600]{0:T(1024)(128)(4,1)} %bitcast.52), calls=%async_computation.7 | async-start | bytes 8388608
  636.8 8.8 %copy-start.9 = (bf16[1024,1280]{1,0:T(8,128)(2,1)S(1)}, bf16[1024,1280]{1,0:T(8,128)(2,1)}, u32[]{:S(2)}) copy-start(bf16[1024,1280]{1,0:T(8,128)(2,1)} %get-tuple-element.80) | copy-start | bytes 7864324
  636.8 17.4 %slice-start.2 = ((s8[5242880]{0:T(1024)(128)(4,1)}), s8[4194304]{0:T(1024)(128)(4,1)S(1)}, s32[]{:S(2)}) async-start(s8[5242880]{0:T(1024)(128)(4,1)} %bitcast.54), calls=%async_computation.8 | async-start | bytes 8388608
  645.6 8.7 %slice-start.3 = ((s8[5242880]{0:T(1024)(128)(4,1)}), s8[1048576]{0:T(1024)(128)(4,1)S(1)}, s32[]{:S(2)}) async-start(s8[5242880]{0:T(1024)(128)(4,1)} %bitcast.54), calls=%async_computation.9 | async-start | bytes 2097152
  780.6 11.1 %copy-start.1 = (bf16[2,10,256,256]{3,2,1,0:T(8,128)(2,1)S(1)}, bf16[2,10,256,256]{3,2,1,0:T(8,128)(2,1)}, u32[]{:S(2)}) copy-start(bf16[2,10,256,256]{3,2,1,0:T(8,128)(2,1)} %param.21) | copy-start | bytes 7864324
Sparse Core Ops, SparseCore 0:
  102.5 173.9 all-gather.2
  278.2 92.1 all-gather.4
  372.7 101.6 reduce-scatter.2
  476.7 193.7 reduce-scatter.4
